TPU v7x, 32 devices: a whole 2x2x4 slice. The times are simulated.
32 devices in a mesh: tp: 4 (over y, x), ep: 8 (over z, core).
Axes of the slice: x: 2, y: 2, z: 4, core: 2. Of those that a mesh axis runs over, the one named last changes fastest.
Arguments:
- tokens: bfloat16 [25088, 768], P('ep'), may hold values from -6 to 6
- cotangent: bfloat16 [25088, 768], P('ep'), may hold values from -6 to 6
- picks: int32 [25088, 2], P('ep'), may hold values from 0 to 7, all different within a row
- priority: int32 [8, 3136], P('ep'), may hold values from 0 to 3135, each once within a row
- router_noise: float32 [25088, 8], P('ep'), may hold values from -3 to 3
- dense_norm_gain: float32 [768], replicated, may hold values from 0.5 to 1.5
- dense_norm_bias: float32 [768], replicated, may hold values from -1.25 to 1.25
- dense_attend_in: bfloat16 [768, 3, 768], P(None, None, 'tp'), may hold values from -0.21875 to 0.21875
- dense_attend_bias: float32 [2, 768], P(None, 'tp'), may hold values from -1.25 to 1.25
- dense_attend_out: bfloat16 [768, 768], P('tp'), may hold values from -1.75 to 1.75
- dense_attend_out_bias: float32 [768], replicated, may hold values from -1.25 to 1.25
- feed_norm_gain: float32 [768], replicated, may hold values from 0.5 to 1.5
- feed_norm_bias: float32 [768], replicated, may hold values from -1.25 to 1.25
- feed_in: bfloat16 [768, 3072], P(None, 'tp'), may hold values from -0.21875 to 0.21875
- feed_in_bias: float32 [3072], P('tp'), may hold values from -1.25 to 1.25
- feed_out: bfloat16 [3072, 768], P('tp'), may hold values from -0.109375 to 0.109375
- feed_out_bias: float32 [768], replicated, may hold values from -1.25 to 1.25
- sparse_norm_gain: float32 [768], replicated, may hold values from 0.5 to 1.5
- sparse_norm_bias: float32 [768], replicated, may hold values from -1.25 to 1.25
- sparse_attend_in: bfloat16 [768, 3, 768], P(None, None, 'tp'), may hold values from -0.21875 to 0.21875
- sparse_attend_bias: float32 [2, 768], P(None, 'tp'), may hold values from -1.25 to 1.25
- sparse_attend_out: bfloat16 [768, 768], P('tp'), may hold values from -1.75 to 1.75
- sparse_attend_out_bias: float32 [768], replicated, may hold values from -1.25 to 1.25
- route_norm_gain: float32 [768], replicated, may hold values from 0.5 to 1.5
- route_norm_bias: float32 [768], replicated, may hold values from -1.25 to 1.25
- router: bfloat16 [768, 8], replicated, may hold values from -0.109375 to 0.109375
- expert_in: bfloat16 [8, 768, 3072], P('ep', None, 'tp'), may hold values from -0.21875 to 0.21875
- expert_in_bias: float32 [8, 3072], P('ep', 'tp'), may hold values from -0.625 to 0.625
- expert_out: bfloat16 [8, 3072, 768], P('ep', 'tp'), may hold values from -0.4375 to 0.4375
- expert_out_bias: float32 [8, 768], P('ep'), may hold values from -3 to 3
Outputs:
- activations: bfloat16 [25088, 768], P('ep')
- input_grad: float32 [25088, 768], P('ep')
- grad_dense_norm_gain: float32 [768], replicated
- grad_dense_norm_bias: float32 [768], replicated
- grad_dense_attend_in: float32 [768, 3, 768], P(None, None, 'tp')
- grad_dense_attend_bias: float32 [2, 768], P(None, 'tp')
- grad_dense_attend_out: float32 [768, 768], P('tp')
- grad_dense_attend_out_bias: float32 [768], replicated
- grad_feed_norm_gain: float32 [768], replicated
- grad_feed_norm_bias: float32 [768], replicated
- grad_feed_in: float32 [768, 3072], P(None, 'tp')
- grad_feed_in_bias: float32 [3072], P('tp')
- grad_feed_out: float32 [3072, 768], P('tp')
- grad_feed_out_bias: float32 [768], replicated
- grad_sparse_norm_gain: float32 [768], replicated
- grad_sparse_norm_bias: float32 [768], replicated
- grad_sparse_attend_in: float32 [768, 3, 768], P(None, None, 'tp')
- grad_sparse_attend_bias: float32 [2, 768], P(None, 'tp')
- grad_sparse_attend_out: float32 [768, 768], P('tp')
- grad_sparse_attend_out_bias: float32 [768], replicated
- grad_route_norm_gain: float32 [768], replicated
- grad_route_norm_bias: float32 [768], replicated
- grad_router: float32 [768, 8], replicated
- grad_expert_in: float32 [8, 768, 3072], P('ep', None, 'tp')
- grad_expert_in_bias: float32 [8, 3072], P('ep', 'tp')
- grad_expert_out: float32 [8, 3072, 768], P('ep', 'tp')
- grad_expert_out_bias: float32 [8, 768], P('ep')
Inputs may be any that keep to these rules, and one draw needn't show every extreme that they name: `picks`: each row names two different experts; every expert is named by some row. `priority`: each row holds every number of 0 to 3135 once.
All inputs are finite; a program needn't handle non-finite values.
Results may differ from a plain program's by a relative error of at most 0.02.
Values may be sent and summed in bfloat16 or wider, within the bound.
A program may use at most 384 MiB of HBM per device.

v0:
```python
import jax
import jax.numpy as jnp
from jax import lax
from jax.sharding import PartitionSpec as P

HEAD = 64
LEN = 196


EPSILON = 1e-06


def layer_norm(residual, norm_gain, norm_bias):
    average = jnp.mean(residual, axis=-1, keepdims=True)
    centred = residual - average
    variance = jnp.mean(centred * centred, axis=-1, keepdims=True)
    return centred * lax.rsqrt(variance + EPSILON) * norm_gain + norm_bias


def gelu_exact(value_in):
    return jax.nn.gelu(value_in, approximate=False)


def norm_backward(residual, norm_gain, norm_bias, grad_normed):
    pullback = jax.vjp(layer_norm, residual, norm_gain, norm_bias)[1]
    return pullback(grad_normed)


def normalize(stream, norm_gain, norm_bias):
    normed = layer_norm(stream, norm_gain, norm_bias).astype(jnp.bfloat16)
    return normed


def add_branch(stream, partial_value, bias_row):
    return stream + lax.psum(partial_value, "tp") + bias_row


def rounded_grad_rows(grad_stream):
    rounded = grad_stream.astype(jnp.bfloat16)
    return rounded


def finish_norm(stream, norm_gain, norm_bias, partial_value, grad_stream):
    grad_normed = lax.psum(partial_value.astype(jnp.bfloat16), "tp").astype(jnp.float32)
    grad_input, grad_gain, grad_bias = norm_backward(stream, norm_gain, norm_bias, grad_normed)
    return (grad_stream + grad_input, grad_gain, grad_bias)


def route(device_picks, device_order, capacity, experts):
    rows_dev = device_picks.shape[0]
    ranked = device_picks[device_order]
    sequence = jnp.concatenate([ranked[:, 0], ranked[:, 1]])
    onehot = (sequence[:, None] == jnp.arange(experts, dtype=jnp.int32)[None, :]).astype(jnp.int32)
    earlier = jnp.cumsum(onehot, axis=0) - onehot
    position = jnp.sum(earlier * onehot, axis=1)
    slot_index = (
        jnp.zeros((rows_dev, 2), jnp.int32).at[device_order].set(position.reshape(2, rows_dev).T)
    )
    kept_mask = slot_index < capacity
    target = jnp.where(kept_mask, device_picks * capacity + slot_index, experts * capacity)
    pair_ids = (
        jnp.arange(2, dtype=jnp.int32)[None, :] * rows_dev
        + jnp.arange(rows_dev, dtype=jnp.int32)[:, None]
    )
    slot_table = jnp.full((experts * capacity + 1,), 2 * rows_dev, jnp.int32)
    slot_table = slot_table.at[target.reshape(-1)].set(pair_ids.reshape(-1))
    return (kept_mask, target, slot_table[: experts * capacity])


def to_experts(buffer):
    whole_rows = lax.all_to_all(buffer, "ep", split_axis=0, concat_axis=0, tiled=True)
    return whole_rows.reshape(-1, whole_rows.shape[2])


def from_experts(partial_value, bias_row):
    sources = lax.axis_size("ep")
    summed_rows = (
        lax.psum(partial_value.astype(jnp.bfloat16), "tp").astype(jnp.float32) + bias_row
    ).astype(jnp.bfloat16)
    whole_rows = lax.all_to_all(
        summed_rows.reshape(sources, -1, summed_rows.shape[1]),
        "ep",
        split_axis=0,
        concat_axis=0,
        tiled=True,
    )
    return whole_rows.reshape(-1, whole_rows.shape[2])


def attend_forward(normed, proj_in, proj_bias, proj_out):
    rows_dev = normed.shape[0]
    local_width = proj_in.shape[2]
    heads_dev = local_width // HEAD
    images = rows_dev // LEN
    score_scale = HEAD ** (-0.5)
    projected = jnp.einsum("td,dkc->tkc", normed, proj_in, preferred_element_type=jnp.float32)
    queries = (
        (projected[:, 0] + proj_bias[0]).astype(jnp.bfloat16).reshape(images, LEN, heads_dev, HEAD)
    )
    keys_in = projected[:, 1].astype(jnp.bfloat16).reshape(images, LEN, heads_dev, HEAD)
    values = (
        (projected[:, 2] + proj_bias[1]).astype(jnp.bfloat16).reshape(images, LEN, heads_dev, HEAD)
    )
    scores = (
        jnp.einsum("bqhc,bkhc->bhqk", queries, keys_in, preferred_element_type=jnp.float32)
        * score_scale
    )
    peak_score = jnp.max(scores, axis=-1, keepdims=True)
    exp_scores = jnp.exp(scores - peak_score)
    total_weight = jnp.sum(exp_scores, axis=-1, keepdims=True)
    weights = (exp_scores / total_weight).astype(jnp.bfloat16)
    log_total = peak_score + jnp.log(total_weight)
    context = jnp.einsum("bhqk,bkhc->bqhc", weights, values, preferred_element_type=jnp.float32)
    context = context.reshape(rows_dev, local_width).astype(jnp.bfloat16)
    partial_value = jnp.dot(context, proj_out, preferred_element_type=jnp.float32)
    return (partial_value, (normed, queries, keys_in, values, log_total, context))


def attend_backward(proj_in, proj_out, kept_state, grad_branch):
    normed, queries, keys_in, values, log_total, context = kept_state
    rows_dev, local_width = context.shape
    score_scale = HEAD ** (-0.5)
    grad_out_bias = jnp.sum(grad_branch, axis=0, dtype=jnp.float32)
    grad_proj_out = jnp.einsum(
        "tc,td->cd", context, grad_branch, preferred_element_type=jnp.float32
    )
    grad_context = jnp.einsum(
        "td,cd->tc", grad_branch, proj_out, preferred_element_type=jnp.float32
    )
    grad_context = grad_context.astype(jnp.bfloat16).reshape(queries.shape)
    scores = (
        jnp.einsum("bqhc,bkhc->bhqk", queries, keys_in, preferred_element_type=jnp.float32)
        * score_scale
    )
    probabilities = jnp.exp(scores - log_total)
    grad_probs = jnp.einsum(
        "bqhc,bkhc->bhqk", grad_context, values, preferred_element_type=jnp.float32
    )
    grad_values = jnp.einsum(
        "bhqk,bqhc->bkhc",
        probabilities.astype(jnp.bfloat16),
        grad_context,
        preferred_element_type=jnp.float32,
    ).astype(jnp.bfloat16)
    grad_scores = probabilities * (
        grad_probs - jnp.sum(probabilities * grad_probs, axis=-1, keepdims=True)
    )
    grad_scores = grad_scores.astype(jnp.bfloat16)
    grad_queries = (
        jnp.einsum("bhqk,bkhc->bqhc", grad_scores, keys_in, preferred_element_type=jnp.float32)
        * score_scale
    ).astype(jnp.bfloat16)
    grad_keys = (
        jnp.einsum("bhqk,bqhc->bkhc", grad_scores, queries, preferred_element_type=jnp.float32)
        * score_scale
    ).astype(jnp.bfloat16)
    grad_projected = jnp.stack(
        [
            grad_queries.reshape(rows_dev, local_width),
            grad_keys.reshape(rows_dev, local_width),
            grad_values.reshape(rows_dev, local_width),
        ],
        axis=1,
    )
    grad_proj_in = jnp.einsum(
        "td,tkc->dkc", normed, grad_projected, preferred_element_type=jnp.float32
    )
    grad_proj_bias = jnp.sum(grad_projected[:, 0::2], axis=0, dtype=jnp.float32)
    partial_value = jnp.einsum(
        "tkc,dkc->td", grad_projected, proj_in, preferred_element_type=jnp.float32
    )
    return (partial_value, (grad_proj_in, grad_proj_bias, grad_proj_out, grad_out_bias))


def feed_forward(normed, weight_in, bias_in, weight_out):
    hidden_pre = jnp.dot(normed, weight_in, preferred_element_type=jnp.float32) + bias_in
    hidden = gelu_exact(hidden_pre).astype(jnp.bfloat16)
    partial_value = jnp.dot(hidden, weight_out, preferred_element_type=jnp.float32)
    return (partial_value, (normed, hidden_pre, hidden))


def feed_backward(weight_in, weight_out, kept_state, grad_branch):
    normed, hidden_pre, hidden = kept_state
    grad_bias_out = jnp.sum(grad_branch, axis=0, dtype=jnp.float32)
    grad_weight_out = jnp.einsum(
        "tf,td->fd", hidden, grad_branch, preferred_element_type=jnp.float32
    )
    grad_hidden = jnp.einsum(
        "td,fd->tf", grad_branch, weight_out, preferred_element_type=jnp.float32
    )
    grad_pre = jax.vjp(gelu_exact, hidden_pre)[1](grad_hidden)[0].astype(jnp.bfloat16)
    grad_bias_in = jnp.sum(grad_pre, axis=0, dtype=jnp.float32)
    grad_weight_in = jnp.einsum("td,tf->df", normed, grad_pre, preferred_element_type=jnp.float32)
    partial_value = jnp.einsum("tf,df->td", grad_pre, weight_in, preferred_element_type=jnp.float32)
    return (partial_value, (grad_weight_in, grad_bias_in, grad_weight_out, grad_bias_out))


def mixture_forward(
    normed,
    router,
    expert_in,
    expert_in_bias,
    expert_out,
    expert_out_bias,
    router_noise,
    picks,
    priority,
):
    rows_dev = normed.shape[0]
    experts = lax.axis_size("ep")
    capacity = rows_dev // experts
    logits = jnp.dot(normed, router, preferred_element_type=jnp.float32) + router_noise
    gate_probs = jax.nn.softmax(logits, axis=-1)
    kept_mask, target, slot_table = route(picks, priority[0], capacity, experts)
    filled = slot_table < 2 * rows_dev
    token_of = slot_table % rows_dev
    buffer = jnp.where(filled[:, None], normed[token_of], jnp.zeros((), jnp.bfloat16))
    inputs = to_experts(buffer.reshape(experts, capacity, buffer.shape[1]))
    hidden_pre = (
        jnp.dot(inputs, expert_in[0], preferred_element_type=jnp.float32) + expert_in_bias[0]
    )
    hidden = gelu_exact(hidden_pre).astype(jnp.bfloat16)
    partial_value = jnp.dot(hidden, expert_out[0], preferred_element_type=jnp.float32)
    returned = from_experts(partial_value, expert_out_bias[0])
    picked_gate = jnp.take_along_axis(gate_probs, picks, axis=1)
    pair_weight = jnp.where(kept_mask, picked_gate, 0.0)
    row_index = jnp.minimum(target, experts * capacity - 1)
    first_rows = returned[row_index[:, 0]]
    second_rows = returned[row_index[:, 1]]
    branch = pair_weight[:, 0:1] * first_rows + pair_weight[:, 1:2] * second_rows
    kept_state = (
        normed,
        gate_probs,
        kept_mask,
        row_index,
        slot_table,
        inputs,
        first_rows,
        second_rows,
        pair_weight,
    )
    return (branch, kept_state)


def mixture_backward(
    router, expert_in, expert_in_bias, expert_out, picks, kept_state, grad_residual
):
    (
        normed,
        gate_probs,
        kept_mask,
        row_index,
        slot_table,
        inputs,
        first_rows,
        second_rows,
        pair_weight,
    ) = kept_state
    rows_dev = normed.shape[0]
    experts = gate_probs.shape[1]
    grad_pair = jnp.stack(
        [jnp.sum(grad_residual * first_rows, axis=1), jnp.sum(grad_residual * second_rows, axis=1)],
        axis=1,
    )
    grad_pair = jnp.where(kept_mask, grad_pair, 0.0)
    expert_ids = jnp.arange(experts, dtype=jnp.int32)[None, :]
    grad_gates = (picks[:, 0:1] == expert_ids) * grad_pair[:, 0:1] + (
        picks[:, 1:2] == expert_ids
    ) * grad_pair[:, 1:2]
    grad_logits = gate_probs * (
        grad_gates - jnp.sum(gate_probs * grad_gates, axis=1, keepdims=True)
    )
    grad_logits = grad_logits.astype(jnp.bfloat16)
    grad_router = jnp.einsum("td,te->de", normed, grad_logits, preferred_element_type=jnp.float32)
    grad_normed = jnp.einsum("te,de->td", grad_logits, router, preferred_element_type=jnp.float32)
    flat_weight = jnp.concatenate([pair_weight[:, 0], pair_weight[:, 1]])
    filled = slot_table < 2 * rows_dev
    slot_weight = jnp.where(filled, flat_weight[jnp.minimum(slot_table, 2 * rows_dev - 1)], 0.0)
    grad_buffer = (slot_weight[:, None] * grad_residual[slot_table % rows_dev]).astype(jnp.bfloat16)
    grad_outputs = to_experts(grad_buffer.reshape(experts, -1, grad_buffer.shape[1]))
    hidden_pre = (
        jnp.dot(inputs, expert_in[0], preferred_element_type=jnp.float32) + expert_in_bias[0]
    )
    hidden = gelu_exact(hidden_pre).astype(jnp.bfloat16)
    grad_out_bias = jnp.sum(grad_outputs, axis=0, dtype=jnp.float32)
    grad_out_weight = jnp.einsum(
        "sf,sd->fd", hidden, grad_outputs, preferred_element_type=jnp.float32
    )
    grad_hidden = jnp.einsum(
        "sd,fd->sf", grad_outputs, expert_out[0], preferred_element_type=jnp.float32
    )
    grad_pre = jax.vjp(gelu_exact, hidden_pre)[1](grad_hidden)[0].astype(jnp.bfloat16)
    grad_in_bias = jnp.sum(grad_pre, axis=0, dtype=jnp.float32)
    grad_in_weight = jnp.einsum("sd,sf->df", inputs, grad_pre, preferred_element_type=jnp.float32)
    zero_bias = jnp.zeros((inputs.shape[1],), jnp.float32)
    grad_inputs = from_experts(
        jnp.einsum("sf,df->sd", grad_pre, expert_in[0], preferred_element_type=jnp.float32),
        zero_bias,
    )
    grad_normed = grad_normed + jnp.where(
        kept_mask[:, 0:1], grad_inputs[row_index[:, 0]], jnp.zeros((), jnp.bfloat16)
    )
    grad_normed = grad_normed + jnp.where(
        kept_mask[:, 1:2], grad_inputs[row_index[:, 1]], jnp.zeros((), jnp.bfloat16)
    )
    expert_grads = (
        grad_in_weight[None],
        grad_in_bias[None],
        grad_out_weight[None],
        grad_out_bias[None],
    )
    return (grad_normed, grad_router, expert_grads)


def body(
    tokens,
    cotangent,
    picks,
    priority,
    router_noise,
    dense_norm_gain,
    dense_norm_bias,
    dense_attend_in,
    dense_attend_bias,
    dense_attend_out,
    dense_attend_out_bias,
    feed_norm_gain,
    feed_norm_bias,
    feed_in,
    feed_in_bias,
    feed_out,
    feed_out_bias,
    sparse_norm_gain,
    sparse_norm_bias,
    sparse_attend_in,
    sparse_attend_bias,
    sparse_attend_out,
    sparse_attend_out_bias,
    route_norm_gain,
    route_norm_bias,
    router,
    expert_in,
    expert_in_bias,
    expert_out,
    expert_out_bias,
):
    level_zero = tokens.astype(jnp.float32)
    normed = normalize(level_zero, dense_norm_gain, dense_norm_bias)
    partial_value, state_one = attend_forward(
        normed, dense_attend_in, dense_attend_bias, dense_attend_out
    )
    level_one = add_branch(level_zero, partial_value, dense_attend_out_bias)
    normed = normalize(level_one, feed_norm_gain, feed_norm_bias)
    partial_value, state_two = feed_forward(normed, feed_in, feed_in_bias, feed_out)
    level_two = add_branch(level_one, partial_value, feed_out_bias)
    normed = normalize(level_two, sparse_norm_gain, sparse_norm_bias)
    partial_value, state_three = attend_forward(
        normed, sparse_attend_in, sparse_attend_bias, sparse_attend_out
    )
    level_three = add_branch(level_two, partial_value, sparse_attend_out_bias)
    normed = normalize(level_three, route_norm_gain, route_norm_bias)
    branch, state_four = mixture_forward(
        normed,
        router,
        expert_in,
        expert_in_bias,
        expert_out,
        expert_out_bias,
        router_noise,
        picks,
        priority,
    )
    final_level = level_three + branch
    final = final_level.astype(jnp.bfloat16)
    grad_full = cotangent.astype(jnp.float32)
    mix_normed, router_grad, expert_grads = mixture_backward(
        router, expert_in, expert_in_bias, expert_out, picks, state_four, grad_full
    )
    mix_input, router_gain, router_bias = norm_backward(
        level_three, route_norm_gain, route_norm_bias, mix_normed
    )
    grad_stream = grad_full + mix_input
    partial_value, second_rest = attend_backward(
        sparse_attend_in, sparse_attend_out, state_three, rounded_grad_rows(grad_stream)
    )
    grad_stream, second_gain, second_bias = finish_norm(
        level_two, sparse_norm_gain, sparse_norm_bias, partial_value, grad_stream
    )
    partial_value, feed_rest = feed_backward(
        feed_in, feed_out, state_two, rounded_grad_rows(grad_stream)
    )
    grad_stream, feed_gain, feed_bias = finish_norm(
        level_one, feed_norm_gain, feed_norm_bias, partial_value, grad_stream
    )
    partial_value, first_rest = attend_backward(
        dense_attend_in, dense_attend_out, state_one, rounded_grad_rows(grad_stream)
    )
    grad_stream, first_gain, first_bias = finish_norm(
        level_zero, dense_norm_gain, dense_norm_bias, partial_value, grad_stream
    )
    first_proj, first_proj_bias, first_outw, first_out_bias = first_rest
    feed_inw, feed_inb, feed_outw, feed_outb = feed_rest
    second_proj, second_proj_bias, second_outw, second_out_bias = second_rest
    summed = lax.psum(
        (
            first_gain,
            first_bias,
            first_proj,
            first_proj_bias,
            first_outw,
            first_out_bias,
            feed_gain,
            feed_bias,
            feed_inw,
            feed_inb,
            feed_outw,
            feed_outb,
            second_gain,
            second_bias,
            second_proj,
            second_proj_bias,
            second_outw,
            second_out_bias,
            router_gain,
            router_bias,
            router_grad,
        ),
        "ep",
    )
    return (final, grad_stream) + tuple(summed) + expert_grads


def solution(mesh):
    in_specs = (
        P("ep", None),
        P("ep", None),
        P("ep", None),
        P("ep", None),
        P("ep", None),
        P(),
        P(),
        P(None, None, "tp"),
        P(None, "tp"),
        P("tp", None),
        P(),
        P(),
        P(),
        P(None, "tp"),
        P("tp"),
        P("tp", None),
        P(),
        P(),
        P(),
        P(None, None, "tp"),
        P(None, "tp"),
        P("tp", None),
        P(),
        P(),
        P(),
        P(),
        P("ep", None, "tp"),
        P("ep", "tp"),
        P("ep", "tp", None),
        P("ep", None),
    )
    out_specs = (
        P("ep", None),
        P("ep", None),
        P(),
        P(),
        P(None, None, "tp"),
        P(None, "tp"),
        P("tp", None),
        P(),
        P(),
        P(),
        P(None, "tp"),
        P("tp"),
        P("tp", None),
        P(),
        P(),
        P(),
        P(None, None, "tp"),
        P(None, "tp"),
        P("tp", None),
        P(),
        P(),
        P(),
        P(),
        P("ep", None, "tp"),
        P("ep", "tp"),
        P("ep", "tp", None),
        P("ep", None),
    )
    return jax.shard_map(body, mesh=mesh, in_specs=in_specs, out_specs=out_specs, check_vma=False)
```

profile of v0, /device:TPU:0, one launch (start us, length us, event | category | flops | bytes accessed | tf_op | source)
XLA Modules:
  0.0 2342.2 jit_solution(819863826242683877)
XLA Ops:
  65.8 194.9 %all-reduce.12.cloned.1.call-done = f32[3136,768]{1,0:T(8,128)} async-done(((f32[3136,768]{1,0:T(8,128)}), f32[3136,768]{1,0:T(8,128)}) %all-reduce.12.cloned.1.call-update) | async-done | bytes 9633808 | tf_op jit(solution)/shard_map/psum | solution.py:35
  279.7 25.8 %multiply_convert_fusion.4 = (bf16[3136,768]{1,0:T(8,128)(2,1)S(1)}, f32[3136,768]{1,0:T(8,128)}, f32[3136,768]{1,0:T(8,128)}) fusion(f32[768]{0:T(1024)S(1)} %copy-done.136, bf16[3136,768]{1,0:T(8,128)(2,1)S(1)} %add_convert_fusion.5, bf16[768,768]{1,0:T(8,128)(2,1)S(1)} %copy-done.132), kind=kOutput, calls=%fused_computation.108 | convolution fusion | flops 3858333696 | bytes 30084096 | tf_op jit(solution)/shard_map/dot_general | solution.py:176
  314.4 192.1 %all-reduce.14.cloned.1.call-done = f32[3136,768]{1,0:T(8,128)} async-done(((f32[3136,768]{1,0:T(8,128)}), f32[3136,768]{1,0:T(8,128)}) %all-reduce.14.cloned.1.call-update) | async-done | bytes 9633808 | tf_op jit(solution)/shard_map/psum | solution.py:35
  506.5 11.2 fusion.146
  593.3 13.9 scatter_custom_fusion
  610.0 30.2 %scatter_custom_fusion.1 = s32[3137]{0:T(1024)S(1)} fusion(s32[6272]{0:T(1024)S(1)} %fusion.115, s32[6272]{0:T(1024)S(1)} %reshape.484, s32[]{:T(128)} %constant.139.clone.1), kind=kCustom, calls=%fused_computation.279 | custom fusion | bytes 12552 | tf_op jit(solution)/shard_map/scatter | solution.py:66
  640.9 127.8 %all-reduce.16.cloned.1.call-done = f32[3136,768]{1,0:T(8,128)} async-done(((f32[3136,768]{1,0:T(8,128)}), f32[3136,768]{1,0:T(8,128)}) %all-reduce.16.cloned.1.call-update) | async-done | bytes 9633808 | tf_op jit(solution)/shard_map/psum | solution.py:35
  768.7 11.3 fusion.145
  790.2 15.9 gather_fusion.1
  823.0 16.6 gather_fusion.5
  844.7 34.2 %gather_fusion.8 = f32[6272]{0:T(1024)S(1)} fusion(f32[3136,8]{0,1:T(8,128)S(1)} %fusion.112, s32[6272]{0:T(1024)S(1)} %reshape.466), kind=kCustom, calls=%fused_computation.8 | custom fusion | bytes 100352 | tf_op jit(solution)/shard_map/jit(take_along_axis)/gather | solution.py:225
  881.3 16.6 gather_fusion.4
  904.7 17.7 all-to-all-done
  927.5 26.5 %multiply_convert_fusion.3 = (bf16[3136,768]{1,0:T(8,128)(2,1)S(1)}, f32[3136,768]{1,0:T(8,128)}, f32[3136,768]{1,0:T(8,128)}) fusion(f32[768]{0:T(1024)S(1)} %reduce.11, bf16[3136,768]{1,0:T(8,128)(2,1)} %bitcast.12, bf16[1,768,768]{2,1,0:T(8,128)(2,1)S(1)} %copy-done), kind=kOutput, calls=%fused_computation.89 | convolution fusion | flops 3858333696 | bytes 30084096 | tf_op jit(solution)/shard_map/dot_general | solution.py:220
  961.8 72.5 %all-to-all-done.2 = bf16[8,392,768]{2,1,0:T(8,128)(2,1)} async-done(((bf16[8,392,768]{2,1,0:T(8,128)(2,1)}), bf16[8,392,768]{2,1,0:T(8,128)(2,1)}, u32[]{:S(2)}, u32[]{:S(2)}) %all-to-all-start.2) | async-done | bytes 4816928 | tf_op jit(solution)/shard_map/all_to_all | solution.py:71
  1034.3 14.3 convert_reduce_fusion.5
  1055.1 190.1 %all-reduce.26.cloned.1.call-done = (bf16[3136,768]{1,0:T(8,128)(2,1)}, bf16[8,392,768]{2,1,0:T(8,128)(2,1)}) async-done(((bf16[3136,768]{1,0:T(8,128)(2,1)}, bf16[8,392,768]{2,1,0:T(8,128)(2,1)}), (bf16[3136,768]{1,0:T(8,128)(2,1)}, bf16[8,392,768]{2,1,0:T(8,128)(2,1)})) %all-reduce.26.cloned.1.call-update) | async-done | bytes 9633808 | tf_op jit(solution)/shard_map/psum | solution.py:78
  1248.5 112.1 %all_to_all.20 = bf16[8,392,768]{2,1,0:T(8,128)(2,1)} all-to-all(bf16[8,392,768]{2,1,0:T(8,128)(2,1)S(1)} %bitcast.203), channel_id=1, replica_groups=mesh['tp'=4,'ep'=8] {'ep'}, dimensions={0} | all-to-all | bytes 9633792 | tf_op jit(solution)/shard_map/all_to_all | solution.py:80
  1365.6 15.9 gather_fusion.3
  1381.5 15.9 gather_fusion.2
  1397.5 75.1 %all-to-all-done.3 = bf16[8,392,768]{2,1,0:T(8,128)(2,1)} async-done(((bf16[8,392,768]{2,1,0:T(8,128)(2,1)}), bf16[8,392,768]{2,1,0:T(8,128)(2,1)}, u32[]{:S(2)}, u32[]{:S(2)}) %all-to-all-start.3) | async-done | bytes 4816928 | tf_op jit(solution)/shard_map/all_to_all | solution.py:80
  1472.6 15.9 gather_fusion.6
  1488.5 15.9 gather_fusion.7
  1513.3 16.5 multiply_reduce_fusion.2
  1624.4 112.2 %all-reduce.18.cloned.1.call-done = bf16[3136,768]{1,0:T(8,128)(2,1)} async-done(((bf16[3136,768]{1,0:T(8,128)(2,1)}), bf16[3136,768]{1,0:T(8,128)(2,1)}) %all-reduce.18.cloned.1.call-update) | async-done | bytes 4816912 | tf_op jit(solution)/shard_map/psum | solution.py:44
  1766.4 15.3 convert_reduce_fusion.8
  1816.5 87.8 %all-reduce.20.cloned.1.call-done = bf16[3136,768]{1,0:T(8,128)(2,1)} async-done(((bf16[3136,768]{1,0:T(8,128)(2,1)}), bf16[3136,768]{1,0:T(8,128)(2,1)}) %all-reduce.20.cloned.1.call-update) | async-done | bytes 4816912 | tf_op jit(solution)/shard_map/psum | solution.py:44
  1954.1 11.2 multiply_convert_fusion
  2041.1 78.7 %all-reduce.22.cloned.1.call-done = bf16[3136,768]{1,0:T(8,128)(2,1)} async-done(((bf16[3136,768]{1,0:T(8,128)(2,1)}), bf16[3136,768]{1,0:T(8,128)(2,1)}) %all-reduce.22.cloned.1.call-update) | async-done | bytes 4816912 | tf_op jit(solution)/shard_map/psum | solution.py:44
  2134.5 33.2 %all-reduce = (f32[768]{0:T(1024)}, f32[768]{0:T(1024)}, f32[2,192]{1,0:T(2,128)}, f32[768]{0:T(1024)}, f32[768]{0:T(1024)}, /*index=5*/f32[768]{0:T(1024)}, f32...) all-reduce(f32[768]{0:T(1024)S(1)} %get-tuple-element.33, ...), channel_id=1, replica_groups=mesh['tp'=4,'ep'=8] {'ep'}, use_global_device_ids=true, to_apply=%region_41.42 | all-reduce | flops 16128 | bytes 129024 | tf_op jit(solution)/shard_map/psum | solution.py:404
  2167.7 14.9 add_add_fusion.4
  2182.6 141.0 %all-reduce.24.cloned.1.call-done = (f32[768,3,192]{0,2,1:T(8,128)}, f32[192,768]{1,0:T(8,128)}, f32[768,768]{1,0:T(8,128)}, f32[768,768]{1,0:T(8,128)}, f32[768,3,192]{0,2,1:T(8,128)}, /*index=5*/f32[192,768]{1,0:T(8,128)}) async-done(((f32[768,3,192]{0,2,1:T(8,128)}, f32[192,768]{1,0:T(8,128)}, f32[768,768]{1,0:T(8,128)}, f32[768,768]{1,0:T(8,128)}, f32[768,3,192]{0,2,1:T(8,128)}, ...) | async-done | bytes 9437200 | tf_op jit(solution)/shard_map/psum | solution.py:404
  (560 shorter events, 552.3 us)
Async XLA Ops:
  7.2 920.3 %copy-start = (bf16[1,768,768]{2,1,0:T(8,128)(2,1)S(1)}, bf16[1,768,768]{2,1,0:T(8,128)(2,1)}, u32[]{:S(2)}) copy-start(bf16[1,768,768]{2,1,0:T(8,128)(2,1)} %param.56) | copy-start | bytes 3538948
  7.3 253.5 %all-reduce.12.cloned.1.call-start = ((), (), s32[]{:S(2)}) async-start(), calls=%async_computation.4 | async-start | bytes 19267584 | tf_op jit(solution)/shard_map/psum | solution.py:35
  60.4 200.3 %copy-start.124 = (f32[768]{0:T(1024)S(1)}, f32[768]{0:T(1024)}, u32[]{:S(2)}) copy-start(f32[768]{0:T(1024)} %param.40) | copy-start | bytes 9220
  65.8 440.7 %all-reduce.14.cloned.1.call-start = ((), (), s32[]{:S(2)}) async-start(), calls=%async_computation.5 | async-start | bytes 19267584 | tf_op jit(solution)/shard_map/psum | solution.py:35
  314.2 192.3 %copy-start.117 = (f32[768]{0:T(1024)S(1)}, f32[768]{0:T(1024)}, u32[]{:S(2)}) copy-start(f32[768]{0:T(1024)} %param.46) | copy-start | bytes 9220
  314.2 454.5 %all-reduce.16.cloned.1.call-start = ((), (), s32[]{:S(2)}) async-start(), calls=%async_computation.6 | async-start | bytes 19267584 | tf_op jit(solution)/shard_map/psum | solution.py:35
  314.3 247.5 %copy-start.114 = (f32[3,64]{1,0:T(4,128)}, f32[3,64]{1,0:T(4,128)S(1)}, u32[]{:S(2)}) copy-start(f32[3,64]{1,0:T(4,128)S(1)} %add.389) | copy-start | bytes 2308
  314.4 239.2 %copy-start.102 = (f32[3,64]{1,0:T(4,128)}, f32[3,64]{1,0:T(4,128)S(1)}, u32[]{:S(2)}) copy-start(f32[3,64]{1,0:T(4,128)S(1)} %add.392) | copy-start | bytes 2308
  584.9 183.8 %copy-start.119 = (f32[768]{0:T(1024)S(1)}, f32[768]{0:T(1024)}, u32[]{:S(2)}) copy-start(f32[768]{0:T(1024)} %param.52) | copy-start | bytes 9220
  640.2 165.9 %copy-start.98 = (pred[8,392]{1,0:T(8,128)(4,1)}, pred[8,392]{1,0:T(8,128)(4,1)S(1)}, u32[]{:S(2)}) copy-start(pred[8,392]{1,0:T(8,128)(4,1)S(1)} %lt.73) | copy-start | bytes 9412
  810.3 112.1 %all-to-all-start = ((bf16[8,392,768]{2,1,0:T(8,128)(2,1)}), bf16[8,392,768]{2,1,0:T(8,128)(2,1)}, u32[]{:S(2)}, u32[]{:S(2)}) async-start(bf16[8,392,768]{2,1,0:T(8,128)(2,1)} %broadcast_select_fusion), calls=%async_computation | async-start | bytes 9633792 | tf_op jit(solution)/shard_map/all_to_all | solution.py:71
  922.4 112.0 %all-to-all-start.2 = ((bf16[8,392,768]{2,1,0:T(8,128)(2,1)}), bf16[8,392,768]{2,1,0:T(8,128)(2,1)}, u32[]{:S(2)}, u32[]{:S(2)}) async-start(bf16[8,392,768]{2,1,0:T(8,128)(2,1)} %multiply_convert_fusion.2), calls=%async_computation.2 | async-start | bytes 9633792 | tf_op jit(solution)/shard_map/all_to_all | solution.py:71
  927.0 318.2 %all-reduce.26.cloned.1.call-start = ((), (), s32[]{:S(2)}) async-start(), calls=%async_computation.11 | async-start | bytes 19267584 | tf_op jit(solution)/shard_map/psum | solution.py:78
  1248.5 116.8 %copy-start.90 = (s32[3136,2]{0,1:T(2,128)S(1)}, s32[3136,2]{0,1:T(2,128)}, u32[]{:S(2)}) copy-start(s32[3136,2]{0,1:T(2,128)} %get-tuple-element.92) | copy-start | bytes 75268
  1248.5 117.0 %copy-start.46 = (f32[16,3,196]{2,1,0:T(4,128)S(1)}, f32[16,3,196]{2,1,0:T(4,128)}, u32[]{:S(2)}) copy-start(f32[16,3,196]{2,1,0:T(4,128)} %copy-done.45) | copy-start | bytes 112900
  1248.5 117.0 %copy-start.68 = (f32[16,3,196]{2,1,0:T(4,128)S(1)}, f32[16,3,196]{2,1,0:T(4,128)}, u32[]{:S(2)}) copy-start(f32[16,3,196]{2,1,0:T(4,128)} %copy-done.67) | copy-start | bytes 112900
  1360.6 112.0 %all-to-all-start.3 = ((bf16[8,392,768]{2,1,0:T(8,128)(2,1)}), bf16[8,392,768]{2,1,0:T(8,128)(2,1)}, u32[]{:S(2)}, u32[]{:S(2)}) async-start(bf16[8,392,768]{2,1,0:T(8,128)(2,1)} %get-tuple-element.81), calls=%async_computation.3 | async-start | bytes 9633792 | tf_op jit(solution)/shard_map/all_to_all | solution.py:80
  1365.2 371.5 %all-reduce.18.cloned.1.call-start = ((), (), s32[]{:S(2)}) async-start(), calls=%async_computation.7 | async-start | bytes 9633792 | tf_op jit(solution)/shard_map/psum | solution.py:44
  1617.3 119.3 %copy-start.42 = (f32[3136]{0:T(1024)S(1)}, f32[3136]{0:T(1024)}, u32[]{:S(2)}) copy-start(f32[3136]{0:T(1024)} %copy-done.41) | copy-start | bytes 37636
  1617.3 119.3 %copy-start.92 = (f32[768]{0:T(1024)S(1)}, f32[768]{0:T(1024)}, u32[]{:S(2)}) copy-start(f32[768]{0:T(1024)} %param.47) | copy-start | bytes 9220
  1624.4 121.3 %copy-start.83 = (f32[3136]{0:T(1024)S(1)}, f32[3136]{0:T(1024)}, u32[]{:S(2)}) copy-start(f32[3136]{0:T(1024)} %copy-done.82) | copy-start | bytes 37636
  1624.4 121.3 %copy-start.60 = (f32[3136]{0:T(1024)S(1)}, f32[3136]{0:T(1024)}, u32[]{:S(2)}) copy-start(f32[3136]{0:T(1024)} %copy-done.59) | copy-start | bytes 37636
  1624.4 279.9 %all-reduce.20.cloned.1.call-start = ((), (), s32[]{:S(2)}) async-start(), calls=%async_computation.8 | async-start | bytes 9633792 | tf_op jit(solution)/shard_map/psum | solution.py:44
  1789.5 330.2 %all-reduce.22.cloned.1.call-start = ((), (), s32[]{:S(2)}) async-start(), calls=%async_computation.9 | async-start | bytes 9633792 | tf_op jit(solution)/shard_map/psum | solution.py:44
  1804.6 99.7 %copy-start.51 = (f32[3136]{0:T(1024)S(1)}, f32[3136]{0:T(1024)}, u32[]{:S(2)}) copy-start(f32[3136]{0:T(1024)} %copy-done.50) | copy-start | bytes 37636
  1804.6 99.7 %copy-start.62 = (f32[3136]{0:T(1024)S(1)}, f32[3136]{0:T(1024)}, u32[]{:S(2)}) copy-start(f32[3136]{0:T(1024)} %copy-done.61) | copy-start | bytes 37636
  1804.6 99.7 %copy-start.95 = (f32[768]{0:T(1024)S(1)}, f32[768]{0:T(1024)}, u32[]{:S(2)}) copy-start(f32[768]{0:T(1024)} %param.41) | copy-start | bytes 9220
  1814.5 99.8 %copy-start.81 = (f32[3136]{0:T(1024)S(1)}, f32[3136]{0:T(1024)}, u32[]{:S(2)}) copy-start(f32[3136]{0:T(1024)} %copy-done.80) | copy-start | bytes 37636
  2005.0 318.7 %all-reduce.24.cloned.1.call-start = ((), (), s32[]{:S(2)}) async-start(), calls=%async_computation.10 | async-start | bytes 18874368 | tf_op jit(solution)/shard_map/psum | solution.py:404
  2041.0 93.5 %copy-start.107 = (f32[768]{0:T(1024)S(1)}, f32[768]{0:T(1024)}, u32[]{:S(2)}) copy-start(f32[768]{0:T(1024)} %get-tuple-element.36) | copy-start | bytes 9220
  2041.0 93.5 %copy-start.108 = (f32[768]{0:T(1024)S(1)}, f32[768]{0:T(1024)}, u32[]{:S(2)}) copy-start(f32[768]{0:T(1024)} %get-tuple-element.29) | copy-start | bytes 9220
  2041.0 93.5 %copy-start.121 = (f32[768]{0:T(1024)S(1)}, f32[768]{0:T(1024)}, u32[]{:S(2)}) copy-start(f32[768]{0:T(1024)} %get-tuple-element.27) | copy-start | bytes 9220
  (153 other events, 1883.4 us)
Sparse Core Ops, SparseCore 0:
  65.9 194.8 all-reduce.11
  314.3 192.1 all-reduce.13
  576.5 192.1 all-reduce.15
  1054.6 190.5 all-reduce.25
  1624.5 112.1 all-reduce.17
  1789.7 114.5 all-reduce.19
  2005.1 114.5 all-reduce.21
  2124.3 199.3 all-reduce.23
where the time goes:
time: 2350 us; the launch traced here: 2340 us
  waiting for transfers between devices  1290 us (55%)
  local copies, waits for them, and re-layouts  364 us (15%)
  matrix products  286 us (12%)
  other arithmetic  225 us (10%)
  blocking collectives  145 us (6%)
    psum x3, waiting for transfers between devices, add_branch(): return stream + lax.psum(partial_value, 'tp') + bias_row  515 us
    psum x3, waiting for transfers between devices, finish_norm(): lax.psum(partial_value.astype(jnp.bfloat16), 'tp').astype(jnp.float32)  279 us
    psum x1, waiting for transfers between devices, from_experts(): lax.psum(partial_value.astype(jnp.bfloat16), 'tp').astype(jnp.float32)  190 us
    psum x1, waiting for transfers between devices, body(): lax.psum((first_gain, first_bias, first_proj, first_proj_bias, first_outw...  141 us
    all_to_all x1, blocking collectives, from_experts(): lax.all_to_all(summed_rows.reshape(sources, -1, summed_rows.shape[1]), 'e...  112 us
    all_to_all x2, waiting for transfers between devices, to_experts(): lax.all_to_all(buffer, 'ep', split_axis=0, concat_axis=0, tiled=True)  90.2 us
    all_to_all x1, waiting for transfers between devices, from_experts(): lax.all_to_all(summed_rows.reshape(sources, -1, summed_rows.shape[1]), 'e...  75.1 us
  transfers between devices with their start and end apart: 11, of which 11 were waited for; matrix products, arithmetic and copies ran while one was open for 13% of the time, Pallas kernels for 0%

commit v1 on v0

v1 whole, which is shorter than its diff:
```python
import jax
import jax.numpy as jnp
from jax import lax
from jax.experimental import pallas as pl
from jax.experimental.pallas import tpu as pltpu
from jax.sharding import PartitionSpec as P

HEAD = 64
LEN = 196
PAD = 208
EPSILON = 1e-06
BF = jnp.bfloat16
F32 = jnp.float32
NN = ((1,), (0,))
NT = ((1,), (1,))
TN = ((0,), (0,))
SQRT_HALF = 0.7071067811865476
VMEM_LIMIT = 60 * 1024 * 1024


def dot(a, b, dims):
    return lax.dot_general(a, b, (dims, ((), ())), preferred_element_type=F32)


def norm_parts(x):
    average = jnp.mean(x, axis=-1, keepdims=True)
    centred = x - average
    variance = jnp.mean(centred * centred, axis=-1, keepdims=True)
    scale = lax.rsqrt(variance + EPSILON)
    return centred * scale, scale


def norm_back(hat, scale, gain, grad):
    inner = grad * gain
    first = jnp.mean(inner, axis=-1, keepdims=True)
    second = jnp.mean(inner * hat, axis=-1, keepdims=True)
    return scale * (inner - first - hat * second)


def gelu_parts(u):
    z = jnp.abs(u) * SQRT_HALF
    t = 1.0 / (1.0 + 0.3275911 * z)
    bell = jnp.exp(-(z * z))
    poly = t * (
        0.254829592
        + t * (-0.284496736 + t * (1.421413741 + t * (-1.453152027 + t * 1.061405429)))
    )
    tail = 0.5 * poly * bell
    cdf = jnp.where(u >= 0.0, 1.0 - tail, tail)
    return u * cdf, cdf + u * (bell * 0.3989422804014327)


def whole():
    return pl.BlockSpec(memory_space=pltpu.VMEM)


def params(semantics=1):
    return pltpu.CompilerParams(
        dimension_semantics=("arbitrary",) * semantics, vmem_limit_bytes=VMEM_LIMIT
    )


def key_mask():
    rows = lax.broadcasted_iota(jnp.int32, (PAD, 1), 0)
    return jnp.where(rows < LEN, 0.0, -1e30)


def attend_backward_kernel(
    g_ref,
    h_ref,
    gain_ref,
    bias_ref,
    w_ref,
    qkv_ref,
    lse_ref,
    ctx_ref,
    gout_ref,
    dw_ref,
    small_ref,
    acc_ref,
    dqkv_ref,
    dc_ref,
    db_ref,
):
    step = pl.program_id(0)
    mine = lax.axis_index("tp")
    shards = w_ref.shape[0]
    width = w_ref.shape[1] // 4
    heads = width // HEAD

    @pl.when(step == 0)
    def _():
        acc_ref[...] = jnp.zeros_like(acc_ref)
        db_ref[...] = jnp.zeros_like(db_ref)
        small_ref[...] = jnp.zeros_like(small_ref)

    grad = g_ref[...]
    hat, scale = norm_parts(h_ref[...])
    a = (hat * gain_ref[...] + bias_ref[...]).astype(BF)
    gr = grad.astype(BF)
    mask = key_mask()
    da = jnp.zeros(grad.shape, F32)
    factor = HEAD**-0.5
    for r in range(shards):
        dc_ref[...] = dot(w_ref[r, 3 * width :, :], gr, NT).astype(BF)
        acc_ref[r, 3 * width :, :] += dot(ctx_ref[0, r], gr, NN)
        for h in range(heads):
            lo = HEAD * h
            q = qkv_ref[0, r, lo : lo + HEAD, :]
            k = qkv_ref[0, r, width + lo : width + lo + HEAD, :]
            v = qkv_ref[0, r, 2 * width + lo : 2 * width + lo + HEAD, :]
            dc = dc_ref[lo : lo + HEAD, :]
            s = dot(k, q, TN) * factor + mask
            p = jnp.exp(s - lse_ref[0, r, h : h + 1, :])
            pb = p.astype(BF)
            dp = dot(v, dc, TN)
            dv = dot(dc, pb, NT)
            pdp = p * dp
            delta = jnp.sum(pdp, axis=0, keepdims=True)
            ds = (pdp - p * delta).astype(BF)
            dq = dot(k, ds, NN) * factor
            dk = dot(q, ds, NT) * factor
            dqkv_ref[lo : lo + HEAD, :] = dq.astype(BF)
            dqkv_ref[width + lo : width + lo + HEAD, :] = dk.astype(BF)
            dqkv_ref[2 * width + lo : 2 * width + lo + HEAD, :] = dv.astype(BF)
        dqkv = dqkv_ref[...]
        acc_ref[r, : 3 * width, :] += dot(dqkv, a, NN)
        db_ref[r] += jnp.sum(dqkv.astype(F32), axis=1, keepdims=True)
        da += dot(dqkv, w_ref[r, : 3 * width, :], TN)
    gout_ref[...] = grad + norm_back(hat, scale, gain_ref[...], da)
    small_ref[0:1, :] += jnp.sum(da * hat, axis=0, keepdims=True)
    small_ref[1:2, :] += jnp.sum(da, axis=0, keepdims=True)
    small_ref[2:3, :] += jnp.sum(gr.astype(F32), axis=0, keepdims=True)

    @pl.when(step == pl.num_programs(0) - 1)
    def _():
        dw_ref[...] = acc_ref[...].astype(BF)
        for r in range(shards):
            line = jnp.transpose(jnp.broadcast_to(db_ref[r], (3 * width, 128)))[0:1, :]
            line = jnp.concatenate([line, jnp.zeros((1, width), F32)], axis=1)
            small_ref[pl.ds(3 + (mine ^ r), 1), :] = line


def attend_backward(grad, h, gain, bias, w, kept):
    qkv, lse, ctx = kept
    rows, depth = h.shape
    images = rows // PAD
    shards, four, _ = w.shape
    width = four // 4
    heads = width // HEAD
    row_block = pl.BlockSpec((PAD, depth), lambda i: (i, 0))
    flops = 2 * rows * depth * depth * 4 + 4 * rows * PAD * depth
    return pl.pallas_call(
        attend_backward_kernel,
        grid=(images,),
        in_specs=[
            row_block,
            row_block,
            whole(),
            whole(),
            whole(),
            pl.BlockSpec((1, shards, 3 * width, PAD), lambda i: (i, 0, 0, 0)),
            pl.BlockSpec((1, shards, heads, PAD), lambda i: (i, 0, 0, 0)),
            pl.BlockSpec((1, shards, width, PAD), lambda i: (i, 0, 0, 0)),
        ],
        out_specs=[row_block, whole(), whole()],
        out_shape=[
            jax.ShapeDtypeStruct((rows, depth), F32),
            jax.ShapeDtypeStruct((shards, four, depth), BF),
            jax.ShapeDtypeStruct((8, depth), F32),
        ],
        scratch_shapes=[
            pltpu.VMEM((shards, four, depth), F32),
            pltpu.VMEM((3 * width, PAD), BF),
            pltpu.VMEM((width, PAD), BF),
            pltpu.VMEM((shards, 3 * width, 1), F32),
        ],
        compiler_params=params(),
        cost_estimate=pl.CostEstimate(
            flops=flops * 6, bytes_accessed=30_000_000, transcendentals=rows * PAD * 12
        ),
        name="attend_backward",
    )(grad, h, gain, bias, w, qkv, lse, ctx)


def feed_backward_kernel(
    g_ref,
    h_ref,
    gain_ref,
    bias_ref,
    w_ref,
    hid_ref,
    slope_ref,
    gout_ref,
    dw_ref,
    small_ref,
    m_ref,
    gr_ref,
    dm_ref,
):
    step = pl.program_id(0)
    depth = h_ref.shape[1]
    mine = lax.axis_index("tp")

    @pl.when(step == 0)
    def _():
        hat, _ = norm_parts(h_ref[...])
        m_ref[...] = (hat * gain_ref[...] + bias_ref[...]).astype(BF)
        gr_ref[...] = g_ref[...].astype(BF)
        dm_ref[...] = jnp.zeros_like(dm_ref)

    gr = gr_ref[...]
    dw_ref[0, depth:, :] = dot(hid_ref[0], gr, TN).astype(BF)
    dr = dot(gr, w_ref[0, depth:, :], NT)
    du = (slope_ref[0].astype(F32) * dr).astype(BF)
    small_ref[pl.ds(3 + (mine ^ step), 1), :] = jnp.sum(du.astype(F32), axis=0, keepdims=True)
    dw_ref[0, :depth, :] = dot(m_ref[...], du, TN).astype(BF)
    dm_ref[...] += dot(du, w_ref[0, :depth, :], NT)

    @pl.when(step == pl.num_programs(0) - 1)
    def _():
        hat, scale = norm_parts(h_ref[...])
        dm = dm_ref[...]
        gout_ref[...] = g_ref[...] + norm_back(hat, scale, gain_ref[...], dm)
        small_ref[0:1, :] = jnp.sum(dm * hat, axis=0, keepdims=True)
        small_ref[1:2, :] = jnp.sum(dm, axis=0, keepdims=True)
        small_ref[2:3, :] = jnp.sum(gr_ref[...].astype(F32), axis=0, keepdims=True)
        small_ref[7:8, :] = jnp.zeros((1, depth), F32)


def feed_backward(grad, h, gain, bias, w, kept):
    hid, slope = kept
    rows, depth = h.shape
    shards, double, hidden = w.shape
    shard = lambda i: (i, 0, 0)
    return pl.pallas_call(
        feed_backward_kernel,
        grid=(shards,),
        in_specs=[
            whole(),
            whole(),
            whole(),
            whole(),
            pl.BlockSpec((1, double, hidden), shard),
            pl.BlockSpec((1, rows, hidden), shard),
            pl.BlockSpec((1, rows, hidden), shard),
        ],
        out_specs=[
            whole(),
            pl.BlockSpec((1, double, hidden), shard),
            whole(),
        ],
        out_shape=[
            jax.ShapeDtypeStruct((rows, depth), F32),
            jax.ShapeDtypeStruct((shards, double, hidden), BF),
            jax.ShapeDtypeStruct((8, depth), F32),
        ],
        scratch_shapes=[
            pltpu.VMEM((rows, depth), BF),
            pltpu.VMEM((rows, depth), BF),
            pltpu.VMEM((rows, depth), F32),
        ],
        compiler_params=params(),
        cost_estimate=pl.CostEstimate(
            flops=8 * rows * depth * hidden * shards * 2,
            bytes_accessed=35_000_000,
            transcendentals=0,
        ),
        name="feed_backward",
    )(grad, h, gain, bias, w, hid, slope)


def expert_pair(mine_ref, other_ref):
    first = lax.rem(lax.axis_index("ep"), 2) == 0
    mine, other = mine_ref[0], other_ref[0]
    return jnp.where(first, mine, other), jnp.where(first, other, mine)


def expert_forward_kernel(x_ref, mine_ref, other_ref, b1_ref, b2_ref, y_ref, hid_ref, slope_ref, acc_ref):
    r = pl.program_id(0)

    @pl.when(r == 0)
    def _():
        acc_ref[...] = jnp.zeros_like(acc_ref)

    w_in, w_out = expert_pair(mine_ref, other_ref)
    u = dot(x_ref[...], w_in, NN) + b1_ref[0]
    value, slope = gelu_parts(u)
    value = value.astype(BF)
    hid_ref[0] = value
    slope_ref[0] = slope.astype(BF)
    acc_ref[...] += dot(value, w_out, NN)

    @pl.when(r == pl.num_programs(0) - 1)
    def _():
        y_ref[...] = (acc_ref[...] + b2_ref[...]).astype(BF)


def expert_forward(x, mine, other, b1, b2):
    rows, depth = x.shape
    shards, _, hidden = mine.shape
    shard = lambda r: (r, 0, 0)
    wide = pl.BlockSpec((1, rows, hidden), shard)
    weight = pl.BlockSpec((1, depth, hidden), shard)
    return pl.pallas_call(
        expert_forward_kernel,
        grid=(shards,),
        in_specs=[whole(), weight, weight, pl.BlockSpec((1, 1, hidden), shard), whole()],
        out_specs=[whole(), wide, wide],
        out_shape=[
            jax.ShapeDtypeStruct((rows, depth), BF),
            jax.ShapeDtypeStruct((shards, rows, hidden), BF),
            jax.ShapeDtypeStruct((shards, rows, hidden), BF),
        ],
        scratch_shapes=[pltpu.VMEM((rows, depth), F32)],
        compiler_params=params(),
        cost_estimate=pl.CostEstimate(
            flops=4 * rows * depth * hidden * shards * 2,
            bytes_accessed=25_000_000,
            transcendentals=rows * hidden * shards,
        ),
        name="expert_forward",
    )(x, mine, other, b1, b2)


def expert_input_kernel(
    y_ref,
    cot_ref,
    gate_ref,
    mine_ref,
    other_ref,
    slope_ref,
    wy_ref,
    dy_ref,
    dx_ref,
    dgate_ref,
    du_ref,
    small_ref,
    acc_ref,
):
    r = pl.program_id(0)
    mine = lax.axis_index("tp")

    @pl.when(r == 0)
    def _():
        y = y_ref[...].astype(F32)
        cot = cot_ref[...].astype(F32)
        gate = gate_ref[...]
        dgate_ref[...] = jnp.sum(cot * y, axis=1, keepdims=True)
        wy_ref[...] = (gate * y).astype(BF)
        dy = (gate * cot).astype(BF)
        dy_ref[...] = dy
        small_ref[4:5, :] = jnp.sum(dy.astype(F32), axis=0, keepdims=True)
        small_ref[5:8, :] = jnp.zeros((3, dy.shape[1]), F32)
        acc_ref[...] = jnp.zeros_like(acc_ref)

    w_in, w_out = expert_pair(mine_ref, other_ref)
    dr = dot(dy_ref[...], w_out, NT)
    du = (slope_ref[0].astype(F32) * dr).astype(BF)
    du_ref[0] = du
    small_ref[pl.ds(mine ^ r, 1), :] = jnp.sum(du.astype(F32), axis=0, keepdims=True)
    acc_ref[...] += dot(du, w_in, NT)

    @pl.when(r == pl.num_programs(0) - 1)
    def _():
        dx_ref[...] = acc_ref[...].astype(BF)


def expert_input(y, cot, gate, mine, other, slope):
    rows, depth = y.shape
    shards, _, hidden = mine.shape
    shard = lambda r: (r, 0, 0)
    wide = pl.BlockSpec((1, rows, hidden), shard)
    weight = pl.BlockSpec((1, depth, hidden), shard)
    return pl.pallas_call(
        expert_input_kernel,
        grid=(shards,),
        in_specs=[whole(), whole(), whole(), weight, weight, wide],
        out_specs=[
            whole(),
            whole(),
            whole(),
            whole(),
            wide,
            whole(),
        ],
        out_shape=[
            jax.ShapeDtypeStruct((rows, depth), BF),
            jax.ShapeDtypeStruct((rows, depth), BF),
            jax.ShapeDtypeStruct((rows, depth), BF),
            jax.ShapeDtypeStruct((rows, 1), F32),
            jax.ShapeDtypeStruct((shards, rows, hidden), BF),
            jax.ShapeDtypeStruct((8, depth), F32),
        ],
        scratch_shapes=[pltpu.VMEM((rows, depth), F32)],
        compiler_params=params(),
        cost_estimate=pl.CostEstimate(
            flops=4 * rows * depth * hidden * shards * 2,
            bytes_accessed=25_000_000,
            transcendentals=0,
        ),
        name="expert_input",
    )(y, cot, gate, mine, other, slope)


def expert_weight_kernel(x_ref, dy_ref, hid_ref, du_ref, dw_ref):
    depth = x_ref.shape[1]
    dw_ref[0, depth:, :] = dot(hid_ref[0], dy_ref[...], TN).astype(BF)
    dw_ref[0, :depth, :] = dot(x_ref[...], du_ref[0], TN).astype(BF)


def expert_weight(x, dy, hid, du):
    rows, depth = x.shape
    shards, _, hidden = hid.shape
    shard = lambda r: (r, 0, 0)
    wide = pl.BlockSpec((1, rows, hidden), shard)
    return pl.pallas_call(
        expert_weight_kernel,
        grid=(shards,),
        in_specs=[whole(), whole(), wide, wide],
        out_specs=pl.BlockSpec((1, 2 * depth, hidden), shard),
        out_shape=jax.ShapeDtypeStruct((shards, 2 * depth, hidden), BF),
        compiler_params=params(),
        cost_estimate=pl.CostEstimate(
            flops=4 * rows * depth * hidden * shards * 2,
            bytes_accessed=25_000_000,
            transcendentals=0,
        ),
        name="expert_weight",
    )(x, dy, hid, du)


ROUTES = 6


def attend_image(x, gain, bias, w_ref, biases_ref, bias_row, bout, qkv_ref, lse_ref, ctx_ref):
    shards = w_ref.shape[0]
    width = w_ref.shape[1] // 4
    heads = width // HEAD
    hat, _ = norm_parts(x)
    a = (hat * gain + bias).astype(BF)
    mask = key_mask()
    branch = jnp.zeros(x.shape, F32)
    for r in range(shards):
        column = jnp.transpose(biases_ref[r])[: 3 * width, bias_row : bias_row + 1]
        qkv = (dot(w_ref[r, : 3 * width, :], a, NT) + column).astype(BF)
        qkv_ref[0, r] = qkv
        for h in range(heads):
            q = qkv[HEAD * h : HEAD * (h + 1)]
            k = qkv[width + HEAD * h : width + HEAD * (h + 1)]
            v = qkv[2 * width + HEAD * h : 2 * width + HEAD * (h + 1)]
            s = dot(k, q, TN) * (HEAD**-0.5) + mask
            peak = jnp.max(s, axis=0, keepdims=True)
            e = jnp.exp(s - peak)
            total = jnp.sum(e, axis=0, keepdims=True)
            lse_ref[0, r, h : h + 1, :] = peak + jnp.log(total)
            c = dot(v, e.astype(BF), NN) * (1.0 / total)
            ctx_ref[0, r, HEAD * h : HEAD * (h + 1), :] = c.astype(BF)
        branch += dot(ctx_ref[0, r], w_ref[r, 3 * width :, :], TN)
    return x + branch + bout


def forward_kernel(
    x_ref,
    vec_ref,
    bias_ref,
    one_ref,
    feed_ref,
    two_ref,
    h1_ref,
    h2_ref,
    h3_ref,
    qkv1_ref,
    lse1_ref,
    ctx1_ref,
    hid_ref,
    slope_ref,
    qkv2_ref,
    lse2_ref,
    ctx2_ref,
    w1_out,
    wf_out,
    w2_out,
    normed_out,
    biases_out,
    h_ref,
    w1_ref,
    wf_ref,
    w2_ref,
    b_ref,
    n_ref,
    send_sem,
    recv_sem,
    n_send,
    n_recv,
    small_send,
    small_recv,
    local_sem,
):
    step = pl.program_id(0)
    images = 4
    mine = lax.axis_index("tp")
    place = lax.axis_index("ep")
    core = lax.rem(place, 2)
    side = lax.rem(mine, 2)
    to_x = {"tp": mine ^ 1}
    to_y = {"tp": mine ^ 2}
    to_far = {"tp": mine ^ 3}
    to_core = {"ep": place ^ 1}
    depth = x_ref.shape[1]

    def remote(src, dst, sends, recvs, index, peer):
        return pltpu.make_async_remote_copy(
            src_ref=src,
            dst_ref=dst,
            send_sem=sends.at[index],
            recv_sem=recvs.at[index],
            device_id=peer,
            device_id_type=pl.DeviceIdType.MESH,
        )

    def copies(group, own, full):
        rows = own.shape[0] // 2
        start = pl.multiple_of(core * rows, rows)
        quarter = rows // 2
        middle = pl.multiple_of(start + quarter, quarter)
        half = pl.ds(start, rows)
        low = pl.ds(start, quarter)
        high = pl.ds(middle, quarter)

        def make(k, src, dst, peer):
            return remote(src, dst, send_sem, recv_sem, (group, k), peer)

        return [
            make(0, own.at[half], full.at[1, half], to_x),
            make(1, own.at[half], full.at[2, half], to_y),
            make(2, full.at[1, low], full.at[3, low], to_y),
            make(3, full.at[2, high], full.at[3, high], to_x),
            make(4, full.at[pl.ds(1, 2), half], full.at[pl.ds(1, 2), half], to_core),
            make(5, full.at[3, half], full.at[3, half], to_core),
        ]

    one = copies(0, one_ref, w1_ref)
    feed = copies(1, feed_ref, wf_ref)
    two = copies(2, two_ref, w2_ref)

    small = [
        remote(bias_ref, b_ref.at[r], small_send, small_recv, r - 1, peer)
        for r, peer in ((1, to_x), (2, to_y), (3, to_far))
    ]
    own_local = [
        pltpu.make_async_copy(one_ref, w1_ref.at[0], local_sem.at[0]),
        pltpu.make_async_copy(feed_ref, wf_ref.at[0], local_sem.at[1]),
        pltpu.make_async_copy(two_ref, w2_ref.at[0], local_sem.at[2]),
    ]
    saves = [
        pltpu.make_async_copy(w1_ref, w1_out, local_sem.at[4]),
        pltpu.make_async_copy(wf_ref, wf_out, local_sem.at[5]),
        pltpu.make_async_copy(w2_ref, w2_out, local_sem.at[6]),
    ]

    def rows_copy(i):
        rows = pl.ds(PAD * i, PAD)
        low, high = pl.ds(PAD * i, 96), pl.ds(PAD * i + 96, PAD - 96)
        return [
            remote(n_ref.at[i], normed_out.at[1, rows], n_send, n_recv, (0, i), to_x),
            remote(n_ref.at[i], normed_out.at[2, rows], n_send, n_recv, (1, i), to_y),
            remote(normed_out.at[1, low], normed_out.at[3, low], n_send, n_recv, (2, i), to_y),
            remote(normed_out.at[2, high], normed_out.at[3, high], n_send, n_recv, (3, i), to_x),
            pltpu.make_async_copy(n_ref.at[i], normed_out.at[0, rows], local_sem.at[8 + i]),
        ]

    def vec(k):
        return vec_ref[k : k + 1, :]

    @pl.when(step == 0)
    def _():
        barrier = pltpu.get_barrier_semaphore()
        for peer in (to_x, to_y, to_far, to_core):
            pl.semaphore_signal(barrier, inc=1, device_id=peer, device_id_type=pl.DeviceIdType.MESH)
        pl.semaphore_wait(barrier, 4)
        one[0].start()
        one[1].start()
        own_local[0].start()
        for copy in small:
            copy.start()
        b_ref[0] = bias_ref[...]
        one[0].wait_recv()
        one[1].wait_recv()
        one[2].start()
        one[3].start()
        one[4].start()
        one[2].wait_recv()
        one[3].wait_recv()
        one[5].start()
        feed[0].start()
        feed[1].start()
        own_local[1].start()
        own_local[2].start()
        own_local[0].wait()
        for copy in small:
            copy.wait_recv()
        one[4].wait_recv()
        one[5].wait_recv()

    @pl.when(step == 2)
    def _():
        saves[0].start()
        feed[0].wait_recv()
        feed[1].wait_recv()
        feed[2].start()
        feed[3].start()
        feed[4].start()

    @pl.when(step == 4)
    def _():
        feed[2].wait_recv()
        feed[3].wait_recv()
        feed[5].start()
        two[0].start()
        two[1].start()
        own_local[1].wait()
        feed[4].wait_recv()
        feed[5].wait_recv()

    @pl.when(step == 6)
    def _():
        saves[1].start()
        two[0].wait_recv()
        two[1].wait_recv()
        two[2].start()
        two[3].start()
        two[4].start()

    @pl.when(step == 7)
    def _():
        two[2].wait_recv()
        two[3].wait_recv()
        two[5].start()

    @pl.when(step == 8)
    def _():
        own_local[2].wait()
        two[4].wait_recv()
        two[5].wait_recv()

    @pl.when(step == 10)
    def _():
        saves[2].start()

    @pl.when(step < images)
    def _():
        x = x_ref[pl.ds(pl.multiple_of(step * PAD, PAD), PAD), :].astype(F32)
        h = attend_image(
            x, vec(0), vec(1), w1_ref, b_ref, 0, vec(2), qkv1_ref, lse1_ref, ctx1_ref
        )
        h_ref[step] = h
        h1_ref[...] = h

    @pl.when((step >= images) & (step < 2 * images))
    def _():
        tile = step - images
        x = h_ref[tile]
        hat, _ = norm_parts(x)
        m = (hat * vec(3) + vec(4)).astype(BF)
        acc = x + vec(5)
        for r in range(wf_ref.shape[0]):
            u = dot(m, wf_ref[r, :depth, :], NN) + b_ref[r, 2:3, :]
            value, slope = gelu_parts(u)
            value = value.astype(BF)
            hid_ref[r] = value
            slope_ref[r] = slope.astype(BF)
            acc += dot(value, wf_ref[r, depth:, :], NN)
        h_ref[tile] = acc
        h2_ref[...] = acc

    @pl.when(step >= 2 * images)
    def _():
        image = step - 2 * images
        h = attend_image(
            h_ref[image], vec(6), vec(7), w2_ref, b_ref, 1, vec(8), qkv2_ref, lse2_ref, ctx2_ref
        )
        h3_ref[...] = h
        hat, _ = norm_parts(h)
        n_ref[image] = (hat * vec(9) + vec(10)).astype(BF)

    for i in range(images):

        @pl.when(step == 2 * images + i)
        def _(i=i):
            to_send = rows_copy(i)
            to_send[0].start()
            to_send[1].start()
            to_send[4].start()
            if i > 0:
                before = rows_copy(i - 1)
                before[0].wait_recv()
                before[1].wait_recv()
                before[2].start()
                before[3].start()

    @pl.when(step == 3 * images - 1)
    def _():
        last = rows_copy(images - 1)
        last[0].wait_recv()
        last[1].wait_recv()
        last[2].start()
        last[3].start()
        pltpu.make_async_copy(b_ref, biases_out, local_sem.at[7]).start()
        for i in range(images):
            moved = rows_copy(i)
            moved[2].wait_recv()
            moved[3].wait_recv()
            for k in range(4):
                moved[k].wait_send()
            moved[4].wait()
        for group in (one, feed, two):
            for copy in group:
                copy.wait_send()
        for copy in small:
            copy.wait_send()
        for copy in saves:
            copy.wait()
        pltpu.make_async_copy(b_ref, biases_out, local_sem.at[7]).wait()


def dense_forward(x, vectors, bias, pack_one, pack_feed, pack_two):
    rows, depth = x.shape
    images = rows // PAD
    shards = 4
    four = pack_one.shape[0]
    width = four // 4
    heads = width // HEAD
    double, hidden = pack_feed.shape
    any_spec = pl.BlockSpec(memory_space=pl.ANY)

    def part(number):
        return lambda s: jnp.clip(s - images * number, 0, images - 1)

    def row_spec(number):
        at = part(number)
        return pl.BlockSpec((PAD, depth), lambda s: (at(s), 0))

    def attend_specs(number):
        at = part(number)
        return [
            pl.BlockSpec((1, shards, 3 * width, PAD), lambda s: (at(s), 0, 0, 0)),
            pl.BlockSpec((1, shards, heads, PAD), lambda s: (at(s), 0, 0, 0)),
            pl.BlockSpec((1, shards, width, PAD), lambda s: (at(s), 0, 0, 0)),
        ]

    tile_at = part(1)
    hid_spec = pl.BlockSpec((shards, PAD, hidden), lambda s: (0, tile_at(s), 0))
    shape = jax.ShapeDtypeStruct
    attend_shapes = [
        shape((images, shards, 3 * width, PAD), BF),
        shape((images, shards, heads, PAD), F32),
        shape((images, shards, width, PAD), BF),
    ]
    out = pl.pallas_call(
        forward_kernel,
        grid=(3 * images,),
        in_specs=[whole(), whole(), whole()] + [any_spec] * 3,
        out_specs=[row_spec(0), row_spec(1), row_spec(2)]
        + attend_specs(0)
        + [hid_spec, hid_spec]
        + attend_specs(2)
        + [any_spec] * 5,
        out_shape=[shape((rows, depth), F32)] * 3
        + attend_shapes
        + [shape((shards, rows, hidden), BF)] * 2
        + attend_shapes
        + [
            shape((shards, four, depth), BF),
            shape((shards, double, hidden), BF),
            shape((shards, four, depth), BF),
            shape((shards, rows, depth), BF),
            shape((shards, 8, depth), F32),
        ],
        scratch_shapes=[
            pltpu.VMEM((images, PAD, depth), F32),
            pltpu.VMEM((shards, four, depth), BF),
            pltpu.VMEM((shards, double, hidden), BF),
            pltpu.VMEM((shards, four, depth), BF),
            pltpu.VMEM((shards, 8, depth), F32),
            pltpu.VMEM((images, PAD, depth), BF),
            pltpu.SemaphoreType.DMA((3, ROUTES)),
            pltpu.SemaphoreType.DMA((3, ROUTES)),
            pltpu.SemaphoreType.DMA((4, 4)),
            pltpu.SemaphoreType.DMA((4, 4)),
            pltpu.SemaphoreType.DMA((3,)),
            pltpu.SemaphoreType.DMA((3,)),
            pltpu.SemaphoreType.DMA((12,)),
        ],
        compiler_params=pltpu.CompilerParams(
            dimension_semantics=("arbitrary",),
            vmem_limit_bytes=VMEM_LIMIT,
            collective_id=0,
            has_side_effects=True,
        ),
        cost_estimate=pl.CostEstimate(
            flops=60_000_000_000, bytes_accessed=60_000_000, transcendentals=10_000_000
        ),
        name="dense_forward",
    )(x, vectors, bias, pack_one, pack_feed, pack_two)
    (h1, h2, h3, q1, l1, c1, hid, slope, q2, l2, c2, w1, wf, w2, normed, biases) = out
    return (h1, h2, h3), (q1, l1, c1), (hid, slope), (q2, l2, c2), (w1, wf, w2), normed, biases


TAIL_ORDER = (0, 1, 2, 3, 0, 1, 0, 2, 0, 1, 3, 0, 1, 2, 4, 0, 3, 1, 2, 0, 3, 1, 2, 4, 0, 3, 1, 2, 4)


def add_rows(dst, src, rows):
    tile = 48

    def body(i, carry):
        at = pl.ds(pl.multiple_of(i * tile, 16), tile)
        dst[at] = (dst[at].astype(F32) + src[at].astype(F32)).astype(BF)
        return carry

    lax.fori_loop(0, rows // tile, body, 0)


def plane_bits(size):
    return [1 << k for k in range(1, size.bit_length() - 1)]


def halvings(rows, bits):
    count = 0
    while count < len(bits) and rows % 32 == 0:
        rows //= 2
        count += 1
    return count


def tail_kernel(size, rows_list, *refs):
    groups = len(rows_list)
    bits = plane_bits(size)
    take = iter(refs)
    sources = [next(take) for _ in range(groups)]
    ig_ref, small_ref = next(take), next(take)
    outs = [next(take) for _ in range(groups)]
    ig_out, total_ref, pair_ref = next(take), next(take), next(take)
    keeps = [next(take) for _ in range(groups)]
    cores = [next(take) for _ in range(groups)]
    firsts = [next(take) for _ in range(groups)]
    seconds = [next(take) for _ in range(groups)]
    planes = [next(take) for _ in range(groups)]
    halves = [next(take) for _ in range(groups)]
    landed = next(take)
    send_sem, recv_sem, local_sem, ig_send, ig_recv, small_send, small_recv = take

    mine = lax.axis_index("tp")
    place = lax.axis_index("ep")
    core = lax.rem(place, 2)
    to_x = {"tp": mine ^ 1}
    to_y = {"tp": mine ^ 2}
    to_core = {"ep": place ^ 1}
    to_plane = [{"ep": place ^ bit} for bit in bits]

    barrier = pltpu.get_barrier_semaphore()
    for peer in [to_x, to_y, to_core] + to_plane:
        pl.semaphore_signal(barrier, inc=1, device_id=peer, device_id_type=pl.DeviceIdType.MESH)
    pl.semaphore_wait(barrier, 3 + len(bits))

    def remote(src, dst, sends, recvs, index, peer):
        return pltpu.make_async_remote_copy(
            src_ref=src,
            dst_ref=dst,
            send_sem=sends.at[index],
            recv_sem=recvs.at[index],
            device_id=peer,
            device_id_type=pl.DeviceIdType.MESH,
        )

    def group_steps(g):
        rows = rows_list[g]
        half, quarter = rows // 2, rows // 4
        source, keep, came, first, second = sources[g], keeps[g], cores[g], firsts[g], seconds[g]
        plane, out, whole_half = planes[g], outs[g], halves[g]
        own_half = pl.ds(pl.multiple_of(core * half, half), half)
        other_half = pl.ds(pl.multiple_of((1 - core) * half, half), half)
        number = iter(range(100))
        sent = []

        def send(src, dst, peer):
            copy = remote(src, dst, send_sem, recv_sem, (g, next(number)), peer)
            copy.start()
            sent.append(copy)
            return copy

        every = pl.ds(0, keep.shape[0])
        local = pltpu.make_async_copy(source.at[every, own_half], keep, local_sem.at[g])
        local.start()
        swap = send(source.at[every, other_half], came, to_core)
        yield
        local.wait()
        swap.wait_recv()
        for r in range(keep.shape[0]):
            add_rows(keep.at[r], came.at[r], half)
        low, high = pl.ds(0, quarter), pl.ds(quarter, quarter)
        waits = [
            send(keep.at[1, low], first.at[0], to_x),
            send(keep.at[3, low], first.at[1], to_x),
            send(keep.at[pl.ds(2, 2), high], first.at[pl.ds(2, 2)], to_y),
        ]
        yield
        for copy in waits:
            copy.wait_recv()
        add_rows(keep.at[2, low], first.at[1], quarter)
        add_rows(keep.at[1, high], first.at[3], quarter)
        waits = [
            send(keep.at[2, low], second.at[0], to_y),
            send(keep.at[1, high], second.at[1], to_x),
        ]
        add_rows(keep.at[0, low], first.at[0], quarter)
        add_rows(keep.at[0, high], first.at[2], quarter)
        yield
        for copy in waits:
            copy.wait_recv()
        add_rows(keep.at[0, low], second.at[0], quarter)
        add_rows(keep.at[0, high], second.at[1], quarter)
        start, length, done = 0, half, []
        offset = 0
        for k, bit in enumerate(bits):
            if k < halvings(half, bits):
                length //= 2
                side = lax.rem(place // bit, 2)
                mine_at = pl.ds(pl.multiple_of(start + side * length, 16), length)
                give_at = pl.ds(pl.multiple_of(start + (1 - side) * length, 16), length)
                land = plane.at[pl.ds(offset, length)]
                copy = send(keep.at[0, give_at], land, to_plane[k])
                done.append((mine_at, k))
                start = start + side * length
            else:
                mine_at = pl.ds(pl.multiple_of(start + 0 * place, 16), length)
                land = plane.at[pl.ds(offset, length)]
                copy = send(keep.at[0, mine_at], land, to_plane[k])
            yield
            copy.wait_recv()
            if k >= halvings(half, bits):
                copy.wait_send()
                sent.pop()
            add_rows(keep.at[0, mine_at], land, length)
            offset += length
        at = done[-1][0]
        whole_half[at] = keep[0, at, :]
        for at, k in done[::-1]:
            copy = send(whole_half.at[at], whole_half.at[at], to_plane[k])
            yield
            copy.wait_recv()
        copy = send(whole_half, out.at[own_half], to_core)
        local = pltpu.make_async_copy(whole_half, out.at[own_half], local_sem.at[groups + g])
        local.start()
        yield
        copy.wait_recv()
        local.wait()
        for copy in sent:
            copy.wait_send()

    def ig_steps():
        half = ig_ref.shape[0] // 32 * 16
        low, high = pl.ds(0, half), pl.ds(half, ig_ref.shape[0] - half)
        near = [
            remote(ig_ref, ig_out.at[mine], ig_send, ig_recv, 0, to_x),
            remote(ig_ref, ig_out.at[mine], ig_send, ig_recv, 1, to_y),
        ]
        local = pltpu.make_async_copy(ig_ref, ig_out.at[mine], local_sem.at[2 * groups])
        local.start()
        for copy in near:
            copy.start()
        yield
        for copy in near:
            copy.wait_recv()
        relay = [
            remote(ig_out.at[mine ^ 1, low], ig_out.at[mine ^ 1, low], ig_send, ig_recv, 2, to_y),
            remote(ig_out.at[mine ^ 2, high], ig_out.at[mine ^ 2, high], ig_send, ig_recv, 3, to_x),
        ]
        for copy in relay:
            copy.start()
        yield
        for copy in relay:
            copy.wait_recv()
        for copy in near + relay:
            copy.wait_send()
        local.wait()

    def small_steps():
        total_ref[...] = small_ref[...]
        peers = [to_x, to_y, to_core] + to_plane
        for k, peer in enumerate(peers):
            copy = remote(total_ref, landed.at[k], small_send, small_recv, k, peer)
            copy.start()
            yield
            copy.wait()
            total_ref[...] += landed[k]
            if k == 2:
                pair_ref[...] = total_ref[...]

    running = [group_steps(g) for g in range(groups)] + [small_steps(), ig_steps()]
    ended = set()

    def advance(which):
        if which not in ended:
            try:
                next(running[which])
            except StopIteration:
                ended.add(which)

    for which in TAIL_ORDER:
        advance(which)
    while len(ended) < len(running):
        for which in range(len(running)):
            advance(which)


def tail(grads, ig, small, size):
    shards, _, depth = grads[0].shape
    rows_list = [g.shape[1] for g in grads]
    groups = len(grads)
    bits = plane_bits(size)
    any_spec = pl.BlockSpec(memory_space=pl.ANY)
    shape = jax.ShapeDtypeStruct

    def plane_rows(rows):
        half, total = rows // 2, 0
        for k in range(len(bits)):
            if k < halvings(rows // 2, bits):
                half //= 2
            total += half
        return total

    copies = 4 + 2 + 2 * len(bits) + 1
    return pl.pallas_call(
        lambda *refs: tail_kernel(size, rows_list, *refs),
        in_specs=[any_spec] * (groups + 1) + [whole()],
        out_specs=[any_spec] * (groups + 1) + [whole(), whole()],
        out_shape=[shape((rows, depth), BF) for rows in rows_list]
        + [shape((shards,) + ig.shape, BF), shape(small.shape, F32), shape(small.shape, F32)],
        scratch_shapes=[pltpu.VMEM((shards, rows // 2, depth), BF) for rows in rows_list]
        + [pltpu.VMEM((shards, rows // 2, depth), BF) for rows in rows_list]
        + [pltpu.VMEM((4, rows // 4, depth), BF) for rows in rows_list]
        + [pltpu.VMEM((2, rows // 4, depth), BF) for rows in rows_list]
        + [pltpu.VMEM((plane_rows(rows), depth), BF) for rows in rows_list]
        + [pltpu.VMEM((rows // 2, depth), BF) for rows in rows_list]
        + [
            pltpu.VMEM((3 + len(bits),) + small.shape, F32),
            pltpu.SemaphoreType.DMA((groups, copies)),
            pltpu.SemaphoreType.DMA((groups, copies)),
            pltpu.SemaphoreType.DMA((2 * groups + 1,)),
            pltpu.SemaphoreType.DMA((4,)),
            pltpu.SemaphoreType.DMA((4,)),
            pltpu.SemaphoreType.DMA((3 + len(bits),)),
            pltpu.SemaphoreType.DMA((3 + len(bits),)),
        ],
        compiler_params=pltpu.CompilerParams(
            vmem_limit_bytes=VMEM_LIMIT, collective_id=1, has_side_effects=True
        ),
        cost_estimate=pl.CostEstimate(flops=30_000_000, bytes_accessed=60_000_000, transcendentals=0),
        name="tail",
    )(*grads, ig, small)


def hop(value, axis, bit):
    size = lax.axis_size(axis)
    return lax.ppermute(value, axis, [(i, i ^ bit) for i in range(size)])


def after(value, *deps):
    return lax.optimization_barrier((value, deps))[0]


def near(value):
    return hop(value, "tp", 1), hop(value, "tp", 2)


def far(from_x, from_y):
    half = from_x.shape[0] // 2
    low = hop(from_x[:half], "tp", 2)
    high = hop(from_y[half:], "tp", 1)
    return jnp.concatenate([low, high])


def gather_tp_small(value):
    return jnp.stack([value, hop(value, "tp", 1), hop(value, "tp", 2), hop(value, "tp", 3)])


def take_half(value, which, axis=0):
    half = value.shape[axis] // 2
    return lax.dynamic_slice_in_dim(value, which * half, half, axis=axis)


def join_halves(value, other, which, axis=0):
    half = value.shape[axis]
    three = jnp.concatenate([value, other, value], axis=axis)
    return lax.dynamic_slice_in_dim(three, which * half, 2 * half, axis=axis)


def plus(a, b):
    return (a.astype(F32) + b.astype(F32)).astype(BF)


def core_sum(value):
    core = lax.axis_index("ep") % 2
    return plus(take_half(value, core, 1), hop(take_half(value, 1 - core, 1), "ep", 1))


def swap_ep(value):
    return lax.all_to_all(value, "ep", split_axis=0, concat_axis=0, tiled=True)


def route_kernel(order_ref, index_ref, hot_ref, out_ref, rank_ref):
    rows = order_ref.shape[1]
    tile = rows // 7
    half = hot_ref.shape[1] // 2
    for i in range(7):
        ids = lax.broadcasted_iota(jnp.int32, (tile, 1), 0) + tile * i
        match = jnp.where(order_ref[...] == ids, 1.0, 0.0).astype(BF)
        rank_ref[tile * i : tile * (i + 1), :] = dot(match, index_ref[...], NN)
    parts = rank_ref[...]
    rank = parts[:, 0:1] * 64.0 + parts[:, 1:2]
    rank_row = jnp.transpose(jnp.broadcast_to(rank, parts.shape))[0:1, :]
    hot = hot_ref[...]
    total = jnp.sum(hot.astype(F32), axis=0, keepdims=True)
    lanes = lax.broadcasted_iota(jnp.int32, (1, 2 * half), 1)
    firsts = jnp.where(lanes < half, total, 0.0)
    firsts = jnp.concatenate([jnp.zeros((1, half), F32), firsts[:, :half]], axis=1)
    for i in range(7):
        at = slice(tile * i, tile * (i + 1))
        earlier = jnp.where(rank_row < rank[at], 1.0, 0.0).astype(BF)
        count = dot(earlier, hot, NN) + firsts
        picked = count * hot[at].astype(F32)
        first = jnp.sum(jnp.where(lanes < half, picked, 0.0), axis=1, keepdims=True)
        second = jnp.sum(jnp.where(lanes < half, 0.0, picked), axis=1, keepdims=True)
        out_ref[at, :] = jnp.where(lanes == 0, first, second)


def route(picks, order):
    rows = picks.shape[0]
    half = 64
    ids = jnp.arange(half, dtype=jnp.int32)[None, :]
    hot = jnp.concatenate([picks[:, 0:1] == ids, picks[:, 1:2] == ids], axis=1).astype(BF)
    line = jnp.arange(rows, dtype=jnp.int32)[:, None]
    column = jnp.arange(2 * half, dtype=jnp.int32)[None, :]
    index = jnp.where(column == 0, line // 64, jnp.where(column == 1, line % 64, 0)).astype(BF)
    out = pl.pallas_call(
        route_kernel,
        in_specs=[whole(), whole(), whole()],
        out_specs=whole(),
        out_shape=jax.ShapeDtypeStruct((rows, 2 * half), F32),
        scratch_shapes=[pltpu.VMEM((rows, 2 * half), F32)],
        compiler_params=pltpu.CompilerParams(vmem_limit_bytes=VMEM_LIMIT),
        cost_estimate=pl.CostEstimate(
            flops=4 * rows * rows * 128, bytes_accessed=4_000_000, transcendentals=0
        ),
        name="route",
    )(order.reshape(1, rows), index, hot)
    return out[:, :2].astype(jnp.int32)


def body(
    tokens,
    cotangent,
    picks,
    priority,
    router_noise,
    dense_norm_gain,
    dense_norm_bias,
    dense_attend_in,
    dense_attend_bias,
    dense_attend_out,
    dense_attend_out_bias,
    feed_norm_gain,
    feed_norm_bias,
    feed_in,
    feed_in_bias,
    feed_out,
    feed_out_bias,
    sparse_norm_gain,
    sparse_norm_bias,
    sparse_attend_in,
    sparse_attend_bias,
    sparse_attend_out,
    sparse_attend_out_bias,
    route_norm_gain,
    route_norm_bias,
    router,
    expert_in,
    expert_in_bias,
    expert_out,
    expert_out_bias,
):
    shards = lax.axis_size("tp")
    experts = lax.axis_size("ep")
    mine = lax.axis_index("tp")
    rows_dev, depth = tokens.shape
    own = rows_dev // shards
    images = own // LEN
    own_pad = images * PAD
    capacity = rows_dev // experts
    part = -(-capacity // (8 * shards)) * 8
    width = dense_attend_bias.shape[1]
    hidden = feed_in_bias.shape[0]

    def pad_images(value):
        blocks = value.reshape(-1, LEN, value.shape[-1])
        return jnp.pad(blocks, ((0, 0), (0, PAD - LEN), (0, 0))).reshape(-1, value.shape[-1])

    def drop_pad(value):
        return value.reshape(images, PAD, depth)[:, :LEN].reshape(own, depth)

    def own_rows(value):
        return lax.dynamic_slice_in_dim(value, mine * own, own, axis=0)

    def by_index(value):
        return jnp.stack(
            [
                lax.dynamic_index_in_dim(value, mine ^ r, axis=0, keepdims=False)
                for r in range(shards)
            ]
        )

    def row(value):
        return value.reshape(1, -1)

    def attend_pack(proj_in, proj_out):
        return jnp.concatenate([proj_in.transpose(1, 2, 0).reshape(3 * width, depth), proj_out])

    pair_side = lax.axis_index("ep") % 2
    chip_side = mine % 2
    same = pair_side == chip_side
    keep_exp = jnp.where(pair_side == 0, expert_in[0], expert_out[0])
    give_exp = jnp.where(pair_side == 0, expert_out[0], expert_in[0])
    vectors = jnp.stack(
        [
            dense_norm_gain,
            dense_norm_bias,
            dense_attend_out_bias,
            feed_norm_gain,
            feed_norm_bias,
            feed_out_bias,
            sparse_norm_gain,
            sparse_norm_bias,
            sparse_attend_out_bias,
            route_norm_gain,
            route_norm_bias,
        ]
    )
    vectors = jnp.pad(vectors, ((0, 5), (0, 0)))

    def bias_line(value):
        gap = jnp.zeros((width,), F32)
        return jnp.concatenate([value[0], gap, value[1], jnp.zeros((depth - 3 * width,), F32)])

    own_biases = jnp.stack(
        [
            bias_line(dense_attend_bias),
            bias_line(sparse_attend_bias),
            feed_in_bias,
            expert_in_bias[0],
            expert_out_bias[0],
        ]
    )
    own_biases = jnp.pad(own_biases, ((0, 3), (0, 0)))
    position = route(picks, priority[0])
    targets = jnp.where(position < capacity, picks * (part * shards) + position, -1).T
    slots = jnp.arange(experts * part, dtype=jnp.int32)

    def slots_of(index):
        block, inside = slots // part, slots % part
        expert = 2 * (block // 2) + index % 2
        quarter = 2 * (index // 2) + block % 2
        return expert * (part * shards) + quarter * part + inside

    slot_ids = slots_of(mine)
    pad_targets = jnp.pad(
        targets.reshape(2, -1, LEN), ((0, 0), (0, 0), (0, PAD - LEN)), constant_values=-1
    ).reshape(2, -1)
    near_targets = jnp.concatenate(
        [
            lax.dynamic_slice_in_dim(pad_targets, (mine ^ r) * own_pad, own_pad, axis=1)
            for r in range(shards)
        ],
        axis=1,
    )
    noise_pad = pad_images(router_noise)
    all_slots = jnp.concatenate([slots_of(mine ^ r) for r in range(shards)])
    own_targets = near_targets[:, :own_pad].T
    back_hot = (own_targets[:, 0:1] == all_slots[None, :]) | (
        own_targets[:, 1:2] == all_slots[None, :]
    )
    back_hot_bf = back_hot.astype(BF)

    swapped = hop(give_exp, "ep", 1)
    home_exp = jnp.where(same, keep_exp, swapped)
    away_exp = jnp.where(same, swapped, keep_exp)
    level_zero = after(pad_images(own_rows(tokens)), home_exp, away_exp)
    (level_one, level_two, level_three), kept_one, kept_feed, kept_two, gathered, normed, biases = (
        dense_forward(
            level_zero,
            vectors,
            own_biases,
            attend_pack(dense_attend_in, dense_attend_out),
            jnp.concatenate([feed_in, feed_out]),
            attend_pack(sparse_attend_in, sparse_attend_out),
        )
    )
    w_one, w_feed, w_two = gathered
    level_zero = level_zero.astype(F32)
    exp_small = biases[:, 3:5]
    exp_small = jnp.where(same, exp_small, hop(exp_small, "ep", 1))
    b_exp = exp_small[:, 0:1]
    b_exp_out = exp_small[0, 1:2]

    home_exp = after(home_exp, normed)
    away_exp = after(away_exp, normed)
    exp_x = hop(away_exp, "tp", 1)
    exp_far = hop(away_exp, "tp", 3)
    exp_y = hop(home_exp, "tp", 2)
    other_home = hop(home_exp, "ep", 1)

    all_normed = normed.reshape(shards * own_pad, depth)
    route_normed = normed[0]
    noise = jnp.concatenate(
        [
            lax.dynamic_slice_in_dim(noise_pad, (mine ^ r) * own_pad, own_pad, axis=0)
            for r in range(shards)
        ]
    )
    logits = dot(all_normed, router, NN) + noise
    gates = jax.nn.softmax(logits, axis=-1)
    own_hot = (slot_ids[:, None] == near_targets[0][None, :]) | (
        slot_ids[:, None] == near_targets[1][None, :]
    )
    side_gates = lax.dynamic_index_in_dim(
        gates.T.reshape(experts // 2, 2, -1), chip_side, axis=1, keepdims=False
    )
    hot_gates = own_hot.reshape(experts // 2, 2 * part, -1).astype(F32) * side_gates[:, None, :]
    slot_gate = jnp.sum(hot_gates, axis=2).reshape(-1, 1)

    def two_parts(value):
        high = lax.reduce_precision(value, 8, 7)
        rest = jnp.zeros((value.shape[0], 126), BF)
        return jnp.concatenate([high.astype(BF), (value - high).astype(BF), rest], axis=1)

    def swap_rows(value):
        wide = value.shape[-1]
        return swap_ep(value.reshape(experts, part, wide)).reshape(experts * part, wide)

    rows = dot(own_hot.astype(BF), all_normed, NN).astype(BF)
    arrived = swap_rows(jnp.concatenate([rows, two_parts(slot_gate)], axis=1))
    cot_hot = (slot_ids[:, None] == targets[0][None, :]) | (slot_ids[:, None] == targets[1][None, :])
    cot_sent = dot(after(cot_hot.astype(BF), rows), cotangent, NN).astype(BF)
    cot_rows = swap_rows(cot_sent)
    exp_mine = jnp.stack([home_exp, exp_x, exp_y, exp_far])
    exp_other = jnp.stack(
        [other_home, hop(exp_x, "ep", 1), hop(exp_y, "ep", 1), hop(exp_far, "ep", 1)]
    )
    inputs = arrived[:, :depth]
    gate_in = arrived[:, depth : depth + 2].astype(F32)
    gate_in = gate_in[:, 0:1] + gate_in[:, 1:2]
    outputs, exp_hidden, exp_slope = expert_forward(inputs, exp_mine, exp_other, b_exp, b_exp_out)
    weighted, grad_outputs, grad_inputs, slot_dot, exp_du, small_exp = (
        expert_input(outputs, cot_rows, gate_in, exp_mine, exp_other, exp_slope)
    )
    returned_sent = jnp.concatenate([grad_inputs, two_parts(slot_dot)], axis=1)
    returned = swap_rows(returned_sent)
    g_exp = expert_weight(after(inputs, returned_sent), grad_outputs, exp_hidden, exp_du)
    part_exp = core_sum(g_exp)
    exp_from_y = hop(part_exp[3], "tp", 2)
    returned = after(returned, g_exp)
    near_grad = near(returned)
    grad_slots = jnp.concatenate([returned, *near_grad, far(*near_grad)])
    dot_slots = grad_slots[:, depth : depth + 2].astype(F32)
    dot_slots = dot_slots[:, 0] + dot_slots[:, 1]
    grad_slots = grad_slots[:, :depth]
    weighted = swap_rows(after(weighted, returned))

    grad_stream = pad_images(own_rows(cotangent)).astype(F32)
    own_gates = gates[:own_pad]
    hot_dots = jnp.where(back_hot, dot_slots[None, :], 0.0).reshape(
        own_pad, 2, 2, experts // 2, 2 * part
    )
    by_side = jnp.sum(hot_dots, axis=(1, 4))
    by_side = jnp.where(chip_side == 0, by_side, by_side[:, ::-1])
    grad_gates = by_side.transpose(0, 2, 1).reshape(own_pad, experts)
    grad_logits = own_gates * (grad_gates - jnp.sum(own_gates * grad_gates, axis=1, keepdims=True))
    grad_logits = grad_logits.astype(BF)
    g_router = dot(grad_logits, route_normed, TN)
    grad_normed = dot(grad_logits, router, NT) + dot(back_hot_bf, grad_slots, NN)
    hat, scale = norm_parts(level_three)
    g_route_gain = jnp.sum(grad_normed * hat, axis=0)
    g_route_bias = jnp.sum(grad_normed, axis=0)
    grad_stream = grad_stream + norm_back(hat, scale, route_norm_gain, grad_normed)

    near_weighted = near(after(weighted, grad_stream))
    grad_stream, g_two, small_two = attend_backward(
        grad_stream, level_two, row(sparse_norm_gain), row(sparse_norm_bias), w_two, kept_two
    )
    near_weighted = after(near_weighted, g_two)
    far_weighted = far(*near_weighted)
    exp_from_y = after(exp_from_y, g_two)
    exp_from_y2 = hop(after(part_exp[2], g_two), "tp", 2)
    exp_give = plus(part_exp[1], exp_from_y)
    exp_away = hop(exp_give, "tp", 1)
    grad_stream, g_feed, small_feed = feed_backward(
        grad_stream, level_one, row(feed_norm_gain), row(feed_norm_bias), w_feed, kept_feed
    )
    far_weighted, exp_from_y2, exp_away = lax.optimization_barrier(
        ((far_weighted, exp_from_y2, exp_away), g_feed)
    )[0]
    exp_keep = plus(part_exp[0], exp_from_y2)
    keep_sum = jnp.where(same, exp_keep, exp_away)
    other_sum = hop(jnp.where(same, exp_away, exp_keep), "ep", 1)
    weighted_slots = jnp.concatenate([weighted, *near_weighted, far_weighted])
    level_four = level_three + dot(back_hot_bf, weighted_slots, NN)
    own_final = drop_pad(level_four.astype(BF))
    near_final = near(own_final)
    grad_stream = after(grad_stream, own_final)
    grad_stream, g_one, small_one = attend_backward(
        grad_stream, level_zero, row(dense_norm_gain), row(dense_norm_bias), w_one, kept_one
    )
    near_final = after(near_final, g_one)
    far_final = far(*near_final)

    blank = jnp.zeros_like(small_exp)
    first = chip_side == 0
    small = jnp.concatenate(
        [
            small_one,
            small_feed,
            small_two,
            jnp.where(first, small_exp, blank),
            jnp.where(first, blank, small_exp),
            g_router,
            jnp.pad(jnp.stack([g_route_gain, g_route_bias]), ((0, 6), (0, 0))),
        ]
    )
    t_two, t_feed, t_one, ig_all, total, pair_total = tail(
        [g_two, g_feed, g_one], drop_pad(grad_stream.astype(BF)), small, experts
    )
    input_grad = ig_all.reshape(rows_dev, depth).astype(F32)
    far_final, other_sum = after((far_final, other_sum), t_one)

    def absolute(blocks, kind):
        out = jnp.zeros((rows_dev, depth), kind)
        for r in range(shards):
            out = lax.dynamic_update_slice_in_dim(
                out, blocks[r].astype(kind), (mine ^ r) * own, axis=0
            )
        return out

    final = absolute([own_final, *near_final, far_final], BF)

    def attend_split(value):
        value = value.astype(F32)
        return (
            value[: 3 * width].reshape(3, width, depth).transpose(2, 0, 1),
            value[3 * width :],
        )

    t_exp_in = jnp.where(pair_side == 0, keep_sum, other_sum).astype(F32)
    t_exp_out = jnp.where(pair_side == 0, other_sum, keep_sum).astype(F32)
    t_in_two, t_out_two = attend_split(t_two)
    t_in_one, t_out_one = attend_split(t_one)
    t_feed = t_feed.astype(F32)

    def own_line(value, start):
        return lax.dynamic_slice_in_dim(value, start + mine, 1, axis=0)[0]

    def two_biases(start):
        line = own_line(total, start)
        return jnp.stack([line[:width], line[2 * width : 3 * width]])

    s_one, s_feed, s_two = total[0:8], total[8:16], total[16:24]
    s_exp = lax.dynamic_slice_in_dim(pair_total, 24 + 8 * pair_side, 8, axis=0)
    s_router = total[40 : 40 + experts].T
    s_route = total[40 + experts :]
    return (
        final,
        input_grad,
        s_one[0],
        s_one[1],
        t_in_one,
        two_biases(3),
        t_out_one,
        s_one[2],
        s_feed[0],
        s_feed[1],
        t_feed[:depth],
        own_line(total, 11),
        t_feed[depth:],
        s_feed[2],
        s_two[0],
        s_two[1],
        t_in_two,
        two_biases(19),
        t_out_two,
        s_two[2],
        s_route[0],
        s_route[1],
        s_router,
        t_exp_in[None],
        own_line(s_exp, 0)[None],
        t_exp_out[None],
        s_exp[4][None],
    )


def solution(mesh):
    in_specs = (
        P("ep", None),
        P("ep", None),
        P("ep", None),
        P("ep", None),
        P("ep", None),
        P(),
        P(),
        P(None, None, "tp"),
        P(None, "tp"),
        P("tp", None),
        P(),
        P(),
        P(),
        P(None, "tp"),
        P("tp"),
        P("tp", None),
        P(),
        P(),
        P(),
        P(None, None, "tp"),
        P(None, "tp"),
        P("tp", None),
        P(),
        P(),
        P(),
        P(),
        P("ep", None, "tp"),
        P("ep", "tp"),
        P("ep", "tp", None),
        P("ep", None),
    )
    out_specs = (
        P("ep", None),
        P("ep", None),
        P(),
        P(),
        P(None, None, "tp"),
        P(None, "tp"),
        P("tp", None),
        P(),
        P(),
        P(),
        P(None, "tp"),
        P("tp"),
        P("tp", None),
        P(),
        P(),
        P(),
        P(None, None, "tp"),
        P(None, "tp"),
        P("tp", None),
        P(),
        P(),
        P(),
        P(),
        P("ep", None, "tp"),
        P("ep", "tp"),
        P("ep", "tp", None),
        P("ep", None),
    )
    return jax.shard_map(body, mesh=mesh, in_specs=in_specs, out_specs=out_specs, check_vma=False)
```

time: 2350 us -> 794 us (0.34)
  waiting for transfers between devices: 1290 us -> 107 us
  Pallas kernels: 0 us -> 471 us
  local copies, waits for them, and re-layouts: 364 us -> 59.7 us
  matrix products: 286 us -> 36.5 us
  other arithmetic: 225 us -> 71.7 us
  blocking collectives: 145 us -> 0 us
  starting transfers between devices: 15.3 us -> 40.1 us
    psum x8 -> x0, waiting for transfers between devices: 1120 us -> none  [the longest x3 515 us: add_branch(): return stream + lax.psum(partial_value, 'tp') + bias_row]
    pallas_call x0 -> x9, Pallas kernels: none -> 471 us  [the longest x1 161 us: tail(): pl.pallas_call(lambda *refs: tail_kernel(size, rows_list, *refs), in_spec...]
    dot_general x35 -> x7, matrix products: 267 us -> 36.5 us  [dot(): return lax.dot_general(a, b, (dims, ((), ())), preferred_element_type=F32)]
    gather x14 -> x0, local copies, waits for them, and re-layouts: 158 us -> none  [the longest x5 37.6 us: mixture_forward(): picked_gate = jnp.take_along_axis(gate_probs, picks, axis=1)]
    reduce_sum x27 -> x6, other arithmetic: 154 us -> 4.48 us  [the longest x1 2.01 us: body(): by_side = jnp.sum(hot_dots, axis=(1, 4))]
    all_to_all x3 -> x4, waiting for transfers between devices: 165 us -> 33.9 us  [swap_ep(): return lax.all_to_all(value, 'ep', split_axis=0, concat_axis=0, tiled=True)]
    all_to_all x1 -> x0, blocking collectives: 112 us -> none  [from_experts(): lax.all_to_all(summed_rows.reshape(sources, -1, summed_rows.shape[1]), 'e...]
    ppermute x0 -> x26, waiting for transfers between devices: none -> 73.2 us  [hop(): return lax.ppermute(value, axis, [(i, i ^ bit) for i in range(size)])]
  transfers between devices with their start and end apart: 11 -> 30, of which waited for: 11 -> 9; matrix products, arithmetic and copies ran while one was open for 13% -> 17% of each run, Pallas kernels for 0% -> 37%
where the time goes in v1:
time: 794 us; the launch traced here: 788 us
  Pallas kernels  471 us (59%)
  waiting for transfers between devices  107 us (13%)
  other arithmetic  71.7 us (9%)
  local copies, waits for them, and re-layouts  59.7 us (8%)
  starting transfers between devices  40.1 us (5%)
  matrix products  36.5 us (5%)
    pallas_call x1, Pallas kernels, tail(): pl.pallas_call(lambda *refs: tail_kernel(size, rows_list, *refs), in_spec...  161 us
    pallas_call x1, Pallas kernels, dense_forward(): pl.pallas_call(forward_kernel, grid=(3 * images,), in_specs=[whole(), who...  144 us
    ppermute x26, waiting for transfers between devices, hop(): return lax.ppermute(value, axis, [(i, i ^ bit) for i in range(size)])  73.2 us
    pallas_call x2, Pallas kernels, attend_backward(): pl.pallas_call(attend_backward_kernel, grid=(images,), in_specs=[row_bloc...  71.3 us
    dot_general x7, matrix products, dot(): return lax.dot_general(a, b, (dims, ((), ())), preferred_element_type=F32)  36.5 us
    all_to_all x4, waiting for transfers between devices, swap_ep(): return lax.all_to_all(value, 'ep', split_axis=0, concat_axis=0, tiled=True)  33.9 us
    pallas_call x1, Pallas kernels, feed_backward(): pl.pallas_call(feed_backward_kernel, grid=(shards,), in_specs=[whole(), w...  28.7 us
    ppermute x26, starting transfers between devices, hop(): return lax.ppermute(value, axis, [(i, i ^ bit) for i in range(size)])  21.2 us
  transfers between devices with their start and end apart: 30, of which 9 were waited for; matrix products, arithmetic and copies ran while one was open for 17% of the time, Pallas kernels for 37%

profile of v1, /device:TPU:0, one launch (start us, length us, event | category | flops | bytes accessed | tf_op | source)
XLA Modules:
  0.0 788.5 jit_solution(4222466799870606891)
XLA Ops:
  15.6 13.8 %route.1 = f32[3136,128]{1,0:T(8,128)} custom-call(s32[1,3136]{1,0:T(1,128)} %order_ref.1, bf16[3136,128]{1,0:T(8,128)(2,1)} %select_convert_fusion.index_ref, bf16[3136,128]{1,0:T(8,128)(2,1)} %add_convert_fusion.2.hot_ref), custom_call_target="tpu_custom_call" | custom-call | flops 5035261952 | bytes 4000000 | tf_op jit(solution)/shard_map/route/pallas_call | solution.py:1146
  43.5 144.4 %dense_forward.1 = (f32[832,768]{1,0:T(8,128)}, f32[832,768]{1,0:T(8,128)}, f32[832,768]{1,0:T(8,128)}, bf16[4,4,576,208]{3,2,1,0:T(8,128)(2,1)}, f32[4,4,3,208]...) custom-call(bf16[832,768]{1,0:T(8,128)(2,1)} %bitcast.110, ...), custom_call_target="tpu_custom_call" | custom-call | flops 60000002048 | bytes 60000000 | tf_op jit(solution)/shard_map/dense_forward/pallas_call | solution.py:760
  191.7 3.9 fusion.87
  195.9 7.3 fusion.31
  206.9 4.9 all-to-all-start
  214.0 3.3 collective-permute-done.1
  217.4 25.6 %collective-permute-done.2 = bf16[768,768]{1,0:T(8,128)(2,1)} collective-permute-done((bf16[768,768]{1,0:T(8,128)(2,1)S(1)}, bf16[768,768]{1,0:T(8,128)(2,1)}, u32[]{:S(2)}, u32[]{:S(2)}) %collective-permute-start.2) | collective-permute-done | bytes 1179680 | tf_op jit(solution)/shard_map/ppermute | solution.py:1066
  243.5 7.9 %convolution_convert_fusion = bf16[832,768]{1,0:T(8,128)(2,1)} fusion(bf16[832,3136]{1,0:T(8,128)(2,1)S(1)} %or_convert_fusion, bf16[3136,768]{1,0:T(8,128)(2,1)} %param.31), kind=kOutput, calls=%fused_computation.56 | convolution fusion | flops 4008296448 | bytes 11313152 | tf_op jit(solution)/shard_map/dot_general | solution.py:22
  252.6 3.9 pad_maximum_fusion.mine_ref
  256.5 5.3 all-to-all-start.1
  261.9 4.0 pad_maximum_fusion.1.other_ref
  268.0 21.1 %expert_forward.1 = (bf16[832,768]{1,0:T(8,128)(2,1)}, bf16[4,832,768]{2,1,0:T(8,128)(2,1)}, bf16[4,832,768]{2,1,0:T(8,128)(2,1)}) custom-call(bf16[832,768]{1,0:T(8,128)(2,1)} %slice.268.x_ref, bf16[4,768,768]{2,1,0:T(8,128)(2,1)} %pad_maximum_fusion.mine_ref, bf16[4,768,768]{2,1,0:T(8,128)(2,1)} %pad_maximum_fusion.1.other_ref, ...), custom_call_target="tpu_custom_call" | custom-call | flops 15703474176 | bytes 25000000 | tf_op jit(solution)/shard_map/expert_forward/pallas_call | solution.py:305
  289.1 4.3 all-to-all-done.1
  293.4 16.5 %expert_input.1 = (bf16[832,768]{1,0:T(8,128)(2,1)}, bf16[832,768]{1,0:T(8,128)(2,1)}, bf16[832,768]{1,0:T(8,128)(2,1)}, f32[832,1]{1,0:T(8,128)}, bf16[4,832,768]{2,1,0:T(8,128)(2,1)}, /*index=5*/f32[8,768]{1,0:T(8,128)}) custom-call(bf16[832,768]{1,0:T(8,128)(2,1)} %get-tuple-element.93.y_ref, bf16[832,768]{1,0:T(8,128)(2,1)} %bitcast.27.cot_ref, ...), custom_call_target="tpu_custom_call" | custom-call | flops 15703474176 | bytes 25000000 | tf_op jit(solution)/shard_map/expert_input/pallas_call | solution.py:375
  313.8 14.5 %expert_weight.1 = bf16[4,1536,768]{2,1,0:T(8,128)(2,1)} custom-call(bf16[832,768]{1,0:T(8,128)(2,1)} %slice.268.x_ref, bf16[832,768]{1,0:T(8,128)(2,1)} %get-tuple-element.100.dy_ref, bf16[4,832,768]{2,1,0:T(8,128)(2,1)} %get-tuple-element.101.hid_ref, bf16[4,832,768]{2,1,0:T(8,128)(2,1)} %get-tuple-element.102.du_ref), custom_call_target="tpu_custom_call" | custom-call | flops 15703474176 | bytes 25000000 | tf_op jit(solution)/shard_map/expert_weight/pallas_call | solution.py:417
  328.3 4.8 constant_dynamic-slice_fusion.5
  333.1 4.5 all-to-all-start.2
  344.0 29.6 %all-to-all-done.2 = bf16[8,104,896]{2,1,0:T(8,128)(2,1)} async-done(((bf16[8,104,896]{2,1,0:T(8,128)(2,1)}), bf16[8,104,896]{2,1,0:T(8,128)(2,1)}, u32[]{:S(2)}, u32[]{:S(2)}) %all-to-all-start.2) | async-done | bytes 1490976 | tf_op jit(solution)/shard_map/all_to_all | solution.py:1109
  376.2 4.3 all-to-all-start.3
  382.0 26.1 %collective-permute-done.9 = bf16[832,896]{1,0:T(8,128)(2,1)} collective-permute-done((bf16[832,896]{1,0:T(8,128)(2,1)}, bf16[832,896]{1,0:T(8,128)(2,1)}, u32[]{:S(2)}, u32[]{:S(2)}) %collective-permute-start.9) | collective-permute-done | bytes 1490976 | tf_op jit(solution)/shard_map/ppermute | solution.py:1066
  415.9 4.9 add_convert_fusion
  422.8 6.2 collective-permute-done.11
  435.8 8.2 %multiply_reduce_fusion = (f32[768]{0:T(1024)S(1)}, f32[832]{0:T(1024)S(1)}, f32[832]{0:T(1024)S(1)}, f32[768]{0:T(1024)S(1)}, f32[832,768]{1,0:T(8,128)S(1)}) fusion(f32[832,768]{1,0:T(8,128)S(1)} %copy-done.3, f32[832]{0:T(1024)S(1)} %add_rsqrt_fusion, f32[832]{0:T(1024)S(1)} %broadcast_multiply_fusion.3, f32[768]{0:T(1024)S(1)} %copy-done.26, ...), kind=kOutput, calls=%fused_computation.33 | convolution fusion | flops 4267717632 | bytes 12822016 | tf_op jit(solution)/shard_map/dot_general | solution.py:22
  448.2 35.7 %attend_backward.2 = (f32[832,768]{1,0:T(8,128)}, bf16[4,768,768]{2,1,0:T(8,128)(2,1)}, f32[8,768]{1,0:T(8,128)}) custom-call(f32[832,768]{1,0:T(8,128)} %convert_add_fusion.g_ref, f32[832,768]{1,0:T(8,128)} %get-tuple-element.106.h_ref, f32[1,768]{1,0:T(1,128)} %copy-done.31, f32[1,768]{1,0:T(1,128)} %copy-done.32, ...), custom_call_target="tpu_custom_call" | custom-call | flops 26744979456 | bytes 30000000 | tf_op jit(solution)/shard_map/attend_backward/pallas_call | solution.py:153
  494.9 28.7 %feed_backward.1 = (f32[832,768]{1,0:T(8,128)}, bf16[4,1536,768]{2,1,0:T(8,128)(2,1)}, f32[8,768]{1,0:T(8,128)}) custom-call(f32[832,768]{1,0:T(8,128)} %get-tuple-element.116.g_ref, f32[832,768]{1,0:T(8,128)} %get-tuple-element.117.h_ref, f32[1,768]{1,0:T(1,128)} %copy-done.29, f32[1,768]{1,0:T(1,128)} %copy-done.30, ...), custom_call_target="tpu_custom_call" | custom-call | flops 31406948352 | bytes 35000000 | tf_op jit(solution)/shard_map/feed_backward/pallas_call | solution.py:236
  527.3 7.0 add_convert_fusion.1
  536.9 35.5 %attend_backward.3 = (f32[832,768]{1,0:T(8,128)}, bf16[4,768,768]{2,1,0:T(8,128)(2,1)}, f32[8,768]{1,0:T(8,128)}) custom-call(f32[832,768]{1,0:T(8,128)} %get-tuple-element.124.g_ref, f32[832,768]{1,0:T(8,128)} %convert_element_type.159.h_ref, f32[1,768]{1,0:T(1,128)} %copy-done.27, f32[1,768]{1,0:T(1,128)} %copy-done.28, ...), custom_call_target="tpu_custom_call" | custom-call | flops 26744979456 | bytes 30000000 | tf_op jit(solution)/shard_map/attend_backward/pallas_call | solution.py:153
  578.0 3.4 broadcast_select_fusion.2
  582.1 160.8 %tail.1 = (bf16[768,768]{1,0:T(8,128)(2,1)}, bf16[1536,768]{1,0:T(8,128)(2,1)}, bf16[768,768]{1,0:T(8,128)(2,1)}, bf16[4,784,768]{2,1,0:T(8,128)(2,1)}, f32[56,768]{1,0:T(8,128)}, /*index=5*/f32[56,768]{1,0:T(8,128)}) custom-call(bf16[4,768,768]{2,1,0:T(8,128)(2,1)} %get-tuple-element.111.refs_0_, bf16[4,1536,768]{2,1,0:T(8,128)(2,1)} %get-tuple-element.121.refs_1_, ...), custom_call_target="tpu_custom_call" | custom-call | flops 30000000 | bytes 60000000 | tf_op jit(solution)/shard_map/tail/pallas_call | solution.py:1034
  742.9 7.0 bitcast_convert_fusion
  772.0 6.8 collective-permute-done.23
  781.5 4.4 bitcast_convert_fusion.1
  (293 shorter events, 127.4 us)
Async XLA Ops:
  0.7 191.0 %copy-start = (bf16[768,8]{0,1:T(8,128)(2,1)S(1)}, bf16[768,8]{0,1:T(8,128)(2,1)}, u32[]{:S(2)}) copy-start(bf16[768,8]{0,1:T(8,128)(2,1)} %param.55) | copy-start | bytes 36868
  3.1 37.7 %collective-permute-start = (bf16[768,768]{1,0:T(8,128)(2,1)}, bf16[768,768]{1,0:T(8,128)(2,1)}, u32[]{:S(2)}, u32[]{:S(2)}) collective-permute-start(bf16[768,768]{1,0:T(8,128)(2,1)} %select_bitcast_fusion.1), channel_id=1, source_target_pairs={{0,1},{1,0},{2,3},{3,2},{4,5},{5,4},{6,7},{7,6},{8,9},{9,8},{10,11... | collective-permute-start | bytes 3538952 | tf_op jit(solution)/shard_map/ppermute | solution.py:1066
  187.9 29.5 %collective-permute-start.1 = (bf16[768,768]{1,0:T(8,128)(2,1)}, bf16[768,768]{1,0:T(8,128)(2,1)}, u32[]{:S(2)}, u32[]{:S(2)}) collective-permute-start(bf16[768,768]{1,0:T(8,128)(2,1)} %get-tuple-element.91), channel_id=1, source_target_pairs={{0,8},{8,0},{16,24},{24,16},{1,9},{9,1},{17,25},{25,17},{2,10},{10... | collective-permute-start | bytes 3538952 | tf_op jit(solution)/shard_map/ppermute | solution.py:1066
  190.1 52.8 %collective-permute-start.3 = (bf16[768,768]{1,0:T(8,128)(2,1)}, bf16[768,768]{1,0:T(8,128)(2,1)}, u32[]{:S(2)}, u32[]{:S(2)}) collective-permute-start(bf16[768,768]{1,0:T(8,128)(2,1)} %get-tuple-element.91), channel_id=1, source_target_pairs={{0,24},{8,16},{16,8},{24,0},{1,25},{9,17},{17,9},{25,1},{2,26},{10... | collective-permute-start | bytes 3538952 | tf_op jit(solution)/shard_map/ppermute | solution.py:1066
  191.6 51.3 %collective-permute-start.2 = (bf16[768,768]{1,0:T(8,128)(2,1)S(1)}, bf16[768,768]{1,0:T(8,128)(2,1)}, u32[]{:S(2)}, u32[]{:S(2)}) collective-permute-start(bf16[768,768]{1,0:T(8,128)(2,1)S(1)} %get-tuple-element.90), channel_id=1, source_target_pairs={{0,16},{8,24},{16,0},{24,8},{1,17},{9,25},{17,1},{25,9},{2,18},{10... | collective-permute-start | bytes 3538952 | tf_op jit(solution)/shard_map/ppermute | solution.py:1066
  206.9 49.6 %all-to-all-start = ((bf16[8,104,896]{2,1,0:T(8,128)(2,1)}), bf16[8,104,896]{2,1,0:T(8,128)(2,1)S(1)}, u32[]{:S(2)}, u32[]{:S(2)}) async-start(bf16[8,104,896]{2,1,0:T(8,128)(2,1)} %maximum_maximum_fusion), calls=%async_computation | async-start | bytes 2981888 | tf_op jit(solution)/shard_map/all_to_all | solution.py:1109
  213.3 48.5 %collective-permute-start.4 = (bf16[768,768]{1,0:T(8,128)(2,1)S(1)}, bf16[768,768]{1,0:T(8,128)(2,1)}, u32[]{:S(2)}, u32[]{:S(2)}) collective-permute-start(bf16[768,768]{1,0:T(8,128)(2,1)S(1)} %get-tuple-element.90), channel_id=1, source_target_pairs={{0,1},{1,0},{2,3},{3,2},{4,5},{5,4},{6,7},{7,6},{8,9},{9,8},{10,11... | collective-permute-start | bytes 3538952 | tf_op jit(solution)/shard_map/ppermute | solution.py:1066
  213.9 37.5 %collective-permute-start.8 = (f32[4,2,768]{2,1,0:T(2,128)S(1)}, f32[4,2,768]{2,1,0:T(2,128)S(1)}, u32[]{:S(2)}, u32[]{:S(2)}) collective-permute-start(f32[4,2,768]{2,1,0:T(2,128)S(1)} %slice.214), channel_id=1, source_target_pairs={{0,1},{1,0},{2,3},{3,2},{4,5},{5,4},{6,7},{7,6},{8,9},{9,8},{10,11... | collective-permute-start | bytes 73736 | tf_op jit(solution)/shard_map/ppermute | solution.py:1066
  217.4 44.5 %collective-permute-start.5 = (bf16[768,768]{1,0:T(8,128)(2,1)}, bf16[768,768]{1,0:T(8,128)(2,1)}, u32[]{:S(2)}, u32[]{:S(2)}) collective-permute-start(bf16[768,768]{1,0:T(8,128)(2,1)} %collective-permute-done.1), channel_id=1, source_target_pairs={{0,1},{1,0},{2,3},{3,2},{4,5},{5,4},{6,7},{7,6},{8,9},{9,8},{10,11... | collective-permute-start | bytes 3538952 | tf_op jit(solution)/shard_map/ppermute | solution.py:1066
  243.0 18.9 %collective-permute-start.6 = (bf16[768,768]{1,0:T(8,128)(2,1)}, bf16[768,768]{1,0:T(8,128)(2,1)}, u32[]{:S(2)}, u32[]{:S(2)}) collective-permute-start(bf16[768,768]{1,0:T(8,128)(2,1)} %collective-permute-done.2), channel_id=1, source_target_pairs={{0,1},{1,0},{2,3},{3,2},{4,5},{5,4},{6,7},{7,6},{8,9},{9,8},{10,11... | collective-permute-start | bytes 3538952 | tf_op jit(solution)/shard_map/ppermute | solution.py:1066
  243.0 18.9 %collective-permute-start.7 = (bf16[768,768]{1,0:T(8,128)(2,1)}, bf16[768,768]{1,0:T(8,128)(2,1)}, u32[]{:S(2)}, u32[]{:S(2)}) collective-permute-start(bf16[768,768]{1,0:T(8,128)(2,1)} %collective-permute-done.3), channel_id=1, source_target_pairs={{0,1},{1,0},{2,3},{3,2},{4,5},{5,4},{6,7},{7,6},{8,9},{9,8},{10,11... | collective-permute-start | bytes 3538952 | tf_op jit(solution)/shard_map/ppermute | solution.py:1066
  256.5 36.9 %all-to-all-start.1 = ((bf16[8,104,768]{2,1,0:T(8,128)(2,1)}), bf16[8,104,768]{2,1,0:T(8,128)(2,1)}, u32[]{:S(2)}, u32[]{:S(2)}) async-start(bf16[8,104,768]{2,1,0:T(8,128)(2,1)} %bitcast.117), calls=%async_computation.1 | async-start | bytes 2555904 | tf_op jit(solution)/shard_map/all_to_all | solution.py:1109
  333.1 82.8 %collective-permute-start.17 = (bf16[4,768,768]{2,1,0:T(8,128)(2,1)}, bf16[4,768,768]{2,1,0:T(8,128)(2,1)}, u32[]{:S(2)}, u32[]{:S(2)}) collective-permute-start(bf16[4,768,768]{2,1,0:T(8,128)(2,1)} %constant_dynamic-slice_fusion.5), channel_id=1, source_target_pairs={{0,1},{1,0},{2,3},{3,2},{4,5},{5,4},{6,7},{7,6},{8,9},{9,8},{10,11... | collective-permute-start | bytes 14155784 | tf_op jit(solution)/shard_map/ppermute | solution.py:1066
  333.1 40.5 %all-to-all-start.2 = ((bf16[8,104,896]{2,1,0:T(8,128)(2,1)}), bf16[8,104,896]{2,1,0:T(8,128)(2,1)}, u32[]{:S(2)}, u32[]{:S(2)}) async-start(bf16[8,104,896]{2,1,0:T(8,128)(2,1)} %bitcast.28), calls=%async_computation.2 | async-start | bytes 2981888 | tf_op jit(solution)/shard_map/all_to_all | solution.py:1109
  373.6 34.5 %collective-permute-start.9 = (bf16[832,896]{1,0:T(8,128)(2,1)}, bf16[832,896]{1,0:T(8,128)(2,1)}, u32[]{:S(2)}, u32[]{:S(2)}) collective-permute-start(bf16[832,896]{1,0:T(8,128)(2,1)} %bitcast.29), channel_id=1, source_target_pairs={{0,8},{8,0},{16,24},{24,16},{1,9},{9,1},{17,25},{25,17},{2,10},{10... | collective-permute-start | bytes 4472840 | tf_op jit(solution)/shard_map/ppermute | solution.py:1066
  374.0 35.8 %collective-permute-start.10 = (bf16[832,896]{1,0:T(8,128)(2,1)}, bf16[832,896]{1,0:T(8,128)(2,1)}, u32[]{:S(2)}, u32[]{:S(2)}) collective-permute-start(bf16[832,896]{1,0:T(8,128)(2,1)} %bitcast.29), channel_id=1, source_target_pairs={{0,16},{8,24},{16,0},{24,8},{1,17},{9,25},{17,1},{25,9},{2,18},{10... | collective-permute-start | bytes 4472840 | tf_op jit(solution)/shard_map/ppermute | solution.py:1066
  376.2 69.9 %all-to-all-start.3 = ((bf16[8,104,768]{2,1,0:T(8,128)(2,1)}), bf16[8,104,768]{2,1,0:T(8,128)(2,1)}, u32[]{:S(2)}, u32[]{:S(2)}) async-start(bf16[8,104,768]{2,1,0:T(8,128)(2,1)} %bitcast.116), calls=%async_computation.3 | async-start | bytes 2555904 | tf_op jit(solution)/shard_map/all_to_all | solution.py:1109
  409.3 19.7 %collective-permute-start.11 = (bf16[416,896]{1,0:T(8,128)(2,1)S(1)}, bf16[416,896]{1,0:T(8,128)(2,1)S(1)}, u32[]{:S(2)}, u32[]{:S(2)}) collective-permute-start(bf16[416,896]{1,0:T(8,128)(2,1)S(1)} %slice.277), channel_id=1, source_target_pairs={{0,16},{8,24},{16,0},{24,8},{1,17},{9,25},{17,1},{25,9},{2,18},{10... | collective-permute-start | bytes 2236424 | tf_op jit(solution)/shard_map/ppermute | solution.py:1066
  411.0 18.2 %collective-permute-start.12 = (bf16[416,896]{1,0:T(8,128)(2,1)S(1)}, bf16[416,896]{1,0:T(8,128)(2,1)S(1)}, u32[]{:S(2)}, u32[]{:S(2)}) collective-permute-start(bf16[416,896]{1,0:T(8,128)(2,1)S(1)} %slice.278), channel_id=1, source_target_pairs={{0,8},{8,0},{16,24},{24,16},{1,9},{9,1},{17,25},{25,17},{2,10},{10... | collective-permute-start | bytes 2236424 | tf_op jit(solution)/shard_map/ppermute | solution.py:1066
  422.5 62.1 %collective-permute-start.19 = (bf16[768,768]{1,0:T(8,128)(2,1)}, bf16[768,768]{1,0:T(8,128)(2,1)}, u32[]{:S(2)}, u32[]{:S(2)}) collective-permute-start(bf16[768,768]{1,0:T(8,128)(2,1)} %get-tuple-element.173), channel_id=1, source_target_pairs={{0,16},{8,24},{16,0},{24,8},{1,17},{9,25},{17,1},{25,9},{2,18},{10... | collective-permute-start | bytes 3538952 | tf_op jit(solution)/shard_map/ppermute | solution.py:1066
  446.1 42.8 %collective-permute-start.13 = (bf16[832,768]{1,0:T(8,128)(2,1)}, bf16[832,768]{1,0:T(8,128)(2,1)}, u32[]{:S(2)}, u32[]{:S(2)}) collective-permute-start(bf16[832,768]{1,0:T(8,128)(2,1)} %bitcast.31), channel_id=1, source_target_pairs={{0,8},{8,0},{16,24},{24,16},{1,9},{9,1},{17,25},{25,17},{2,10},{10... | collective-permute-start | bytes 3833864 | tf_op jit(solution)/shard_map/ppermute | solution.py:1066
  446.7 42.2 %collective-permute-start.14 = (bf16[832,768]{1,0:T(8,128)(2,1)}, bf16[832,768]{1,0:T(8,128)(2,1)}, u32[]{:S(2)}, u32[]{:S(2)}) collective-permute-start(bf16[832,768]{1,0:T(8,128)(2,1)} %bitcast.31), channel_id=1, source_target_pairs={{0,16},{8,24},{16,0},{24,8},{1,17},{9,25},{17,1},{25,9},{2,18},{10... | collective-permute-start | bytes 3833864 | tf_op jit(solution)/shard_map/ppermute | solution.py:1066
  483.9 43.3 %collective-permute-start.18 = (bf16[768,768]{1,0:T(8,128)(2,1)}, bf16[768,768]{1,0:T(8,128)(2,1)}, u32[]{:S(2)}, u32[]{:S(2)}) collective-permute-start(bf16[768,768]{1,0:T(8,128)(2,1)} %get-tuple-element.114), channel_id=1, source_target_pairs={{0,16},{8,24},{16,0},{24,8},{1,17},{9,25},{17,1},{25,9},{2,18},{10... | collective-permute-start | bytes 3538952 | tf_op jit(solution)/shard_map/ppermute | solution.py:1066
  487.5 39.8 %collective-permute-start.20 = (bf16[768,768]{1,0:T(8,128)(2,1)}, bf16[768,768]{1,0:T(8,128)(2,1)}, u32[]{:S(2)}, u32[]{:S(2)}) collective-permute-start(bf16[768,768]{1,0:T(8,128)(2,1)} %fusion.24), channel_id=1, source_target_pairs={{0,8},{8,0},{16,24},{24,16},{1,9},{9,1},{17,25},{25,17},{2,10},{10... | collective-permute-start | bytes 3538952 | tf_op jit(solution)/shard_map/ppermute | solution.py:1066
  490.9 32.7 %collective-permute-start.15 = (bf16[416,768]{1,0:T(8,128)(2,1)}, bf16[416,768]{1,0:T(8,128)(2,1)S(1)}, u32[]{:S(2)}, u32[]{:S(2)}) collective-permute-start(bf16[416,768]{1,0:T(8,128)(2,1)} %slice.229), channel_id=1, source_target_pairs={{0,16},{8,24},{16,0},{24,8},{1,17},{9,25},{17,1},{25,9},{2,18},{10... | collective-permute-start | bytes 1916936 | tf_op jit(solution)/shard_map/ppermute | solution.py:1066
  493.4 32.7 %collective-permute-start.16 = (bf16[416,768]{1,0:T(8,128)(2,1)}, bf16[416,768]{1,0:T(8,128)(2,1)}, u32[]{:S(2)}, u32[]{:S(2)}) collective-permute-start(bf16[416,768]{1,0:T(8,128)(2,1)} %slice.230), channel_id=1, source_target_pairs={{0,8},{8,0},{16,24},{24,16},{1,9},{9,1},{17,25},{25,17},{2,10},{10... | collective-permute-start | bytes 1916936 | tf_op jit(solution)/shard_map/ppermute | solution.py:1066
  534.9 226.6 %collective-permute-start.21 = (bf16[784,768]{1,0:T(8,128)(2,1)S(1)}, bf16[784,768]{1,0:T(8,128)(2,1)}, u32[]{:S(2)}, u32[]{:S(2)}) collective-permute-start(bf16[784,768]{1,0:T(8,128)(2,1)S(1)} %reshape.420), channel_id=1, source_target_pairs={{0,8},{8,0},{16,24},{24,16},{1,9},{9,1},{17,25},{25,17},{2,10},{10... | collective-permute-start | bytes 3612680 | tf_op jit(solution)/shard_map/ppermute | solution.py:1066
  535.3 226.2 %collective-permute-start.22 = (bf16[784,768]{1,0:T(8,128)(2,1)S(1)}, bf16[784,768]{1,0:T(8,128)(2,1)}, u32[]{:S(2)}, u32[]{:S(2)}) collective-permute-start(bf16[784,768]{1,0:T(8,128)(2,1)S(1)} %reshape.420), channel_id=1, source_target_pairs={{0,16},{8,24},{16,0},{24,8},{1,17},{9,25},{17,1},{25,9},{2,18},{10... | collective-permute-start | bytes 3612680 | tf_op jit(solution)/shard_map/ppermute | solution.py:1066
  536.9 36.3 %copy-start.19 = (f32[8,768]{1,0:T(8,128)S(1)}, f32[8,768]{1,0:T(8,128)}, u32[]{:S(2)}) copy-start(f32[8,768]{1,0:T(8,128)} %get-tuple-element.138) | copy-start | bytes 73732
  581.4 200.1 %collective-permute-start.25 = (bf16[768,768]{1,0:T(8,128)(2,1)}, bf16[768,768]{1,0:T(8,128)(2,1)S(1)}, u32[]{:S(2)}, u32[]{:S(2)}) collective-permute-start(bf16[768,768]{1,0:T(8,128)(2,1)} %broadcast_select_fusion.2), channel_id=1, source_target_pairs={{0,1},{1,0},{2,3},{3,2},{4,5},{5,4},{6,7},{7,6},{8,9},{9,8},{10,11... | collective-permute-start | bytes 3538952 | tf_op jit(solution)/shard_map/ppermute | solution.py:1066
  762.6 16.1 %collective-permute-start.23 = (bf16[392,768]{1,0:T(8,128)(2,1)S(1)}, bf16[392,768]{1,0:T(8,128)(2,1)S(1)}, u32[]{:S(2)}, u32[]{:S(2)}) collective-permute-start(bf16[392,768]{1,0:T(8,128)(2,1)S(1)} %slice.235), channel_id=1, source_target_pairs={{0,16},{8,24},{16,0},{24,8},{1,17},{9,25},{17,1},{25,9},{2,18},{10... | collective-permute-start | bytes 1806344 | tf_op jit(solution)/shard_map/ppermute | solution.py:1066
  765.7 15.6 %collective-permute-start.24 = (bf16[392,768]{1,0:T(8,128)(2,1)S(1)}, bf16[392,768]{1,0:T(8,128)(2,1)S(1)}, u32[]{:S(2)}, u32[]{:S(2)}) collective-permute-start(bf16[392,768]{1,0:T(8,128)(2,1)S(1)} %slice.236), channel_id=1, source_target_pairs={{0,8},{8,0},{16,24},{24,16},{1,9},{9,1},{17,25},{25,17},{2,10},{10... | collective-permute-start | bytes 1806344 | tf_op jit(solution)/shard_map/ppermute | solution.py:1066
  (46 other events, 221.4 us)

commit v2 on v1

--- a/solution.py
+++ b/solution.py
@@ -403,31 +403,151 @@
     )(y, cot, gate, mine, other, slope)
 
 
-def expert_weight_kernel(x_ref, dy_ref, hid_ref, du_ref, dw_ref):
+def expert_return_kernel(
+    size,
+    x_ref,
+    dy_ref,
+    hid_ref,
+    du_ref,
+    sent_ref,
+    dw_ref,
+    out_ref,
+    swap_send,
+    swap_recv,
+    pass_send,
+    pass_recv,
+    local_sem,
+):
+    step = pl.program_id(0)
     depth = x_ref.shape[1]
+    mine = lax.axis_index("tp")
+    place = lax.axis_index("ep")
+    to_x = {"tp": mine ^ 1}
+    to_y = {"tp": mine ^ 2}
+
+    def remote(src, dst, sends, recvs, index, peer):
+        return pltpu.make_async_remote_copy(
+            src_ref=src,
+            dst_ref=dst,
+            send_sem=sends.at[index],
+            recv_sem=recvs.at[index],
+            device_id=peer,
+            device_id_type=pl.DeviceIdType.MESH,
+        )
+
+    def exchange(k):
+        peer = place ^ k
+        return remote(
+            sent_ref.at[peer], out_ref.at[0, place], swap_send, swap_recv, k, {"ep": peer}
+        )
+
+    def keep():
+        return pltpu.make_async_copy(sent_ref.at[place], out_ref.at[0, place], local_sem)
+
+    def along(k, way):
+        slab = place ^ k
+        return remote(
+            out_ref.at[0, slab],
+            out_ref.at[1 + way, slab],
+            pass_send,
+            pass_recv,
+            (way, k),
+            (to_x, to_y)[way],
+        )
+
+    def relay(k):
+        slab = place ^ k
+        way = k % 2
+        return remote(
+            out_ref.at[1 + way, slab],
+            out_ref.at[3, slab],
+            pass_send,
+            pass_recv,
+            (2, k),
+            (to_y, to_x)[way],
+        )
+
+    def forward(group):
+        for k in range(size // 4 * group, size // 4 * (group + 1)):
+            if k == 0:
+                keep().wait()
+            else:
+                exchange(k).wait_recv()
+            along(k, 0).start()
+            along(k, 1).start()
+
+    @pl.when(step == 0)
+    def _():
+        barrier = pltpu.get_barrier_semaphore()
+        for peer in [to_x, to_y] + [{"ep": place ^ k} for k in range(1, size)]:
+            pl.semaphore_signal(barrier, inc=1, device_id=peer, device_id_type=pl.DeviceIdType.MESH)
+        pl.semaphore_wait(barrier, size + 1)
+        keep().start()
+        for k in range(1, size):
+            exchange(k).start()
+
+    for group in range(3):
+
+        @pl.when(step == group + 1)
+        def _(group=group):
+            forward(group)
+
     dw_ref[0, depth:, :] = dot(hid_ref[0], dy_ref[...], TN).astype(BF)
     dw_ref[0, :depth, :] = dot(x_ref[...], du_ref[0], TN).astype(BF)
 
-
-def expert_weight(x, dy, hid, du):
+    @pl.when(step == 3)
+    def _():
+        forward(3)
+        for k in range(size):
+            along(k, k % 2).wait_recv()
+            relay(k).start()
+        for k in range(size):
+            along(k, 1 - k % 2).wait_recv()
+            relay(k).wait_recv()
+        for k in range(size):
+            if k > 0:
+                exchange(k).wait_send()
+            along(k, 0).wait_send()
+            along(k, 1).wait_send()
+            relay(k).wait_send()
+
+
+def expert_return(x, dy, hid, du, sent):
     rows, depth = x.shape
     shards, _, hidden = hid.shape
+    size = sent.shape[0]
     shard = lambda r: (r, 0, 0)
     wide = pl.BlockSpec((1, rows, hidden), shard)
+    any_spec = pl.BlockSpec(memory_space=pl.ANY)
     return pl.pallas_call(
-        expert_weight_kernel,
+        lambda *refs: expert_return_kernel(size, *refs),
         grid=(shards,),
-        in_specs=[whole(), whole(), wide, wide],
-        out_specs=pl.BlockSpec((1, 2 * depth, hidden), shard),
-        out_shape=jax.ShapeDtypeStruct((shards, 2 * depth, hidden), BF),
-        compiler_params=params(),
+        in_specs=[whole(), whole(), wide, wide, any_spec],
+        out_specs=[pl.BlockSpec((1, 2 * depth, hidden), shard), any_spec],
+        out_shape=[
+            jax.ShapeDtypeStruct((shards, 2 * depth, hidden), BF),
+            jax.ShapeDtypeStruct((shards,) + sent.shape, BF),
+        ],
+        scratch_shapes=[
+            pltpu.SemaphoreType.DMA((size,)),
+            pltpu.SemaphoreType.DMA((size,)),
+            pltpu.SemaphoreType.DMA((3, size)),
+            pltpu.SemaphoreType.DMA((3, size)),
+            pltpu.SemaphoreType.DMA,
+        ],
+        compiler_params=pltpu.CompilerParams(
+            dimension_semantics=("arbitrary",),
+            vmem_limit_bytes=VMEM_LIMIT,
+            collective_id=2,
+            has_side_effects=True,
+        ),
         cost_estimate=pl.CostEstimate(
             flops=4 * rows * depth * hidden * shards * 2,
-            bytes_accessed=25_000_000,
+            bytes_accessed=40_000_000,
             transcendentals=0,
         ),
-        name="expert_weight",
-    )(x, dy, hid, du)
+        name="expert_return",
+    )(x, dy, hid, du, sent)
 
 
 ROUTES = 6
@@ -838,9 +958,9 @@
     bits = plane_bits(size)
     take = iter(refs)
     sources = [next(take) for _ in range(groups)]
-    ig_ref, small_ref = next(take), next(take)
+    ig_ref, act_x, act_y, small_ref = [next(take) for _ in range(4)]
     outs = [next(take) for _ in range(groups)]
-    ig_out, total_ref, pair_ref = next(take), next(take), next(take)
+    ig_out, act_out, total_ref, pair_ref = [next(take) for _ in range(4)]
     keeps = [next(take) for _ in range(groups)]
     cores = [next(take) for _ in range(groups)]
     firsts = [next(take) for _ in range(groups)]
@@ -970,6 +1090,12 @@
         for copy in near:
             copy.start()
         yield
+        passed = [
+            remote(act_x.at[low], act_out.at[low], ig_send, ig_recv, 4, to_y),
+            remote(act_y.at[high], act_out.at[high], ig_send, ig_recv, 5, to_x),
+        ]
+        for copy in passed:
+            copy.start()
         for copy in near:
             copy.wait_recv()
         relay = [
@@ -981,7 +1107,9 @@
         yield
         for copy in relay:
             copy.wait_recv()
-        for copy in near + relay:
+        for copy in passed:
+            copy.wait_recv()
+        for copy in near + relay + passed:
             copy.wait_send()
         local.wait()
 
@@ -1014,7 +1142,7 @@
             advance(which)
 
 
-def tail(grads, ig, small, size):
+def tail(grads, ig, act_x, act_y, small, size):
     shards, _, depth = grads[0].shape
     rows_list = [g.shape[1] for g in grads]
     groups = len(grads)
@@ -1033,10 +1161,10 @@
     copies = 4 + 2 + 2 * len(bits) + 1
     return pl.pallas_call(
         lambda *refs: tail_kernel(size, rows_list, *refs),
-        in_specs=[any_spec] * (groups + 1) + [whole()],
-        out_specs=[any_spec] * (groups + 1) + [whole(), whole()],
+        in_specs=[any_spec] * (groups + 3) + [whole()],
+        out_specs=[any_spec] * (groups + 2) + [whole(), whole()],
         out_shape=[shape((rows, depth), BF) for rows in rows_list]
-        + [shape((shards,) + ig.shape, BF), shape(small.shape, F32), shape(small.shape, F32)],
+        + [shape((shards,) + ig.shape, BF), shape(ig.shape, BF), shape(small.shape, F32), shape(small.shape, F32)],
         scratch_shapes=[pltpu.VMEM((shards, rows // 2, depth), BF) for rows in rows_list]
         + [pltpu.VMEM((shards, rows // 2, depth), BF) for rows in rows_list]
         + [pltpu.VMEM((4, rows // 4, depth), BF) for rows in rows_list]
@@ -1048,8 +1176,8 @@
             pltpu.SemaphoreType.DMA((groups, copies)),
             pltpu.SemaphoreType.DMA((groups, copies)),
             pltpu.SemaphoreType.DMA((2 * groups + 1,)),
-            pltpu.SemaphoreType.DMA((4,)),
-            pltpu.SemaphoreType.DMA((4,)),
+            pltpu.SemaphoreType.DMA((6,)),
+            pltpu.SemaphoreType.DMA((6,)),
             pltpu.SemaphoreType.DMA((3 + len(bits),)),
             pltpu.SemaphoreType.DMA((3 + len(bits),)),
         ],
@@ -1058,7 +1186,7 @@
         ),
         cost_estimate=pl.CostEstimate(flops=30_000_000, bytes_accessed=60_000_000, transcendentals=0),
         name="tail",
-    )(*grads, ig, small)
+    )(*grads, ig, act_x, act_y, small)
 
 
 def hop(value, axis, bit):
@@ -1262,35 +1390,6 @@
         ]
     )
     own_biases = jnp.pad(own_biases, ((0, 3), (0, 0)))
-    position = route(picks, priority[0])
-    targets = jnp.where(position < capacity, picks * (part * shards) + position, -1).T
-    slots = jnp.arange(experts * part, dtype=jnp.int32)
-
-    def slots_of(index):
-        block, inside = slots // part, slots % part
-        expert = 2 * (block // 2) + index % 2
-        quarter = 2 * (index // 2) + block % 2
-        return expert * (part * shards) + quarter * part + inside
-
-    slot_ids = slots_of(mine)
-    pad_targets = jnp.pad(
-        targets.reshape(2, -1, LEN), ((0, 0), (0, 0), (0, PAD - LEN)), constant_values=-1
-    ).reshape(2, -1)
-    near_targets = jnp.concatenate(
-        [
-            lax.dynamic_slice_in_dim(pad_targets, (mine ^ r) * own_pad, own_pad, axis=1)
-            for r in range(shards)
-        ],
-        axis=1,
-    )
-    noise_pad = pad_images(router_noise)
-    all_slots = jnp.concatenate([slots_of(mine ^ r) for r in range(shards)])
-    own_targets = near_targets[:, :own_pad].T
-    back_hot = (own_targets[:, 0:1] == all_slots[None, :]) | (
-        own_targets[:, 1:2] == all_slots[None, :]
-    )
-    back_hot_bf = back_hot.astype(BF)
-
     swapped = hop(give_exp, "ep", 1)
     home_exp = jnp.where(same, keep_exp, swapped)
     away_exp = jnp.where(same, swapped, keep_exp)
@@ -1319,6 +1418,35 @@
     exp_y = hop(home_exp, "tp", 2)
     other_home = hop(home_exp, "ep", 1)
 
+    position = route(after(picks, normed), priority[0])
+    targets = jnp.where(position < capacity, picks * (part * shards) + position, -1).T
+    slots = jnp.arange(experts * part, dtype=jnp.int32)
+
+    def slots_of(index):
+        block, inside = slots // part, slots % part
+        expert = 2 * (block // 2) + index % 2
+        quarter = 2 * (index // 2) + block % 2
+        return expert * (part * shards) + quarter * part + inside
+
+    slot_ids = slots_of(mine)
+    pad_targets = jnp.pad(
+        targets.reshape(2, -1, LEN), ((0, 0), (0, 0), (0, PAD - LEN)), constant_values=-1
+    ).reshape(2, -1)
+    near_targets = jnp.concatenate(
+        [
+            lax.dynamic_slice_in_dim(pad_targets, (mine ^ r) * own_pad, own_pad, axis=1)
+            for r in range(shards)
+        ],
+        axis=1,
+    )
+    noise_pad = pad_images(router_noise)
+    all_slots = jnp.concatenate([slots_of(mine ^ r) for r in range(shards)])
+    own_targets = near_targets[:, :own_pad].T
+    back_hot = (own_targets[:, 0:1] == all_slots[None, :]) | (
+        own_targets[:, 1:2] == all_slots[None, :]
+    )
+    back_hot_bf = back_hot.astype(BF)
+
     all_normed = normed.reshape(shards * own_pad, depth)
     route_normed = normed[0]
     noise = jnp.concatenate(
@@ -1352,6 +1480,7 @@
     cot_hot = (slot_ids[:, None] == targets[0][None, :]) | (slot_ids[:, None] == targets[1][None, :])
     cot_sent = dot(after(cot_hot.astype(BF), rows), cotangent, NN).astype(BF)
     cot_rows = swap_rows(cot_sent)
+    exp_x, exp_y, exp_far = after((exp_x, exp_y, exp_far), cot_sent)
     exp_mine = jnp.stack([home_exp, exp_x, exp_y, exp_far])
     exp_other = jnp.stack(
         [other_home, hop(exp_x, "ep", 1), hop(exp_y, "ep", 1), hop(exp_far, "ep", 1)]
@@ -1363,18 +1492,17 @@
     weighted, grad_outputs, grad_inputs, slot_dot, exp_du, small_exp = (
         expert_input(outputs, cot_rows, gate_in, exp_mine, exp_other, exp_slope)
     )
-    returned_sent = jnp.concatenate([grad_inputs, two_parts(slot_dot)], axis=1)
-    returned = swap_rows(returned_sent)
-    g_exp = expert_weight(after(inputs, returned_sent), grad_outputs, exp_hidden, exp_du)
+    sent = jnp.concatenate([grad_inputs, two_parts(slot_dot)], axis=1)
+    g_exp, grad_slots = expert_return(
+        inputs, grad_outputs, exp_hidden, exp_du, sent.reshape(experts, part, sent.shape[1])
+    )
+    grad_slots = grad_slots.reshape(shards * experts * part, sent.shape[1])
     part_exp = core_sum(g_exp)
     exp_from_y = hop(part_exp[3], "tp", 2)
-    returned = after(returned, g_exp)
-    near_grad = near(returned)
-    grad_slots = jnp.concatenate([returned, *near_grad, far(*near_grad)])
     dot_slots = grad_slots[:, depth : depth + 2].astype(F32)
     dot_slots = dot_slots[:, 0] + dot_slots[:, 1]
+    weighted = swap_rows(after(weighted, grad_slots))
     grad_slots = grad_slots[:, :depth]
-    weighted = swap_rows(after(weighted, returned))
 
     grad_stream = pad_images(own_rows(cotangent)).astype(F32)
     own_gates = gates[:own_pad]
@@ -1421,7 +1549,6 @@
         grad_stream, level_zero, row(dense_norm_gain), row(dense_norm_bias), w_one, kept_one
     )
     near_final = after(near_final, g_one)
-    far_final = far(*near_final)
 
     blank = jnp.zeros_like(small_exp)
     first = chip_side == 0
@@ -1436,11 +1563,11 @@
             jnp.pad(jnp.stack([g_route_gain, g_route_bias]), ((0, 6), (0, 0))),
         ]
     )
-    t_two, t_feed, t_one, ig_all, total, pair_total = tail(
-        [g_two, g_feed, g_one], drop_pad(grad_stream.astype(BF)), small, experts
+    t_two, t_feed, t_one, ig_all, far_final, total, pair_total = tail(
+        [g_two, g_feed, g_one], drop_pad(grad_stream.astype(BF)), *near_final, small, experts
     )
     input_grad = ig_all.reshape(rows_dev, depth).astype(F32)
-    far_final, other_sum = after((far_final, other_sum), t_one)
+    other_sum = after(other_sum, t_one)
 
     def absolute(blocks, kind):
         out = jnp.zeros((rows_dev, depth), kind)

time: 794 us -> 777 us (0.979)
  waiting for transfers between devices: 107 us -> 45.3 us
  Pallas kernels: 471 us -> 521 us
  starting transfers between devices: 40.1 us -> 29 us
    ppermute x26 -> x20, waiting for transfers between devices: 73.2 us -> 22.7 us  [hop(): return lax.ppermute(value, axis, [(i, i ^ bit) for i in range(size)])]
    pallas_call x1, Pallas kernels: 14.5 us -> 63.4 us  [expert_return(): pl.pallas_call(lambda *refs: expert_return_kernel(size, *refs), grid=(sha...]
    all_to_all x4 -> x3, waiting for transfers between devices: 33.9 us -> 22.5 us  [swap_ep(): return lax.all_to_all(value, 'ep', split_axis=0, concat_axis=0, tiled=True)]
    ppermute x26 -> x20, starting transfers between devices: 21.2 us -> 14.6 us  [hop(): return lax.ppermute(value, axis, [(i, i ^ bit) for i in range(size)])]
    all_to_all x4 -> x3, starting transfers between devices: 19 us -> 14.4 us  [swap_ep(): return lax.all_to_all(value, 'ep', split_axis=0, concat_axis=0, tiled=True)]
  transfers between devices with their start and end apart: 30 -> 23, of which waited for: 9 -> 5; matrix products, arithmetic and copies ran while one was open for 17% -> 15% of each run, Pallas kernels for 37% -> 37%
where the time goes in v2:
time: 777 us; the launch traced here: 772 us
  Pallas kernels  521 us (67%)
  other arithmetic  77.3 us (10%)
  local copies, waits for them, and re-layouts  59.1 us (8%)
  waiting for transfers between devices  45.3 us (6%)
  matrix products  38.1 us (5%)
  starting transfers between devices  29 us (4%)
    pallas_call x1, Pallas kernels, tail(): pl.pallas_call(lambda *refs: tail_kernel(size, rows_list, *refs), in_spec...  162 us
    pallas_call x1, Pallas kernels, dense_forward(): pl.pallas_call(forward_kernel, grid=(3 * images,), in_specs=[whole(), who...  144 us
    pallas_call x2, Pallas kernels, attend_backward(): pl.pallas_call(attend_backward_kernel, grid=(images,), in_specs=[row_bloc...  71.3 us
    pallas_call x1, Pallas kernels, expert_return(): pl.pallas_call(lambda *refs: expert_return_kernel(size, *refs), grid=(sha...  63.4 us
    dot_general x7, matrix products, dot(): return lax.dot_general(a, b, (dims, ((), ())), preferred_element_type=F32)  38.1 us
    pallas_call x1, Pallas kernels, feed_backward(): pl.pallas_call(feed_backward_kernel, grid=(shards,), in_specs=[whole(), w...  28.5 us
    ppermute x20, waiting for transfers between devices, hop(): return lax.ppermute(value, axis, [(i, i ^ bit) for i in range(size)])  22.7 us
    all_to_all x3, waiting for transfers between devices, swap_ep(): return lax.all_to_all(value, 'ep', split_axis=0, concat_axis=0, tiled=True)  22.5 us
  transfers between devices with their start and end apart: 23, of which 5 were waited for; matrix products, arithmetic and copies ran while one was open for 15% of the time, Pallas kernels for 37%

profile of v2, /device:TPU:0, one launch (start us, length us, event | category | flops | bytes accessed | tf_op | source)
XLA Modules:
  0.0 772.0 jit_solution(9995523238550651430)
XLA Ops:
  18.1 3.1 pad_maximum_fusion.4
  21.4 3.0 pad_maximum_fusion.2.feed_ref
  27.3 3.0 bitcast_select_fusion
  30.3 144.4 %dense_forward.1 = (f32[832,768]{1,0:T(8,128)}, f32[832,768]{1,0:T(8,128)}, f32[832,768]{1,0:T(8,128)}, bf16[4,4,576,208]{3,2,1,0:T(8,128)(2,1)}, f32[4,4,3,208]...) custom-call(bf16[832,768]{1,0:T(8,128)(2,1)} %bitcast.108, ...), custom_call_target="tpu_custom_call" | custom-call | flops 60000002048 | bytes 60000000 | tf_op jit(solution)/shard_map/dense_forward/pallas_call | solution.py:880
  179.5 13.7 %route.1 = f32[3136,128]{1,0:T(8,128)} custom-call(s32[1,3136]{1,0:T(1,128)} %order_ref.1, bf16[3136,128]{1,0:T(8,128)(2,1)} %select_convert_fusion.index_ref, bf16[3136,128]{1,0:T(8,128)(2,1)} %add_convert_fusion.2.hot_ref), custom_call_target="tpu_custom_call" | custom-call | flops 5035261952 | bytes 4000000 | tf_op jit(solution)/shard_map/route/pallas_call | solution.py:1274
  201.8 3.9 fusion.85
  206.0 7.3 fusion.27
  217.0 4.9 all-to-all-start
  221.9 3.9 or_convert_fusion
  226.0 9.4 %convolution_convert_fusion = bf16[832,768]{1,0:T(8,128)(2,1)} fusion(bf16[832,3136]{1,0:T(8,128)(2,1)} %or_convert_fusion, bf16[3136,768]{1,0:T(8,128)(2,1)} %param.31), kind=kOutput, calls=%fused_computation.54 | convolution fusion | flops 4008296448 | bytes 11313152 | tf_op jit(solution)/shard_map/dot_general | solution.py:22
  235.5 16.4 %collective-permute-done.2 = bf16[768,768]{1,0:T(8,128)(2,1)} collective-permute-done((bf16[768,768]{1,0:T(8,128)(2,1)}, bf16[768,768]{1,0:T(8,128)(2,1)}, u32[]{:S(2)}, u32[]{:S(2)}) %collective-permute-start.2) | collective-permute-done | bytes 1179680 | tf_op jit(solution)/shard_map/ppermute | solution.py:1194
  254.1 4.1 pad_maximum_fusion.mine_ref
  258.2 5.2 all-to-all-start.1
  263.5 4.0 pad_maximum_fusion.1.other_ref
  271.8 21.1 %expert_forward.1 = (bf16[832,768]{1,0:T(8,128)(2,1)}, bf16[4,832,768]{2,1,0:T(8,128)(2,1)}, bf16[4,832,768]{2,1,0:T(8,128)(2,1)}) custom-call(bf16[832,768]{1,0:T(8,128)(2,1)} %slice.252.x_ref.refs_0_, bf16[4,768,768]{2,1,0:T(8,128)(2,1)} %pad_maximum_fusion.mine_ref, bf16[4,768,768]{2,1,0:T(8,128)(2,1)} %pad_maximum_fusion.1.other_ref, ...), custom_call_target="tpu_custom_call" | custom-call | flops 15703474176 | bytes 25000000 | tf_op jit(solution)/shard_map/expert_forward/pallas_call | solution.py:305
  295.0 16.5 %expert_input.1 = (bf16[832,768]{1,0:T(8,128)(2,1)}, bf16[832,768]{1,0:T(8,128)(2,1)}, bf16[832,768]{1,0:T(8,128)(2,1)}, f32[832,1]{1,0:T(8,128)}, bf16[4,832,768]{2,1,0:T(8,128)(2,1)}, /*index=5*/f32[8,768]{1,0:T(8,128)}) custom-call(bf16[832,768]{1,0:T(8,128)(2,1)} %get-tuple-element.102.y_ref, bf16[832,768]{1,0:T(8,128)(2,1)} %bitcast.27.cot_ref, ...), custom_call_target="tpu_custom_call" | custom-call | flops 15703474176 | bytes 25000000 | tf_op jit(solution)/shard_map/expert_input/pallas_call | solution.py:375
  315.4 63.4 %expert_return.1 = (bf16[4,1536,768]{2,1,0:T(8,128)(2,1)}, bf16[4,8,104,896]{3,2,1,0:T(8,128)(2,1)}) custom-call(bf16[832,768]{1,0:T(8,128)(2,1)} %slice.252.x_ref.refs_0_, bf16[832,768]{1,0:T(8,128)(2,1)} %get-tuple-element.105.refs_1_, bf16[4,832,768]{2,1,0:T(8,128)(2,1)} %get-tuple-element.106.refs_2_, bf16[4,832,768]{2,1,0:T(8,128)(2,1)} %get-tuple-element.107.refs_3_, ...), custom_call_target="tpu_custom_call" | custom-call | flops 15703474176 | bytes 40000000 | tf_op jit(solution)/shard_map/expert_return/pallas_call | solution.py:522
  378.8 4.9 constant_dynamic-slice_fusion.5
  389.2 3.1 select_reduce_fusion
  392.4 4.3 all-to-all-start.2
  396.7 7.3 fusion.5
  407.7 20.4 %all-to-all-done.2 = bf16[8,104,768]{2,1,0:T(8,128)(2,1)} async-done(((bf16[8,104,768]{2,1,0:T(8,128)(2,1)}), bf16[8,104,768]{2,1,0:T(8,128)(2,1)}, u32[]{:S(2)}, u32[]{:S(2)}) %all-to-all-start.2) | async-done | bytes 1277984 | tf_op jit(solution)/shard_map/all_to_all | solution.py:1237
  430.2 4.9 add_convert_fusion
  439.7 35.7 %attend_backward.2 = (f32[832,768]{1,0:T(8,128)}, bf16[4,768,768]{2,1,0:T(8,128)(2,1)}, f32[8,768]{1,0:T(8,128)}) custom-call(f32[832,768]{1,0:T(8,128)} %convert_add_fusion.g_ref, f32[832,768]{1,0:T(8,128)} %get-tuple-element.113.h_ref, f32[1,768]{1,0:T(1,128)} %copy-done.41, f32[1,768]{1,0:T(1,128)} %copy-done.42, ...), custom_call_target="tpu_custom_call" | custom-call | flops 26744979456 | bytes 30000000 | tf_op jit(solution)/shard_map/attend_backward/pallas_call | solution.py:153
  488.6 28.5 %feed_backward.1 = (f32[832,768]{1,0:T(8,128)}, bf16[4,1536,768]{2,1,0:T(8,128)(2,1)}, f32[8,768]{1,0:T(8,128)}) custom-call(f32[832,768]{1,0:T(8,128)} %get-tuple-element.124.g_ref, f32[832,768]{1,0:T(8,128)} %get-tuple-element.125.h_ref, f32[1,768]{1,0:T(1,128)} %copy-done.39, f32[1,768]{1,0:T(1,128)} %copy-done.40, ...), custom_call_target="tpu_custom_call" | custom-call | flops 31406948352 | bytes 35000000 | tf_op jit(solution)/shard_map/feed_backward/pallas_call | solution.py:236
  518.3 4.0 collective-permute-done.14
  522.4 7.0 add_convert_fusion.1
  533.0 3.4 broadcast_select_fusion.1
  536.4 35.5 %attend_backward.3 = (f32[832,768]{1,0:T(8,128)}, bf16[4,768,768]{2,1,0:T(8,128)(2,1)}, f32[8,768]{1,0:T(8,128)}) custom-call(f32[832,768]{1,0:T(8,128)} %get-tuple-element.132.g_ref, f32[832,768]{1,0:T(8,128)} %convert_element_type.159.h_ref, f32[1,768]{1,0:T(1,128)} %copy-done.37, f32[1,768]{1,0:T(1,128)} %copy-done.38, ...), custom_call_target="tpu_custom_call" | custom-call | flops 26744979456 | bytes 30000000 | tf_op jit(solution)/shard_map/attend_backward/pallas_call | solution.py:153
  582.1 161.7 %tail.1 = (bf16[768,768]{1,0:T(8,128)(2,1)}, bf16[1536,768]{1,0:T(8,128)(2,1)}, bf16[768,768]{1,0:T(8,128)(2,1)}, bf16[4,784,768]{2,1,0:T(8,128)(2,1)}, bf16[784...) custom-call(bf16[4,768,768]{2,1,0:T(8,128)(2,1)} %get-tuple-element.118.refs_0_, ...), custom_call_target="tpu_custom_call" | custom-call | flops 30000000 | bytes 60000000 | tf_op jit(solution)/shard_map/tail/pallas_call | solution.py:1162
  749.5 5.4 bitcast_convert_fusion.1
  755.0 4.9 bitcast_convert_fusion
  (306 shorter events, 110.8 us)
Async XLA Ops:
  0.7 201.1 %copy-start = (bf16[768,8]{0,1:T(8,128)(2,1)S(1)}, bf16[768,8]{0,1:T(8,128)(2,1)}, u32[]{:S(2)}) copy-start(bf16[768,8]{0,1:T(8,128)(2,1)} %param.55) | copy-start | bytes 36868
  3.1 24.1 %collective-permute-start = (bf16[768,768]{1,0:T(8,128)(2,1)}, bf16[768,768]{1,0:T(8,128)(2,1)}, u32[]{:S(2)}, u32[]{:S(2)}) collective-permute-start(bf16[768,768]{1,0:T(8,128)(2,1)} %select_bitcast_fusion.1), channel_id=1, source_target_pairs={{0,1},{1,0},{2,3},{3,2},{4,5},{5,4},{6,7},{7,6},{8,9},{9,8},{10,11... | collective-permute-start | bytes 3538952 | tf_op jit(solution)/shard_map/ppermute | solution.py:1194
  30.3 144.4 %copy-start.24 = (s32[3136,2]{0,1:T(2,128)S(1)}, s32[3136,2]{0,1:T(2,128)}, u32[]{:S(2)}) copy-start(s32[3136,2]{0,1:T(2,128)} %param.32) | copy-start | bytes 75268
  196.8 38.7 %collective-permute-start.1 = (bf16[768,768]{1,0:T(8,128)(2,1)}, bf16[768,768]{1,0:T(8,128)(2,1)}, u32[]{:S(2)}, u32[]{:S(2)}) collective-permute-start(bf16[768,768]{1,0:T(8,128)(2,1)} %get-tuple-element.96), channel_id=1, source_target_pairs={{0,8},{8,0},{16,24},{24,16},{1,9},{9,1},{17,25},{25,17},{2,10},{10... | collective-permute-start | bytes 3538952 | tf_op jit(solution)/shard_map/ppermute | solution.py:1194
  198.9 53.0 %collective-permute-start.3 = (bf16[768,768]{1,0:T(8,128)(2,1)}, bf16[768,768]{1,0:T(8,128)(2,1)}, u32[]{:S(2)}, u32[]{:S(2)}) collective-permute-start(bf16[768,768]{1,0:T(8,128)(2,1)} %get-tuple-element.96), channel_id=1, source_target_pairs={{0,24},{8,16},{16,8},{24,0},{1,25},{9,17},{17,9},{25,1},{2,26},{10... | collective-permute-start | bytes 3538952 | tf_op jit(solution)/shard_map/ppermute | solution.py:1194
  200.4 51.5 %collective-permute-start.2 = (bf16[768,768]{1,0:T(8,128)(2,1)}, bf16[768,768]{1,0:T(8,128)(2,1)}, u32[]{:S(2)}, u32[]{:S(2)}) collective-permute-start(bf16[768,768]{1,0:T(8,128)(2,1)} %get-tuple-element.95), channel_id=1, source_target_pairs={{0,16},{8,24},{16,0},{24,8},{1,17},{9,25},{17,1},{25,9},{2,18},{10... | collective-permute-start | bytes 3538952 | tf_op jit(solution)/shard_map/ppermute | solution.py:1194
  200.5 62.9 %collective-permute-start.4 = (bf16[768,768]{1,0:T(8,128)(2,1)}, bf16[768,768]{1,0:T(8,128)(2,1)}, u32[]{:S(2)}, u32[]{:S(2)}) collective-permute-start(bf16[768,768]{1,0:T(8,128)(2,1)} %get-tuple-element.95), channel_id=1, source_target_pairs={{0,1},{1,0},{2,3},{3,2},{4,5},{5,4},{6,7},{7,6},{8,9},{9,8},{10,11... | collective-permute-start | bytes 3538952 | tf_op jit(solution)/shard_map/ppermute | solution.py:1194
  200.5 52.4 %collective-permute-start.8 = (f32[4,2,768]{2,1,0:T(2,128)S(1)}, f32[4,2,768]{2,1,0:T(2,128)S(1)}, u32[]{:S(2)}, u32[]{:S(2)}) collective-permute-start(f32[4,2,768]{2,1,0:T(2,128)S(1)} %slice.204), channel_id=1, source_target_pairs={{0,1},{1,0},{2,3},{3,2},{4,5},{5,4},{6,7},{7,6},{8,9},{9,8},{10,11... | collective-permute-start | bytes 73736 | tf_op jit(solution)/shard_map/ppermute | solution.py:1194
  217.0 41.1 %all-to-all-start = ((bf16[8,104,896]{2,1,0:T(8,128)(2,1)}), bf16[8,104,896]{2,1,0:T(8,128)(2,1)}, u32[]{:S(2)}, u32[]{:S(2)}) async-start(bf16[8,104,896]{2,1,0:T(8,128)(2,1)} %maximum_maximum_fusion), calls=%async_computation | async-start | bytes 2981888 | tf_op jit(solution)/shard_map/all_to_all | solution.py:1237
  251.9 11.5 %collective-permute-start.5 = (bf16[768,768]{1,0:T(8,128)(2,1)}, bf16[768,768]{1,0:T(8,128)(2,1)}, u32[]{:S(2)}, u32[]{:S(2)}) collective-permute-start(bf16[768,768]{1,0:T(8,128)(2,1)} %collective-permute-done.1), channel_id=1, source_target_pairs={{0,1},{1,0},{2,3},{3,2},{4,5},{5,4},{6,7},{7,6},{8,9},{9,8},{10,11... | collective-permute-start | bytes 3538952 | tf_op jit(solution)/shard_map/ppermute | solution.py:1194
  251.9 11.6 %collective-permute-start.6 = (bf16[768,768]{1,0:T(8,128)(2,1)}, bf16[768,768]{1,0:T(8,128)(2,1)}, u32[]{:S(2)}, u32[]{:S(2)}) collective-permute-start(bf16[768,768]{1,0:T(8,128)(2,1)} %collective-permute-done.2), channel_id=1, source_target_pairs={{0,1},{1,0},{2,3},{3,2},{4,5},{5,4},{6,7},{7,6},{8,9},{9,8},{10,11... | collective-permute-start | bytes 3538952 | tf_op jit(solution)/shard_map/ppermute | solution.py:1194
  252.4 11.1 %collective-permute-start.7 = (bf16[768,768]{1,0:T(8,128)(2,1)}, bf16[768,768]{1,0:T(8,128)(2,1)}, u32[]{:S(2)}, u32[]{:S(2)}) collective-permute-start(bf16[768,768]{1,0:T(8,128)(2,1)} %collective-permute-done.3), channel_id=1, source_target_pairs={{0,1},{1,0},{2,3},{3,2},{4,5},{5,4},{6,7},{7,6},{8,9},{9,8},{10,11... | collective-permute-start | bytes 3538952 | tf_op jit(solution)/shard_map/ppermute | solution.py:1194
  258.2 36.8 %all-to-all-start.1 = ((bf16[8,104,768]{2,1,0:T(8,128)(2,1)}), bf16[8,104,768]{2,1,0:T(8,128)(2,1)}, u32[]{:S(2)}, u32[]{:S(2)}) async-start(bf16[8,104,768]{2,1,0:T(8,128)(2,1)} %bitcast.119), calls=%async_computation.1 | async-start | bytes 2555904 | tf_op jit(solution)/shard_map/all_to_all | solution.py:1237
  383.7 46.5 %collective-permute-start.13 = (bf16[4,768,768]{2,1,0:T(8,128)(2,1)}, bf16[4,768,768]{2,1,0:T(8,128)(2,1)}, u32[]{:S(2)}, u32[]{:S(2)}) collective-permute-start(bf16[4,768,768]{2,1,0:T(8,128)(2,1)} %constant_dynamic-slice_fusion.5), channel_id=1, source_target_pairs={{0,1},{1,0},{2,3},{3,2},{4,5},{5,4},{6,7},{7,6},{8,9},{9,8},{10,11... | collective-permute-start | bytes 14155784 | tf_op jit(solution)/shard_map/ppermute | solution.py:1194
  388.3 8.4 %copy-start.30 = (s32[3328]{0:T(1024)S(1)}, s32[3328]{0:T(1024)}, u32[]{:S(2)}) copy-start(s32[3328]{0:T(1024)} %copy-done.29) | copy-start | bytes 39940
  388.3 8.4 %copy-start.36 = (s32[832]{0:T(1024)S(1)}, s32[832]{0:T(1024)}, u32[]{:S(2)}) copy-start(s32[832]{0:T(1024)} %get-tuple-element.178) | copy-start | bytes 9988
  392.4 35.8 %all-to-all-start.2 = ((bf16[8,104,768]{2,1,0:T(8,128)(2,1)}), bf16[8,104,768]{2,1,0:T(8,128)(2,1)}, u32[]{:S(2)}, u32[]{:S(2)}) async-start(bf16[8,104,768]{2,1,0:T(8,128)(2,1)} %bitcast.118), calls=%async_computation.2 | async-start | bytes 2555904 | tf_op jit(solution)/shard_map/all_to_all | solution.py:1237
  396.7 7.3 copy-start.32
  428.2 47.3 %collective-permute-start.10 = (bf16[832,768]{1,0:T(8,128)(2,1)}, bf16[832,768]{1,0:T(8,128)(2,1)}, u32[]{:S(2)}, u32[]{:S(2)}) collective-permute-start(bf16[832,768]{1,0:T(8,128)(2,1)} %bitcast.31), channel_id=1, source_target_pairs={{0,16},{8,24},{16,0},{24,8},{1,17},{9,25},{17,1},{25,9},{2,18},{10... | collective-permute-start | bytes 3833864 | tf_op jit(solution)/shard_map/ppermute | solution.py:1194
  429.1 46.4 %collective-permute-start.9 = (bf16[832,768]{1,0:T(8,128)(2,1)}, bf16[832,768]{1,0:T(8,128)(2,1)}, u32[]{:S(2)}, u32[]{:S(2)}) collective-permute-start(bf16[832,768]{1,0:T(8,128)(2,1)} %bitcast.31), channel_id=1, source_target_pairs={{0,8},{8,0},{16,24},{24,16},{1,9},{9,1},{17,25},{25,17},{2,10},{10... | collective-permute-start | bytes 3833864 | tf_op jit(solution)/shard_map/ppermute | solution.py:1194
  438.8 46.0 %collective-permute-start.15 = (bf16[768,768]{1,0:T(8,128)(2,1)}, bf16[768,768]{1,0:T(8,128)(2,1)}, u32[]{:S(2)}, u32[]{:S(2)}) collective-permute-start(bf16[768,768]{1,0:T(8,128)(2,1)} %get-tuple-element.181), channel_id=1, source_target_pairs={{0,16},{8,24},{16,0},{24,8},{1,17},{9,25},{17,1},{25,9},{2,18},{10... | collective-permute-start | bytes 3538952 | tf_op jit(solution)/shard_map/ppermute | solution.py:1194
  477.4 39.7 %collective-permute-start.11 = (bf16[416,768]{1,0:T(8,128)(2,1)}, bf16[416,768]{1,0:T(8,128)(2,1)S(1)}, u32[]{:S(2)}, u32[]{:S(2)}) collective-permute-start(bf16[416,768]{1,0:T(8,128)(2,1)} %slice.215), channel_id=1, source_target_pairs={{0,16},{8,24},{16,0},{24,8},{1,17},{9,25},{17,1},{25,9},{2,18},{10... | collective-permute-start | bytes 1916936 | tf_op jit(solution)/shard_map/ppermute | solution.py:1194
  480.5 36.7 %collective-permute-start.12 = (bf16[416,768]{1,0:T(8,128)(2,1)}, bf16[416,768]{1,0:T(8,128)(2,1)}, u32[]{:S(2)}, u32[]{:S(2)}) collective-permute-start(bf16[416,768]{1,0:T(8,128)(2,1)} %slice.216), channel_id=1, source_target_pairs={{0,8},{8,0},{16,24},{24,16},{1,9},{9,1},{17,25},{25,17},{2,10},{10... | collective-permute-start | bytes 1916936 | tf_op jit(solution)/shard_map/ppermute | solution.py:1194
  481.4 40.9 %collective-permute-start.14 = (bf16[768,768]{1,0:T(8,128)(2,1)}, bf16[768,768]{1,0:T(8,128)(2,1)}, u32[]{:S(2)}, u32[]{:S(2)}) collective-permute-start(bf16[768,768]{1,0:T(8,128)(2,1)} %get-tuple-element.122), channel_id=1, source_target_pairs={{0,16},{8,24},{16,0},{24,8},{1,17},{9,25},{17,1},{25,9},{2,18},{10... | collective-permute-start | bytes 3538952 | tf_op jit(solution)/shard_map/ppermute | solution.py:1194
  487.7 34.7 %collective-permute-start.16 = (bf16[768,768]{1,0:T(8,128)(2,1)}, bf16[768,768]{1,0:T(8,128)(2,1)}, u32[]{:S(2)}, u32[]{:S(2)}) collective-permute-start(bf16[768,768]{1,0:T(8,128)(2,1)} %fusion.24), channel_id=1, source_target_pairs={{0,8},{8,0},{16,24},{24,16},{1,9},{9,1},{17,25},{25,17},{2,10},{10... | collective-permute-start | bytes 3538952 | tf_op jit(solution)/shard_map/ppermute | solution.py:1194
  530.9 48.0 %collective-permute-start.17 = (bf16[784,768]{1,0:T(8,128)(2,1)}, bf16[784,768]{1,0:T(8,128)(2,1)S(1)}, u32[]{:S(2)}, u32[]{:S(2)}) collective-permute-start(bf16[784,768]{1,0:T(8,128)(2,1)} %reshape.420), channel_id=1, source_target_pairs={{0,8},{8,0},{16,24},{24,16},{1,9},{9,1},{17,25},{25,17},{2,10},{10... | collective-permute-start | bytes 3612680 | tf_op jit(solution)/shard_map/ppermute | solution.py:1194
  531.9 49.2 %collective-permute-start.18 = (bf16[784,768]{1,0:T(8,128)(2,1)}, bf16[784,768]{1,0:T(8,128)(2,1)}, u32[]{:S(2)}, u32[]{:S(2)}) collective-permute-start(bf16[784,768]{1,0:T(8,128)(2,1)} %reshape.420), channel_id=1, source_target_pairs={{0,16},{8,24},{16,0},{24,8},{1,17},{9,25},{17,1},{25,9},{2,18},{10... | collective-permute-start | bytes 3612680 | tf_op jit(solution)/shard_map/ppermute | solution.py:1194
  536.4 213.2 %collective-permute-start.19 = (bf16[768,768]{1,0:T(8,128)(2,1)}, bf16[768,768]{1,0:T(8,128)(2,1)}, u32[]{:S(2)}, u32[]{:S(2)}) collective-permute-start(bf16[768,768]{1,0:T(8,128)(2,1)} %broadcast_select_fusion.1), channel_id=1, source_target_pairs={{0,1},{1,0},{2,3},{3,2},{4,5},{5,4},{6,7},{7,6},{8,9},{9,8},{10,11... | collective-permute-start | bytes 3538952 | tf_op jit(solution)/shard_map/ppermute | solution.py:1194
  749.5 18.0 %slice-start.2 = ((s8[4816896]{0:T(1024)(128)(4,1)}), s8[4194304]{0:T(1024)(128)(4,1)S(1)}, s32[]{:S(2)}) async-start(s8[4816896]{0:T(1024)(128)(4,1)} %bitcast.113), calls=%async_computation.5 | async-start | bytes 8388608
  754.9 12.6 %slice-start.3 = ((s8[4816896]{0:T(1024)(128)(4,1)}), s8[622592]{0:T(1024)(128)(4,1)S(1)}, s32[]{:S(2)}) async-start(s8[4816896]{0:T(1024)(128)(4,1)} %bitcast.113), calls=%async_computation.6 | async-start | bytes 1245184
  759.8 7.7 %copy-start.9 = (bf16[784,768]{1,0:T(8,128)(2,1)S(1)}, bf16[784,768]{1,0:T(8,128)(2,1)}, u32[]{:S(2)}) copy-start(bf16[784,768]{1,0:T(8,128)(2,1)} %copy-done.8) | copy-start | bytes 3612676
  762.4 6.7 copy-start.17
  (55 other events, 165.4 us)

commit v3 on v2

--- a/solution.py
+++ b/solution.py
@@ -410,12 +410,20 @@
     hid_ref,
     du_ref,
     sent_ref,
+    y_ref,
     dw_ref,
     out_ref,
+    y_out,
+    stage_ref,
+    came_ref,
     swap_send,
     swap_recv,
     pass_send,
     pass_recv,
+    y_send,
+    y_recv,
+    core_send,
+    core_recv,
     local_sem,
 ):
     step = pl.program_id(0)
@@ -442,7 +450,26 @@
         )
 
     def keep():
-        return pltpu.make_async_copy(sent_ref.at[place], out_ref.at[0, place], local_sem)
+        return pltpu.make_async_copy(sent_ref.at[place], out_ref.at[0, place], local_sem.at[0])
+
+    def y_exchange(k):
+        peer = place ^ k
+        return remote(y_ref.at[peer], y_out.at[place], y_send, y_recv, k, {"ep": peer})
+
+    def y_keep():
+        return pltpu.make_async_copy(y_ref.at[place], y_out.at[place], local_sem.at[1])
+
+    core = lax.rem(place, 2)
+    own_half = pl.ds(pl.multiple_of(core * depth, depth), depth)
+    other_half = pl.ds(pl.multiple_of((1 - core) * depth, depth), depth)
+
+    def give(r):
+        return remote(
+            stage_ref.at[r, other_half], came_ref.at[r], core_send, core_recv, r, {"ep": place ^ 1}
+        )
+
+    def save(r):
+        return pltpu.make_async_copy(stage_ref.at[r, own_half], dw_ref.at[r], local_sem.at[2 + r])
 
     def along(k, way):
         slab = place ^ k
@@ -492,15 +519,37 @@
         def _(group=group):
             forward(group)
 
-    dw_ref[0, depth:, :] = dot(hid_ref[0], dy_ref[...], TN).astype(BF)
-    dw_ref[0, :depth, :] = dot(x_ref[...], du_ref[0], TN).astype(BF)
+    @pl.when(step == 2)
+    def _():
+        y_keep().start()
+        for k in range(1, size):
+            y_exchange(k).start()
+
+    stage_ref[step, depth:, :] = dot(hid_ref[0], dy_ref[...], TN).astype(BF)
+    stage_ref[step, :depth, :] = dot(x_ref[...], du_ref[0], TN).astype(BF)
+    for r in range(stage_ref.shape[0]):
+
+        @pl.when(step == r)
+        def _(r=r):
+            give(r).start()
 
     @pl.when(step == 3)
     def _():
         forward(3)
+        for r in range(stage_ref.shape[0]):
+            give(r).wait_recv()
+            add_rows(stage_ref.at[r, own_half], came_ref.at[r], depth)
+            save(r).start()
         for k in range(size):
             along(k, k % 2).wait_recv()
             relay(k).start()
+        y_keep().wait()
+        for k in range(1, size):
+            y_exchange(k).wait_recv()
+            y_exchange(k).wait_send()
+        for r in range(stage_ref.shape[0]):
+            give(r).wait_send()
+            save(r).wait()
         for k in range(size):
             along(k, 1 - k % 2).wait_recv()
             relay(k).wait_recv()
@@ -512,7 +561,7 @@
             relay(k).wait_send()
 
 
-def expert_return(x, dy, hid, du, sent):
+def expert_return(x, dy, hid, du, sent, y):
     rows, depth = x.shape
     shards, _, hidden = hid.shape
     size = sent.shape[0]
@@ -522,18 +571,25 @@
     return pl.pallas_call(
         lambda *refs: expert_return_kernel(size, *refs),
         grid=(shards,),
-        in_specs=[whole(), whole(), wide, wide, any_spec],
-        out_specs=[pl.BlockSpec((1, 2 * depth, hidden), shard), any_spec],
+        in_specs=[whole(), whole(), wide, wide, any_spec, any_spec],
+        out_specs=[any_spec] * 3,
         out_shape=[
-            jax.ShapeDtypeStruct((shards, 2 * depth, hidden), BF),
+            jax.ShapeDtypeStruct((shards, depth, hidden), BF),
             jax.ShapeDtypeStruct((shards,) + sent.shape, BF),
+            jax.ShapeDtypeStruct(y.shape, BF),
         ],
         scratch_shapes=[
+            pltpu.VMEM((shards, 2 * depth, hidden), BF),
+            pltpu.VMEM((shards, depth, hidden), BF),
             pltpu.SemaphoreType.DMA((size,)),
             pltpu.SemaphoreType.DMA((size,)),
             pltpu.SemaphoreType.DMA((3, size)),
             pltpu.SemaphoreType.DMA((3, size)),
-            pltpu.SemaphoreType.DMA,
+            pltpu.SemaphoreType.DMA((size,)),
+            pltpu.SemaphoreType.DMA((size,)),
+            pltpu.SemaphoreType.DMA((shards,)),
+            pltpu.SemaphoreType.DMA((shards,)),
+            pltpu.SemaphoreType.DMA((2 + shards,)),
         ],
         compiler_params=pltpu.CompilerParams(
             dimension_semantics=("arbitrary",),
@@ -547,7 +603,7 @@
             transcendentals=0,
         ),
         name="expert_return",
-    )(x, dy, hid, du, sent)
+    )(x, dy, hid, du, sent, y)
 
 
 ROUTES = 6
@@ -710,11 +766,11 @@
         one[2].start()
         one[3].start()
         one[4].start()
+        feed[0].start()
+        feed[1].start()
         one[2].wait_recv()
         one[3].wait_recv()
         one[5].start()
-        feed[0].start()
-        feed[1].start()
         own_local[1].start()
         own_local[2].start()
         own_local[0].wait()
@@ -927,7 +983,7 @@
     return (h1, h2, h3), (q1, l1, c1), (hid, slope), (q2, l2, c2), (w1, wf, w2), normed, biases
 
 
-TAIL_ORDER = (0, 1, 2, 3, 0, 1, 0, 2, 0, 1, 3, 0, 1, 2, 4, 0, 3, 1, 2, 0, 3, 1, 2, 4, 0, 3, 1, 2, 4)
+TAIL_ORDER = (0, 3, 0, 1, 3, 0, 1, 2, 0, 3, 0, 2, 0, 0, 1, 3, 0, 2, 1, 2, 4, 0, 1, 2, 3, 1, 2, 4, 1, 2, 3, 1, 2, 4)
 
 
 def add_rows(dst, src, rows):
@@ -1282,7 +1338,7 @@
             flops=4 * rows * rows * 128, bytes_accessed=4_000_000, transcendentals=0
         ),
         name="route",
-    )(order.reshape(1, rows), index, hot)
+    )(order.reshape(1, rows), after(index, hot), hot)
     return out[:, :2].astype(jnp.int32)
 
 
@@ -1493,18 +1549,22 @@
         expert_input(outputs, cot_rows, gate_in, exp_mine, exp_other, exp_slope)
     )
     sent = jnp.concatenate([grad_inputs, two_parts(slot_dot)], axis=1)
-    g_exp, grad_slots = expert_return(
-        inputs, grad_outputs, exp_hidden, exp_du, sent.reshape(experts, part, sent.shape[1])
-    )
+    part_exp, grad_slots, weighted = expert_return(
+        inputs,
+        grad_outputs,
+        exp_hidden,
+        exp_du,
+        sent.reshape(experts, part, sent.shape[1]),
+        weighted.reshape(experts, part, depth),
+    )
+    weighted = weighted.reshape(experts * part, depth)
     grad_slots = grad_slots.reshape(shards * experts * part, sent.shape[1])
-    part_exp = core_sum(g_exp)
     exp_from_y = hop(part_exp[3], "tp", 2)
     dot_slots = grad_slots[:, depth : depth + 2].astype(F32)
     dot_slots = dot_slots[:, 0] + dot_slots[:, 1]
-    weighted = swap_rows(after(weighted, grad_slots))
     grad_slots = grad_slots[:, :depth]
 
-    grad_stream = pad_images(own_rows(cotangent)).astype(F32)
+    grad_stream = pad_images(own_rows(after(cotangent, cot_sent))).astype(F32)
     own_gates = gates[:own_pad]
     hot_dots = jnp.where(back_hot, dot_slots[None, :], 0.0).reshape(
         own_pad, 2, 2, experts // 2, 2 * part

time: 777 us -> 760 us (0.978)
  waiting for transfers between devices: 45.3 us -> 31.8 us
    all_to_all x3 -> x2, waiting for transfers between devices: 22.5 us -> 2.3 us  [swap_ep(): return lax.all_to_all(value, 'ep', split_axis=0, concat_axis=0, tiled=True)]
    ppermute x20 -> x19, waiting for transfers between devices: 22.7 us -> 29.5 us  [hop(): return lax.ppermute(value, axis, [(i, i ^ bit) for i in range(size)])]
  transfers between devices with their start and end apart: 23 -> 21, of which waited for: 5 -> 5; matrix products, arithmetic and copies ran while one was open for 15% -> 13% of each run, Pallas kernels for 37% -> 38%
where the time goes in v3:
time: 760 us; the launch traced here: 754 us
  Pallas kernels  524 us (69%)
  other arithmetic  74.8 us (10%)
  local copies, waits for them, and re-layouts  56.4 us (7%)
  matrix products  40.1 us (5%)
  waiting for transfers between devices  31.8 us (4%)
  starting transfers between devices  23.9 us (3%)
    pallas_call x1, Pallas kernels, tail(): pl.pallas_call(lambda *refs: tail_kernel(size, rows_list, *refs), in_spec...  167 us
    pallas_call x1, Pallas kernels, dense_forward(): pl.pallas_call(forward_kernel, grid=(3 * images,), in_specs=[whole(), who...  143 us
    pallas_call x2, Pallas kernels, attend_backward(): pl.pallas_call(attend_backward_kernel, grid=(images,), in_specs=[row_bloc...  71.2 us
    pallas_call x1, Pallas kernels, expert_return(): pl.pallas_call(lambda *refs: expert_return_kernel(size, *refs), grid=(sha...  63.2 us
    dot_general x7, matrix products, dot(): return lax.dot_general(a, b, (dims, ((), ())), preferred_element_type=F32)  40.1 us
    ppermute x19, waiting for transfers between devices, hop(): return lax.ppermute(value, axis, [(i, i ^ bit) for i in range(size)])  29.5 us
    pallas_call x1, Pallas kernels, feed_backward(): pl.pallas_call(feed_backward_kernel, grid=(shards,), in_specs=[whole(), w...  28.5 us
    pallas_call x1, Pallas kernels, expert_forward(): pl.pallas_call(expert_forward_kernel, grid=(shards,), in_specs=[whole(),...  21.1 us
  transfers between devices with their start and end apart: 21, of which 5 were waited for; matrix products, arithmetic and copies ran while one was open for 13% of the time, Pallas kernels for 38%

profile of v3, /device:TPU:0, one launch (start us, length us, event | category | flops | bytes accessed | tf_op | source)
XLA Modules:
  0.0 753.6 jit_solution(17561068046697245654)
XLA Ops:
  15.6 3.1 pad_maximum_fusion.4
  18.9 3.0 pad_maximum_fusion.2.feed_ref
  21.9 2.8 select_convert_fusion.index_ref
  24.8 3.0 bitcast_select_fusion
  27.8 143.3 %dense_forward.1 = (f32[832,768]{1,0:T(8,128)}, f32[832,768]{1,0:T(8,128)}, f32[832,768]{1,0:T(8,128)}, bf16[4,4,576,208]{3,2,1,0:T(8,128)(2,1)}, f32[4,4,3,208]...) custom-call(bf16[832,768]{1,0:T(8,128)(2,1)} %bitcast.108, ...), custom_call_target="tpu_custom_call" | custom-call | flops 60000002048 | bytes 60000000 | tf_op jit(solution)/shard_map/dense_forward/pallas_call | solution.py:936
  175.8 13.8 %route.1 = f32[3136,128]{1,0:T(8,128)} custom-call(s32[1,3136]{1,0:T(1,128)} %order_ref.1, bf16[3136,128]{1,0:T(8,128)(2,1)} %select_convert_fusion.index_ref, bf16[3136,128]{1,0:T(8,128)(2,1)} %add_convert_fusion.1.hot_ref), custom_call_target="tpu_custom_call" | custom-call | flops 5035261952 | bytes 4000000 | tf_op jit(solution)/shard_map/route/pallas_call | solution.py:1330
  198.8 3.9 or_convert_fusion
  202.7 8.4 %fusion.27 = bf16[832,768]{1,0:T(8,128)(2,1)} fusion(bf16[3328,768]{1,0:T(8,128)(2,1)} %bitcast.102, s32[3328]{0:T(1024)S(1)} %get-tuple-element.178, s32[3328]{0:T(1024)S(1)} %get-tuple-element.177, s32[832]{0:T(1024)S(1)} %get-tuple-element.221), kind=kOutput, calls=%fused_computation.52 | convolution fusion | flops 4261969920 | bytes 6419712 | tf_op jit(solution)/shard_map/dot_general | solution.py:22
  215.2 2.9 maximum_maximum_fusion
  218.1 4.9 all-to-all-start
  223.2 9.4 %convolution_convert_fusion = bf16[832,768]{1,0:T(8,128)(2,1)} fusion(bf16[832,3136]{1,0:T(8,128)(2,1)} %or_convert_fusion, bf16[3136,768]{1,0:T(8,128)(2,1)} %param.31), kind=kOutput, calls=%fused_computation.53 | convolution fusion | flops 4008296448 | bytes 11313152 | tf_op jit(solution)/shard_map/dot_general | solution.py:22
  235.6 9.6 %collective-permute-done.2 = bf16[768,768]{1,0:T(8,128)(2,1)} collective-permute-done((bf16[768,768]{1,0:T(8,128)(2,1)}, bf16[768,768]{1,0:T(8,128)(2,1)}, u32[]{:S(2)}, u32[]{:S(2)}) %collective-permute-start.2) | collective-permute-done | bytes 1179680 | tf_op jit(solution)/shard_map/ppermute | solution.py:1250
  254.9 4.1 pad_maximum_fusion.mine_ref
  259.2 5.0 all-to-all-start.1
  264.3 4.0 pad_maximum_fusion.1.other_ref
  272.6 21.1 %expert_forward.1 = (bf16[832,768]{1,0:T(8,128)(2,1)}, bf16[4,832,768]{2,1,0:T(8,128)(2,1)}, bf16[4,832,768]{2,1,0:T(8,128)(2,1)}) custom-call(bf16[832,768]{1,0:T(8,128)(2,1)} %slice.252.x_ref.refs_0_, bf16[4,768,768]{2,1,0:T(8,128)(2,1)} %pad_maximum_fusion.mine_ref, bf16[4,768,768]{2,1,0:T(8,128)(2,1)} %pad_maximum_fusion.1.other_ref, ...), custom_call_target="tpu_custom_call" | custom-call | flops 15703474176 | bytes 25000000 | tf_op jit(solution)/shard_map/expert_forward/pallas_call | solution.py:305
  295.8 16.5 %expert_input.1 = (bf16[832,768]{1,0:T(8,128)(2,1)}, bf16[832,768]{1,0:T(8,128)(2,1)}, bf16[832,768]{1,0:T(8,128)(2,1)}, f32[832,1]{1,0:T(8,128)}, bf16[4,832,768]{2,1,0:T(8,128)(2,1)}, /*index=5*/f32[8,768]{1,0:T(8,128)}) custom-call(bf16[832,768]{1,0:T(8,128)(2,1)} %get-tuple-element.105.y_ref, bf16[832,768]{1,0:T(8,128)(2,1)} %bitcast.27.cot_ref, ...), custom_call_target="tpu_custom_call" | custom-call | flops 15703474176 | bytes 25000000 | tf_op jit(solution)/shard_map/expert_input/pallas_call | solution.py:375
  313.4 2.8 maximum_maximum_fusion.1
  316.2 63.2 %expert_return.1 = (bf16[4,768,768]{2,1,0:T(8,128)(2,1)}, bf16[4,8,104,896]{3,2,1,0:T(8,128)(2,1)}, bf16[8,104,768]{2,1,0:T(8,128)(2,1)}) custom-call(bf16[832,768]{1,0:T(8,128)(2,1)} %slice.252.x_ref.refs_0_, bf16[832,768]{1,0:T(8,128)(2,1)} %get-tuple-element.107.refs_1_, bf16[4,832,768]{2,1,0:T(8,128)(2,1)} %get-tuple-element.108.refs_2_, ...), custom_call_target="tpu_custom_call" | custom-call | flops 15703474176 | bytes 40000000 | tf_op jit(solution)/shard_map/expert_return/pallas_call | solution.py:571
  382.5 8.8 %fusion.5 = f32[832,768]{1,0:T(8,128)} fusion(s32[3328]{0:T(1024)S(1)} %copy-done.27, s32[832]{0:T(1024)} %get-tuple-element.182, s32[832]{0:T(1024)S(1)} %copy-done.32, bf16[3328,896]{1,0:T(8,128)(2,1)} %bitcast.125), kind=kOutput, calls=%fused_computation.9 | convolution fusion | flops 4261330944 | bytes 7688448 | tf_op jit(solution)/shard_map/dot_general | solution.py:22
  393.5 3.3 multiply_reduce_fusion
  402.9 35.7 %attend_backward.2 = (f32[832,768]{1,0:T(8,128)}, bf16[4,768,768]{2,1,0:T(8,128)(2,1)}, f32[8,768]{1,0:T(8,128)}) custom-call(f32[832,768]{1,0:T(8,128)} %convert_add_fusion.g_ref, f32[832,768]{1,0:T(8,128)} %get-tuple-element.117.h_ref, f32[1,768]{1,0:T(1,128)} %copy-done.38, f32[1,768]{1,0:T(1,128)} %copy-done.39, ...), custom_call_target="tpu_custom_call" | custom-call | flops 26744979456 | bytes 30000000 | tf_op jit(solution)/shard_map/attend_backward/pallas_call | solution.py:153
  440.3 15.2 %collective-permute-done.14 = bf16[768,768]{1,0:T(8,128)(2,1)} collective-permute-done((bf16[768,768]{1,0:T(8,128)(2,1)}, bf16[768,768]{1,0:T(8,128)(2,1)}, u32[]{:S(2)}, u32[]{:S(2)}) %collective-permute-start.14) | collective-permute-done | bytes 1179680 | tf_op jit(solution)/shard_map/ppermute | solution.py:1250
  455.5 2.9 fusion.24
  464.7 28.5 %feed_backward.1 = (f32[832,768]{1,0:T(8,128)}, bf16[4,1536,768]{2,1,0:T(8,128)(2,1)}, f32[8,768]{1,0:T(8,128)}) custom-call(f32[832,768]{1,0:T(8,128)} %get-tuple-element.128.g_ref, f32[832,768]{1,0:T(8,128)} %get-tuple-element.129.h_ref, f32[1,768]{1,0:T(1,128)} %copy-done.36, f32[1,768]{1,0:T(1,128)} %copy-done.37, ...), custom_call_target="tpu_custom_call" | custom-call | flops 31406948352 | bytes 35000000 | tf_op jit(solution)/shard_map/feed_backward/pallas_call | solution.py:236
  493.3 4.7 collective-permute-done.12
  499.1 7.0 add_convert_fusion
  509.7 3.4 broadcast_select_fusion.1
  513.1 35.5 %attend_backward.3 = (f32[832,768]{1,0:T(8,128)}, bf16[4,768,768]{2,1,0:T(8,128)(2,1)}, f32[8,768]{1,0:T(8,128)}) custom-call(f32[832,768]{1,0:T(8,128)} %get-tuple-element.136.g_ref, f32[832,768]{1,0:T(8,128)} %convert_element_type.147.h_ref, f32[1,768]{1,0:T(1,128)} %copy-done.34, f32[1,768]{1,0:T(1,128)} %copy-done.35, ...), custom_call_target="tpu_custom_call" | custom-call | flops 26744979456 | bytes 30000000 | tf_op jit(solution)/shard_map/attend_backward/pallas_call | solution.py:153
  558.9 166.5 %tail.1 = (bf16[768,768]{1,0:T(8,128)(2,1)}, bf16[1536,768]{1,0:T(8,128)(2,1)}, bf16[768,768]{1,0:T(8,128)(2,1)}, bf16[4,784,768]{2,1,0:T(8,128)(2,1)}, bf16[784...) custom-call(bf16[4,768,768]{2,1,0:T(8,128)(2,1)} %get-tuple-element.122.refs_0_, ...), custom_call_target="tpu_custom_call" | custom-call | flops 30000000 | bytes 60000000 | tf_op jit(solution)/shard_map/tail/pallas_call | solution.py:1218
  731.2 5.4 bitcast_convert_fusion.1
  736.6 4.9 bitcast_convert_fusion
  (303 shorter events, 104.2 us)
Async XLA Ops:
  0.7 210.5 %copy-start = (bf16[768,8]{0,1:T(8,128)(2,1)S(1)}, bf16[768,8]{0,1:T(8,128)(2,1)}, u32[]{:S(2)}) copy-start(bf16[768,8]{0,1:T(8,128)(2,1)} %param.55) | copy-start | bytes 36868
  3.1 21.6 %collective-permute-start = (bf16[768,768]{1,0:T(8,128)(2,1)}, bf16[768,768]{1,0:T(8,128)(2,1)}, u32[]{:S(2)}, u32[]{:S(2)}) collective-permute-start(bf16[768,768]{1,0:T(8,128)(2,1)} %select_bitcast_fusion.1), channel_id=1, source_target_pairs={{0,1},{1,0},{2,3},{3,2},{4,5},{5,4},{6,7},{7,6},{8,9},{9,8},{10,11... | collective-permute-start | bytes 3538952 | tf_op jit(solution)/shard_map/ppermute | solution.py:1250
  27.8 143.3 %copy-start.22 = (s32[3136,2]{0,1:T(2,128)S(1)}, s32[3136,2]{0,1:T(2,128)}, u32[]{:S(2)}) copy-start(s32[3136,2]{0,1:T(2,128)} %param.32) | copy-start | bytes 75268
  193.1 42.5 %collective-permute-start.1 = (bf16[768,768]{1,0:T(8,128)(2,1)}, bf16[768,768]{1,0:T(8,128)(2,1)}, u32[]{:S(2)}, u32[]{:S(2)}) collective-permute-start(bf16[768,768]{1,0:T(8,128)(2,1)} %get-tuple-element.99), channel_id=1, source_target_pairs={{0,8},{8,0},{16,24},{24,16},{1,9},{9,1},{17,25},{25,17},{2,10},{10... | collective-permute-start | bytes 3538952 | tf_op jit(solution)/shard_map/ppermute | solution.py:1250
  194.2 51.0 %collective-permute-start.3 = (bf16[768,768]{1,0:T(8,128)(2,1)}, bf16[768,768]{1,0:T(8,128)(2,1)}, u32[]{:S(2)}, u32[]{:S(2)}) collective-permute-start(bf16[768,768]{1,0:T(8,128)(2,1)} %get-tuple-element.99), channel_id=1, source_target_pairs={{0,24},{8,16},{16,8},{24,0},{1,25},{9,17},{17,9},{25,1},{2,26},{10... | collective-permute-start | bytes 3538952 | tf_op jit(solution)/shard_map/ppermute | solution.py:1250
  195.7 49.6 %collective-permute-start.2 = (bf16[768,768]{1,0:T(8,128)(2,1)}, bf16[768,768]{1,0:T(8,128)(2,1)}, u32[]{:S(2)}, u32[]{:S(2)}) collective-permute-start(bf16[768,768]{1,0:T(8,128)(2,1)} %get-tuple-element.98), channel_id=1, source_target_pairs={{0,16},{8,24},{16,0},{24,8},{1,17},{9,25},{17,1},{25,9},{2,18},{10... | collective-permute-start | bytes 3538952 | tf_op jit(solution)/shard_map/ppermute | solution.py:1250
  196.7 67.5 %collective-permute-start.4 = (bf16[768,768]{1,0:T(8,128)(2,1)}, bf16[768,768]{1,0:T(8,128)(2,1)}, u32[]{:S(2)}, u32[]{:S(2)}) collective-permute-start(bf16[768,768]{1,0:T(8,128)(2,1)} %get-tuple-element.98), channel_id=1, source_target_pairs={{0,1},{1,0},{2,3},{3,2},{4,5},{5,4},{6,7},{7,6},{8,9},{9,8},{10,11... | collective-permute-start | bytes 3538952 | tf_op jit(solution)/shard_map/ppermute | solution.py:1250
  197.6 55.2 %collective-permute-start.8 = (f32[4,2,768]{2,1,0:T(2,128)S(1)}, f32[4,2,768]{2,1,0:T(2,128)S(1)}, u32[]{:S(2)}, u32[]{:S(2)}) collective-permute-start(f32[4,2,768]{2,1,0:T(2,128)S(1)} %slice.204), channel_id=1, source_target_pairs={{0,1},{1,0},{2,3},{3,2},{4,5},{5,4},{6,7},{7,6},{8,9},{9,8},{10,11... | collective-permute-start | bytes 73736 | tf_op jit(solution)/shard_map/ppermute | solution.py:1250
  198.8 12.3 %slice-start = ((s8[5111808]{0:T(1024)(128)(4,1)}), s8[4194304]{0:T(1024)(128)(4,1)S(1)}, s32[]{:S(2)}) async-start(s8[5111808]{0:T(1024)(128)(4,1)} %bitcast.103), calls=%async_computation.2 | async-start | bytes 8388608
  202.7 8.4 %slice-start.1 = ((s8[5111808]{0:T(1024)(128)(4,1)}), s8[917504]{0:T(1024)(128)(4,1)S(1)}, s32[]{:S(2)}) async-start(s8[5111808]{0:T(1024)(128)(4,1)} %bitcast.103), calls=%async_computation.3 | async-start | bytes 1835008
  215.2 7.8 %copy-start.2 = (f32[832,768]{1,0:T(8,128)S(1)}, f32[832,768]{1,0:T(8,128)}, u32[]{:S(2)}) copy-start(f32[832,768]{1,0:T(8,128)} %get-tuple-element.94) | copy-start | bytes 7667716
  218.1 41.1 %all-to-all-start = ((bf16[8,104,896]{2,1,0:T(8,128)(2,1)}), bf16[8,104,896]{2,1,0:T(8,128)(2,1)}, u32[]{:S(2)}, u32[]{:S(2)}) async-start(bf16[8,104,896]{2,1,0:T(8,128)(2,1)} %maximum_maximum_fusion), calls=%async_computation | async-start | bytes 2981888 | tf_op jit(solution)/shard_map/all_to_all | solution.py:1293
  232.7 13.8 %copy-start.4 = (bf16[4,208,768]{2,1,0:T(8,128)(2,1)S(1)}, bf16[4,208,768]{2,1,0:T(8,128)(2,1)}, u32[]{:S(2)}) copy-start(bf16[4,208,768]{2,1,0:T(8,128)(2,1)} %pad.27) | copy-start | bytes 3833860
  245.3 18.9 %collective-permute-start.5 = (bf16[768,768]{1,0:T(8,128)(2,1)}, bf16[768,768]{1,0:T(8,128)(2,1)}, u32[]{:S(2)}, u32[]{:S(2)}) collective-permute-start(bf16[768,768]{1,0:T(8,128)(2,1)} %collective-permute-done.1), channel_id=1, source_target_pairs={{0,1},{1,0},{2,3},{3,2},{4,5},{5,4},{6,7},{7,6},{8,9},{9,8},{10,11... | collective-permute-start | bytes 3538952 | tf_op jit(solution)/shard_map/ppermute | solution.py:1250
  245.3 18.9 %collective-permute-start.6 = (bf16[768,768]{1,0:T(8,128)(2,1)}, bf16[768,768]{1,0:T(8,128)(2,1)}, u32[]{:S(2)}, u32[]{:S(2)}) collective-permute-start(bf16[768,768]{1,0:T(8,128)(2,1)} %collective-permute-done.2), channel_id=1, source_target_pairs={{0,1},{1,0},{2,3},{3,2},{4,5},{5,4},{6,7},{7,6},{8,9},{9,8},{10,11... | collective-permute-start | bytes 3538952 | tf_op jit(solution)/shard_map/ppermute | solution.py:1250
  245.8 18.4 %collective-permute-start.7 = (bf16[768,768]{1,0:T(8,128)(2,1)}, bf16[768,768]{1,0:T(8,128)(2,1)}, u32[]{:S(2)}, u32[]{:S(2)}) collective-permute-start(bf16[768,768]{1,0:T(8,128)(2,1)} %collective-permute-done.3), channel_id=1, source_target_pairs={{0,1},{1,0},{2,3},{3,2},{4,5},{5,4},{6,7},{7,6},{8,9},{9,8},{10,11... | collective-permute-start | bytes 3538952 | tf_op jit(solution)/shard_map/ppermute | solution.py:1250
  259.2 36.6 %all-to-all-start.1 = ((bf16[8,104,768]{2,1,0:T(8,128)(2,1)}), bf16[8,104,768]{2,1,0:T(8,128)(2,1)}, u32[]{:S(2)}, u32[]{:S(2)}) async-start(bf16[8,104,768]{2,1,0:T(8,128)(2,1)} %bitcast.118), calls=%async_computation.1 | async-start | bytes 2555904 | tf_op jit(solution)/shard_map/all_to_all | solution.py:1293
  382.5 8.9 %copy-start.24 = (s32[2,2,4,208]{3,2,1,0:T(4,128)S(1)}, s32[2,2,4,208]{3,2,1,0:T(4,128)}, u32[]{:S(2)}) copy-start(s32[2,2,4,208]{3,2,1,0:T(4,128)} %eq.238) | copy-start | bytes 39940
  382.5 8.8 %copy-start.33 = (s32[832]{0:T(1024)S(1)}, s32[832]{0:T(1024)}, u32[]{:S(2)}) copy-start(s32[832]{0:T(1024)} %get-tuple-element.182) | copy-start | bytes 9988
  382.5 11.0 %copy-start.29 = (f32[768]{0:T(1024)S(1)}, f32[768]{0:T(1024)}, u32[]{:S(2)}) copy-start(f32[768]{0:T(1024)} %param.53) | copy-start | bytes 9220
  398.9 59.9 %collective-permute-start.10 = (bf16[832,768]{1,0:T(8,128)(2,1)}, bf16[832,768]{1,0:T(8,128)(2,1)}, u32[]{:S(2)}, u32[]{:S(2)}) collective-permute-start(bf16[832,768]{1,0:T(8,128)(2,1)} %bitcast.30), channel_id=1, source_target_pairs={{0,16},{8,24},{16,0},{24,8},{1,17},{9,25},{17,1},{25,9},{2,18},{10... | collective-permute-start | bytes 3833864 | tf_op jit(solution)/shard_map/ppermute | solution.py:1250
  399.3 59.5 %collective-permute-start.9 = (bf16[832,768]{1,0:T(8,128)(2,1)}, bf16[832,768]{1,0:T(8,128)(2,1)}, u32[]{:S(2)}, u32[]{:S(2)}) collective-permute-start(bf16[832,768]{1,0:T(8,128)(2,1)} %bitcast.30), channel_id=1, source_target_pairs={{0,8},{8,0},{16,24},{24,16},{1,9},{9,1},{17,25},{25,17},{2,10},{10... | collective-permute-start | bytes 3833864 | tf_op jit(solution)/shard_map/ppermute | solution.py:1250
  402.5 53.0 %collective-permute-start.14 = (bf16[768,768]{1,0:T(8,128)(2,1)}, bf16[768,768]{1,0:T(8,128)(2,1)}, u32[]{:S(2)}, u32[]{:S(2)}) collective-permute-start(bf16[768,768]{1,0:T(8,128)(2,1)} %get-tuple-element.185), channel_id=1, source_target_pairs={{0,16},{8,24},{16,0},{24,8},{1,17},{9,25},{17,1},{25,9},{2,18},{10... | collective-permute-start | bytes 3538952 | tf_op jit(solution)/shard_map/ppermute | solution.py:1250
  438.5 60.5 %collective-permute-start.13 = (bf16[768,768]{1,0:T(8,128)(2,1)}, bf16[768,768]{1,0:T(8,128)(2,1)}, u32[]{:S(2)}, u32[]{:S(2)}) collective-permute-start(bf16[768,768]{1,0:T(8,128)(2,1)} %get-tuple-element.126), channel_id=1, source_target_pairs={{0,16},{8,24},{16,0},{24,8},{1,17},{9,25},{17,1},{25,9},{2,18},{10... | collective-permute-start | bytes 3538952 | tf_op jit(solution)/shard_map/ppermute | solution.py:1250
  458.4 40.7 %collective-permute-start.15 = (bf16[768,768]{1,0:T(8,128)(2,1)}, bf16[768,768]{1,0:T(8,128)(2,1)}, u32[]{:S(2)}, u32[]{:S(2)}) collective-permute-start(bf16[768,768]{1,0:T(8,128)(2,1)} %fusion.24), channel_id=1, source_target_pairs={{0,8},{8,0},{16,24},{24,16},{1,9},{9,1},{17,25},{25,17},{2,10},{10... | collective-permute-start | bytes 3538952 | tf_op jit(solution)/shard_map/ppermute | solution.py:1250
  460.7 32.5 %collective-permute-start.11 = (bf16[416,768]{1,0:T(8,128)(2,1)}, bf16[416,768]{1,0:T(8,128)(2,1)S(1)}, u32[]{:S(2)}, u32[]{:S(2)}) collective-permute-start(bf16[416,768]{1,0:T(8,128)(2,1)} %slice.215), channel_id=1, source_target_pairs={{0,16},{8,24},{16,0},{24,8},{1,17},{9,25},{17,1},{25,9},{2,18},{10... | collective-permute-start | bytes 1916936 | tf_op jit(solution)/shard_map/ppermute | solution.py:1250
  464.4 33.5 %collective-permute-start.12 = (bf16[416,768]{1,0:T(8,128)(2,1)}, bf16[416,768]{1,0:T(8,128)(2,1)}, u32[]{:S(2)}, u32[]{:S(2)}) collective-permute-start(bf16[416,768]{1,0:T(8,128)(2,1)} %slice.216), channel_id=1, source_target_pairs={{0,8},{8,0},{16,24},{24,16},{1,9},{9,1},{17,25},{25,17},{2,10},{10... | collective-permute-start | bytes 1916936 | tf_op jit(solution)/shard_map/ppermute | solution.py:1250
  507.6 48.1 %collective-permute-start.16 = (bf16[784,768]{1,0:T(8,128)(2,1)}, bf16[784,768]{1,0:T(8,128)(2,1)S(1)}, u32[]{:S(2)}, u32[]{:S(2)}) collective-permute-start(bf16[784,768]{1,0:T(8,128)(2,1)} %reshape.420), channel_id=1, source_target_pairs={{0,8},{8,0},{16,24},{24,16},{1,9},{9,1},{17,25},{25,17},{2,10},{10... | collective-permute-start | bytes 3612680 | tf_op jit(solution)/shard_map/ppermute | solution.py:1250
  508.0 49.8 %collective-permute-start.17 = (bf16[784,768]{1,0:T(8,128)(2,1)}, bf16[784,768]{1,0:T(8,128)(2,1)}, u32[]{:S(2)}, u32[]{:S(2)}) collective-permute-start(bf16[784,768]{1,0:T(8,128)(2,1)} %reshape.420), channel_id=1, source_target_pairs={{0,16},{8,24},{16,0},{24,8},{1,17},{9,25},{17,1},{25,9},{2,18},{10... | collective-permute-start | bytes 3612680 | tf_op jit(solution)/shard_map/ppermute | solution.py:1250
  513.1 218.1 %collective-permute-start.18 = (bf16[768,768]{1,0:T(8,128)(2,1)}, bf16[768,768]{1,0:T(8,128)(2,1)}, u32[]{:S(2)}, u32[]{:S(2)}) collective-permute-start(bf16[768,768]{1,0:T(8,128)(2,1)} %broadcast_select_fusion.1), channel_id=1, source_target_pairs={{0,1},{1,0},{2,3},{3,2},{4,5},{5,4},{6,7},{7,6},{8,9},{9,8},{10,11... | collective-permute-start | bytes 3538952 | tf_op jit(solution)/shard_map/ppermute | solution.py:1250
  731.2 18.0 %slice-start.6 = ((s8[4816896]{0:T(1024)(128)(4,1)}), s8[4194304]{0:T(1024)(128)(4,1)S(1)}, s32[]{:S(2)}) async-start(s8[4816896]{0:T(1024)(128)(4,1)} %bitcast.113), calls=%async_computation.8 | async-start | bytes 8388608
  736.6 12.6 %slice-start.7 = ((s8[4816896]{0:T(1024)(128)(4,1)}), s8[622592]{0:T(1024)(128)(4,1)S(1)}, s32[]{:S(2)}) async-start(s8[4816896]{0:T(1024)(128)(4,1)} %bitcast.113), calls=%async_computation.9 | async-start | bytes 1245184
  (54 other events, 181.6 us)

commit v4 on v3

--- a/solution.py
+++ b/solution.py
@@ -983,7 +983,7 @@
     return (h1, h2, h3), (q1, l1, c1), (hid, slope), (q2, l2, c2), (w1, wf, w2), normed, biases
 
 
-TAIL_ORDER = (0, 3, 0, 1, 3, 0, 1, 2, 0, 3, 0, 2, 0, 0, 1, 3, 0, 2, 1, 2, 4, 0, 1, 2, 3, 1, 2, 4, 1, 2, 3, 1, 2, 4)
+TAIL_ORDER = (0, 3, 0, 1, 1, 0, 2, 3, 0, 1, 0, 2, 1, 3, 0, 2, 0, 1, 2, 4, 0, 1, 2, 3, 1, 2, 4, 1, 2, 0, 3, 1, 2, 4)
 
 
 def add_rows(dst, src, rows):
@@ -1581,16 +1581,16 @@
     g_route_bias = jnp.sum(grad_normed, axis=0)
     grad_stream = grad_stream + norm_back(hat, scale, route_norm_gain, grad_normed)
 
+    grad_stream, exp_from_y = lax.optimization_barrier((grad_stream, exp_from_y))
     near_weighted = near(after(weighted, grad_stream))
     grad_stream, g_two, small_two = attend_backward(
         grad_stream, level_two, row(sparse_norm_gain), row(sparse_norm_bias), w_two, kept_two
     )
     near_weighted = after(near_weighted, g_two)
     far_weighted = far(*near_weighted)
-    exp_from_y = after(exp_from_y, g_two)
     exp_from_y2 = hop(after(part_exp[2], g_two), "tp", 2)
     exp_give = plus(part_exp[1], exp_from_y)
-    exp_away = hop(exp_give, "tp", 1)
+    exp_away = hop(after(exp_give, g_two), "tp", 1)
     grad_stream, g_feed, small_feed = feed_backward(
         grad_stream, level_one, row(feed_norm_gain), row(feed_norm_bias), w_feed, kept_feed
     )

time: 760 us -> 754 us (level)
  Pallas kernels: 524 us -> 513 us
    pallas_call x1, Pallas kernels: 167 us -> 156 us  [tail(): pl.pallas_call(lambda *refs: tail_kernel(size, rows_list, *refs), in_spec...]
  transfers between devices with their start and end apart: 21 -> 21, of which waited for: 5 -> 5; matrix products, arithmetic and copies ran while one was open for 13% -> 14% of each run, Pallas kernels for 38% -> 37%
where the time goes in v4:
time: 754 us; the launch traced here: 750 us
  Pallas kernels  513 us (68%)
  other arithmetic  74.8 us (10%)
  local copies, waits for them, and re-layouts  57.7 us (8%)
  waiting for transfers between devices  39.4 us (5%)
  matrix products  38.3 us (5%)
  starting transfers between devices  23.8 us (3%)
    pallas_call x1, Pallas kernels, tail(): pl.pallas_call(lambda *refs: tail_kernel(size, rows_list, *refs), in_spec...  156 us
    pallas_call x1, Pallas kernels, dense_forward(): pl.pallas_call(forward_kernel, grid=(3 * images,), in_specs=[whole(), who...  143 us
    pallas_call x2, Pallas kernels, attend_backward(): pl.pallas_call(attend_backward_kernel, grid=(images,), in_specs=[row_bloc...  71.2 us
    pallas_call x1, Pallas kernels, expert_return(): pl.pallas_call(lambda *refs: expert_return_kernel(size, *refs), grid=(sha...  63.2 us
    dot_general x7, matrix products, dot(): return lax.dot_general(a, b, (dims, ((), ())), preferred_element_type=F32)  38.3 us
    ppermute x19, waiting for transfers between devices, hop(): return lax.ppermute(value, axis, [(i, i ^ bit) for i in range(size)])  37.1 us
    pallas_call x1, Pallas kernels, feed_backward(): pl.pallas_call(feed_backward_kernel, grid=(shards,), in_specs=[whole(), w...  28.5 us
    pallas_call x1, Pallas kernels, expert_forward(): pl.pallas_call(expert_forward_kernel, grid=(shards,), in_specs=[whole(),...  21.1 us
  transfers between devices with their start and end apart: 21, of which 5 were waited for; matrix products, arithmetic and copies ran while one was open for 14% of the time, Pallas kernels for 37%

profile of v4, /device:TPU:0, one launch (start us, length us, event | category | flops | bytes accessed | tf_op | source)
XLA Modules:
  0.0 749.7 jit_solution(6382005343824626074)
XLA Ops:
  15.6 3.1 pad_maximum_fusion.4
  18.9 3.0 pad_maximum_fusion.2.feed_ref
  21.9 2.8 select_convert_fusion.index_ref
  24.8 3.0 bitcast_select_fusion
  27.8 143.3 %dense_forward.1 = (f32[832,768]{1,0:T(8,128)}, f32[832,768]{1,0:T(8,128)}, f32[832,768]{1,0:T(8,128)}, bf16[4,4,576,208]{3,2,1,0:T(8,128)(2,1)}, f32[4,4,3,208]...) custom-call(bf16[832,768]{1,0:T(8,128)(2,1)} %bitcast.106, ...), custom_call_target="tpu_custom_call" | custom-call | flops 60000002048 | bytes 60000000 | tf_op jit(solution)/shard_map/dense_forward/pallas_call | solution.py:936
  175.9 13.7 %route.1 = f32[3136,128]{1,0:T(8,128)} custom-call(s32[1,3136]{1,0:T(1,128)} %order_ref.1, bf16[3136,128]{1,0:T(8,128)(2,1)} %select_convert_fusion.index_ref, bf16[3136,128]{1,0:T(8,128)(2,1)} %add_convert_fusion.1.hot_ref), custom_call_target="tpu_custom_call" | custom-call | flops 5035261952 | bytes 4000000 | tf_op jit(solution)/shard_map/route/pallas_call | solution.py:1330
  198.9 3.9 or_convert_fusion
  202.7 8.4 %fusion.27 = bf16[832,768]{1,0:T(8,128)(2,1)} fusion(bf16[3328,768]{1,0:T(8,128)(2,1)} %bitcast.102, s32[3328]{0:T(1024)S(1)} %get-tuple-element.182, s32[3328]{0:T(1024)S(1)} %get-tuple-element.181, s32[832]{0:T(1024)S(1)} %get-tuple-element.225), kind=kOutput, calls=%fused_computation.52 | convolution fusion | flops 4261969920 | bytes 6419712 | tf_op jit(solution)/shard_map/dot_general | solution.py:22
  215.2 2.9 maximum_maximum_fusion
  218.1 4.9 all-to-all-start
  223.2 9.4 %convolution_convert_fusion = bf16[832,768]{1,0:T(8,128)(2,1)} fusion(bf16[832,3136]{1,0:T(8,128)(2,1)} %or_convert_fusion, bf16[3136,768]{1,0:T(8,128)(2,1)} %param.31), kind=kOutput, calls=%fused_computation.53 | convolution fusion | flops 4008296448 | bytes 11313152 | tf_op jit(solution)/shard_map/dot_general | solution.py:22
  235.7 9.6 %collective-permute-done.2 = bf16[768,768]{1,0:T(8,128)(2,1)} collective-permute-done((bf16[768,768]{1,0:T(8,128)(2,1)}, bf16[768,768]{1,0:T(8,128)(2,1)}, u32[]{:S(2)}, u32[]{:S(2)}) %collective-permute-start.2) | collective-permute-done | bytes 1179680 | tf_op jit(solution)/shard_map/ppermute | solution.py:1250
  254.9 4.1 pad_maximum_fusion.mine_ref
  259.2 5.0 all-to-all-start.1
  264.3 4.0 pad_maximum_fusion.1.other_ref
  272.7 21.1 %expert_forward.1 = (bf16[832,768]{1,0:T(8,128)(2,1)}, bf16[4,832,768]{2,1,0:T(8,128)(2,1)}, bf16[4,832,768]{2,1,0:T(8,128)(2,1)}) custom-call(bf16[832,768]{1,0:T(8,128)(2,1)} %slice.252.x_ref.refs_0_, bf16[4,768,768]{2,1,0:T(8,128)(2,1)} %pad_maximum_fusion.mine_ref, bf16[4,768,768]{2,1,0:T(8,128)(2,1)} %pad_maximum_fusion.1.other_ref, ...), custom_call_target="tpu_custom_call" | custom-call | flops 15703474176 | bytes 25000000 | tf_op jit(solution)/shard_map/expert_forward/pallas_call | solution.py:305
  295.8 16.5 %expert_input.1 = (bf16[832,768]{1,0:T(8,128)(2,1)}, bf16[832,768]{1,0:T(8,128)(2,1)}, bf16[832,768]{1,0:T(8,128)(2,1)}, f32[832,1]{1,0:T(8,128)}, bf16[4,832,768]{2,1,0:T(8,128)(2,1)}, /*index=5*/f32[8,768]{1,0:T(8,128)}) custom-call(bf16[832,768]{1,0:T(8,128)(2,1)} %get-tuple-element.107.y_ref, bf16[832,768]{1,0:T(8,128)(2,1)} %bitcast.27.cot_ref, ...), custom_call_target="tpu_custom_call" | custom-call | flops 15703474176 | bytes 25000000 | tf_op jit(solution)/shard_map/expert_input/pallas_call | solution.py:375
  313.4 2.8 maximum_maximum_fusion.1
  316.2 63.2 %expert_return.1 = (bf16[4,768,768]{2,1,0:T(8,128)(2,1)}, bf16[4,8,104,896]{3,2,1,0:T(8,128)(2,1)}, bf16[8,104,768]{2,1,0:T(8,128)(2,1)}) custom-call(bf16[832,768]{1,0:T(8,128)(2,1)} %slice.252.x_ref.refs_0_, bf16[832,768]{1,0:T(8,128)(2,1)} %get-tuple-element.109.refs_1_, bf16[4,832,768]{2,1,0:T(8,128)(2,1)} %get-tuple-element.110.refs_2_, ...), custom_call_target="tpu_custom_call" | custom-call | flops 15703474176 | bytes 40000000 | tf_op jit(solution)/shard_map/expert_return/pallas_call | solution.py:571
  382.5 8.8 %fusion.5 = f32[832,768]{1,0:T(8,128)} fusion(s32[3328]{0:T(1024)S(1)} %copy-done.28, s32[832]{0:T(1024)} %get-tuple-element.186, s32[832]{0:T(1024)S(1)} %copy-done.33, bf16[3328,896]{1,0:T(8,128)(2,1)} %bitcast.123), kind=kOutput, calls=%fused_computation.9 | convolution fusion | flops 4261330944 | bytes 7688448 | tf_op jit(solution)/shard_map/dot_general | solution.py:22
  393.5 2.9 slice_bitcast_fusion
  400.5 23.7 %collective-permute-done.9 = bf16[768,768]{1,0:T(8,128)(2,1)} collective-permute-done((bf16[768,768]{1,0:T(8,128)(2,1)S(1)}, bf16[768,768]{1,0:T(8,128)(2,1)}, u32[]{:S(2)}, u32[]{:S(2)}) %collective-permute-start.9) | collective-permute-done | bytes 1179680 | tf_op jit(solution)/shard_map/ppermute | solution.py:1250
  426.2 35.7 %attend_backward.2 = (f32[832,768]{1,0:T(8,128)}, bf16[4,768,768]{2,1,0:T(8,128)(2,1)}, f32[8,768]{1,0:T(8,128)}) custom-call(f32[832,768]{1,0:T(8,128)} %convert_add_fusion.g_ref, f32[832,768]{1,0:T(8,128)} %get-tuple-element.121.h_ref, f32[1,768]{1,0:T(1,128)} %copy-done.39, f32[1,768]{1,0:T(1,128)} %copy-done.40, ...), custom_call_target="tpu_custom_call" | custom-call | flops 26744979456 | bytes 30000000 | tf_op jit(solution)/shard_map/attend_backward/pallas_call | solution.py:153
  461.9 2.9 fusion.24
  472.8 28.5 %feed_backward.1 = (f32[832,768]{1,0:T(8,128)}, bf16[4,1536,768]{2,1,0:T(8,128)(2,1)}, f32[8,768]{1,0:T(8,128)}) custom-call(f32[832,768]{1,0:T(8,128)} %get-tuple-element.132.g_ref, f32[832,768]{1,0:T(8,128)} %get-tuple-element.133.h_ref, f32[1,768]{1,0:T(1,128)} %copy-done.37, f32[1,768]{1,0:T(1,128)} %copy-done.38, ...), custom_call_target="tpu_custom_call" | custom-call | flops 31406948352 | bytes 35000000 | tf_op jit(solution)/shard_map/feed_backward/pallas_call | solution.py:236
  501.3 3.7 collective-permute-done.12
  506.2 7.0 add_convert_fusion
  516.8 3.4 broadcast_select_fusion.1
  520.2 35.5 %attend_backward.3 = (f32[832,768]{1,0:T(8,128)}, bf16[4,768,768]{2,1,0:T(8,128)(2,1)}, f32[8,768]{1,0:T(8,128)}) custom-call(f32[832,768]{1,0:T(8,128)} %get-tuple-element.140.g_ref, f32[832,768]{1,0:T(8,128)} %convert_element_type.147.h_ref, f32[1,768]{1,0:T(1,128)} %copy-done.35, f32[1,768]{1,0:T(1,128)} %copy-done.36, ...), custom_call_target="tpu_custom_call" | custom-call | flops 26744979456 | bytes 30000000 | tf_op jit(solution)/shard_map/attend_backward/pallas_call | solution.py:153
  565.9 155.6 %tail.1 = (bf16[768,768]{1,0:T(8,128)(2,1)}, bf16[1536,768]{1,0:T(8,128)(2,1)}, bf16[768,768]{1,0:T(8,128)(2,1)}, bf16[4,784,768]{2,1,0:T(8,128)(2,1)}, bf16[784...) custom-call(bf16[4,768,768]{2,1,0:T(8,128)(2,1)} %get-tuple-element.126.refs_0_, ...), custom_call_target="tpu_custom_call" | custom-call | flops 30000000 | bytes 60000000 | tf_op jit(solution)/shard_map/tail/pallas_call | solution.py:1218
  727.3 5.4 bitcast_convert_fusion.1
  732.7 4.9 bitcast_convert_fusion
  (300 shorter events, 104.1 us)
Async XLA Ops:
  0.7 210.5 %copy-start = (bf16[768,8]{0,1:T(8,128)(2,1)S(1)}, bf16[768,8]{0,1:T(8,128)(2,1)}, u32[]{:S(2)}) copy-start(bf16[768,8]{0,1:T(8,128)(2,1)} %param.55) | copy-start | bytes 36868
  3.1 21.6 %collective-permute-start = (bf16[768,768]{1,0:T(8,128)(2,1)}, bf16[768,768]{1,0:T(8,128)(2,1)}, u32[]{:S(2)}, u32[]{:S(2)}) collective-permute-start(bf16[768,768]{1,0:T(8,128)(2,1)} %select_bitcast_fusion.1), channel_id=1, source_target_pairs={{0,1},{1,0},{2,3},{3,2},{4,5},{5,4},{6,7},{7,6},{8,9},{9,8},{10,11... | collective-permute-start | bytes 3538952 | tf_op jit(solution)/shard_map/ppermute | solution.py:1250
  27.8 143.3 %copy-start.23 = (s32[3136,2]{0,1:T(2,128)S(1)}, s32[3136,2]{0,1:T(2,128)}, u32[]{:S(2)}) copy-start(s32[3136,2]{0,1:T(2,128)} %param.32) | copy-start | bytes 75268
  193.1 42.5 %collective-permute-start.1 = (bf16[768,768]{1,0:T(8,128)(2,1)}, bf16[768,768]{1,0:T(8,128)(2,1)}, u32[]{:S(2)}, u32[]{:S(2)}) collective-permute-start(bf16[768,768]{1,0:T(8,128)(2,1)} %get-tuple-element.101), channel_id=1, source_target_pairs={{0,8},{8,0},{16,24},{24,16},{1,9},{9,1},{17,25},{25,17},{2,10},{10... | collective-permute-start | bytes 3538952 | tf_op jit(solution)/shard_map/ppermute | solution.py:1250
  194.3 51.0 %collective-permute-start.3 = (bf16[768,768]{1,0:T(8,128)(2,1)}, bf16[768,768]{1,0:T(8,128)(2,1)}, u32[]{:S(2)}, u32[]{:S(2)}) collective-permute-start(bf16[768,768]{1,0:T(8,128)(2,1)} %get-tuple-element.101), channel_id=1, source_target_pairs={{0,24},{8,16},{16,8},{24,0},{1,25},{9,17},{17,9},{25,1},{2,26},{10... | collective-permute-start | bytes 3538952 | tf_op jit(solution)/shard_map/ppermute | solution.py:1250
  195.7 49.6 %collective-permute-start.2 = (bf16[768,768]{1,0:T(8,128)(2,1)}, bf16[768,768]{1,0:T(8,128)(2,1)}, u32[]{:S(2)}, u32[]{:S(2)}) collective-permute-start(bf16[768,768]{1,0:T(8,128)(2,1)} %get-tuple-element.100), channel_id=1, source_target_pairs={{0,16},{8,24},{16,0},{24,8},{1,17},{9,25},{17,1},{25,9},{2,18},{10... | collective-permute-start | bytes 3538952 | tf_op jit(solution)/shard_map/ppermute | solution.py:1250
  196.7 67.6 %collective-permute-start.4 = (bf16[768,768]{1,0:T(8,128)(2,1)}, bf16[768,768]{1,0:T(8,128)(2,1)}, u32[]{:S(2)}, u32[]{:S(2)}) collective-permute-start(bf16[768,768]{1,0:T(8,128)(2,1)} %get-tuple-element.100), channel_id=1, source_target_pairs={{0,1},{1,0},{2,3},{3,2},{4,5},{5,4},{6,7},{7,6},{8,9},{9,8},{10,11... | collective-permute-start | bytes 3538952 | tf_op jit(solution)/shard_map/ppermute | solution.py:1250
  197.6 55.2 %collective-permute-start.8 = (f32[4,2,768]{2,1,0:T(2,128)S(1)}, f32[4,2,768]{2,1,0:T(2,128)S(1)}, u32[]{:S(2)}, u32[]{:S(2)}) collective-permute-start(f32[4,2,768]{2,1,0:T(2,128)S(1)} %slice.204), channel_id=1, source_target_pairs={{0,1},{1,0},{2,3},{3,2},{4,5},{5,4},{6,7},{7,6},{8,9},{9,8},{10,11... | collective-permute-start | bytes 73736 | tf_op jit(solution)/shard_map/ppermute | solution.py:1250
  198.9 12.3 %slice-start = ((s8[5111808]{0:T(1024)(128)(4,1)}), s8[4194304]{0:T(1024)(128)(4,1)S(1)}, s32[]{:S(2)}) async-start(s8[5111808]{0:T(1024)(128)(4,1)} %bitcast.103), calls=%async_computation.2 | async-start | bytes 8388608
  202.7 8.4 %slice-start.1 = ((s8[5111808]{0:T(1024)(128)(4,1)}), s8[917504]{0:T(1024)(128)(4,1)S(1)}, s32[]{:S(2)}) async-start(s8[5111808]{0:T(1024)(128)(4,1)} %bitcast.103), calls=%async_computation.3 | async-start | bytes 1835008
  215.2 7.8 %copy-start.2 = (f32[832,768]{1,0:T(8,128)S(1)}, f32[832,768]{1,0:T(8,128)}, u32[]{:S(2)}) copy-start(f32[832,768]{1,0:T(8,128)} %get-tuple-element.96) | copy-start | bytes 7667716
  218.1 41.1 %all-to-all-start = ((bf16[8,104,896]{2,1,0:T(8,128)(2,1)}), bf16[8,104,896]{2,1,0:T(8,128)(2,1)}, u32[]{:S(2)}, u32[]{:S(2)}) async-start(bf16[8,104,896]{2,1,0:T(8,128)(2,1)} %maximum_maximum_fusion), calls=%async_computation | async-start | bytes 2981888 | tf_op jit(solution)/shard_map/all_to_all | solution.py:1293
  232.7 13.8 %copy-start.4 = (bf16[4,208,768]{2,1,0:T(8,128)(2,1)S(1)}, bf16[4,208,768]{2,1,0:T(8,128)(2,1)}, u32[]{:S(2)}) copy-start(bf16[4,208,768]{2,1,0:T(8,128)(2,1)} %pad.27) | copy-start | bytes 3833860
  245.3 18.9 %collective-permute-start.5 = (bf16[768,768]{1,0:T(8,128)(2,1)}, bf16[768,768]{1,0:T(8,128)(2,1)}, u32[]{:S(2)}, u32[]{:S(2)}) collective-permute-start(bf16[768,768]{1,0:T(8,128)(2,1)} %collective-permute-done.1), channel_id=1, source_target_pairs={{0,1},{1,0},{2,3},{3,2},{4,5},{5,4},{6,7},{7,6},{8,9},{9,8},{10,11... | collective-permute-start | bytes 3538952 | tf_op jit(solution)/shard_map/ppermute | solution.py:1250
  245.3 18.9 %collective-permute-start.6 = (bf16[768,768]{1,0:T(8,128)(2,1)}, bf16[768,768]{1,0:T(8,128)(2,1)}, u32[]{:S(2)}, u32[]{:S(2)}) collective-permute-start(bf16[768,768]{1,0:T(8,128)(2,1)} %collective-permute-done.2), channel_id=1, source_target_pairs={{0,1},{1,0},{2,3},{3,2},{4,5},{5,4},{6,7},{7,6},{8,9},{9,8},{10,11... | collective-permute-start | bytes 3538952 | tf_op jit(solution)/shard_map/ppermute | solution.py:1250
  245.8 18.4 %collective-permute-start.7 = (bf16[768,768]{1,0:T(8,128)(2,1)}, bf16[768,768]{1,0:T(8,128)(2,1)}, u32[]{:S(2)}, u32[]{:S(2)}) collective-permute-start(bf16[768,768]{1,0:T(8,128)(2,1)} %collective-permute-done.3), channel_id=1, source_target_pairs={{0,1},{1,0},{2,3},{3,2},{4,5},{5,4},{6,7},{7,6},{8,9},{9,8},{10,11... | collective-permute-start | bytes 3538952 | tf_op jit(solution)/shard_map/ppermute | solution.py:1250
  259.2 36.6 %all-to-all-start.1 = ((bf16[8,104,768]{2,1,0:T(8,128)(2,1)}), bf16[8,104,768]{2,1,0:T(8,128)(2,1)}, u32[]{:S(2)}, u32[]{:S(2)}) async-start(bf16[8,104,768]{2,1,0:T(8,128)(2,1)} %bitcast.116), calls=%async_computation.1 | async-start | bytes 2555904 | tf_op jit(solution)/shard_map/all_to_all | solution.py:1293
  382.5 8.8 %copy-start.25 = (s32[2,2,4,208]{3,2,1,0:T(4,128)S(1)}, s32[2,2,4,208]{3,2,1,0:T(4,128)}, u32[]{:S(2)}) copy-start(s32[2,2,4,208]{3,2,1,0:T(4,128)} %eq.238) | copy-start | bytes 39940
  382.5 8.8 %copy-start.34 = (s32[832]{0:T(1024)S(1)}, s32[832]{0:T(1024)}, u32[]{:S(2)}) copy-start(s32[832]{0:T(1024)} %get-tuple-element.186) | copy-start | bytes 9988
  396.4 27.7 %collective-permute-start.9 = (bf16[768,768]{1,0:T(8,128)(2,1)S(1)}, bf16[768,768]{1,0:T(8,128)(2,1)}, u32[]{:S(2)}, u32[]{:S(2)}) collective-permute-start(bf16[768,768]{1,0:T(8,128)(2,1)S(1)} %get-tuple-element.190), channel_id=1, source_target_pairs={{0,16},{8,24},{16,0},{24,8},{1,17},{9,25},{17,1},{25,9},{2,18},{10... | collective-permute-start | bytes 3538952 | tf_op jit(solution)/shard_map/ppermute | solution.py:1250
  424.2 42.6 %collective-permute-start.10 = (bf16[832,768]{1,0:T(8,128)(2,1)}, bf16[832,768]{1,0:T(8,128)(2,1)}, u32[]{:S(2)}, u32[]{:S(2)}) collective-permute-start(bf16[832,768]{1,0:T(8,128)(2,1)} %bitcast.30), channel_id=1, source_target_pairs={{0,8},{8,0},{16,24},{24,16},{1,9},{9,1},{17,25},{25,17},{2,10},{10... | collective-permute-start | bytes 3833864 | tf_op jit(solution)/shard_map/ppermute | solution.py:1250
  424.5 42.3 %collective-permute-start.11 = (bf16[832,768]{1,0:T(8,128)(2,1)}, bf16[832,768]{1,0:T(8,128)(2,1)}, u32[]{:S(2)}, u32[]{:S(2)}) collective-permute-start(bf16[832,768]{1,0:T(8,128)(2,1)} %bitcast.30), channel_id=1, source_target_pairs={{0,16},{8,24},{16,0},{24,8},{1,17},{9,25},{17,1},{25,9},{2,18},{10... | collective-permute-start | bytes 3833864 | tf_op jit(solution)/shard_map/ppermute | solution.py:1250
  464.8 41.4 %collective-permute-start.15 = (bf16[768,768]{1,0:T(8,128)(2,1)}, bf16[768,768]{1,0:T(8,128)(2,1)}, u32[]{:S(2)}, u32[]{:S(2)}) collective-permute-start(bf16[768,768]{1,0:T(8,128)(2,1)} %fusion.24), channel_id=1, source_target_pairs={{0,8},{8,0},{16,24},{24,16},{1,9},{9,1},{17,25},{25,17},{2,10},{10... | collective-permute-start | bytes 3538952 | tf_op jit(solution)/shard_map/ppermute | solution.py:1250
  465.2 41.0 %collective-permute-start.14 = (bf16[768,768]{1,0:T(8,128)(2,1)}, bf16[768,768]{1,0:T(8,128)(2,1)}, u32[]{:S(2)}, u32[]{:S(2)}) collective-permute-start(bf16[768,768]{1,0:T(8,128)(2,1)} %get-tuple-element.129), channel_id=1, source_target_pairs={{0,16},{8,24},{16,0},{24,8},{1,17},{9,25},{17,1},{25,9},{2,18},{10... | collective-permute-start | bytes 3538952 | tf_op jit(solution)/shard_map/ppermute | solution.py:1250
  468.8 36.2 %collective-permute-start.12 = (bf16[416,768]{1,0:T(8,128)(2,1)}, bf16[416,768]{1,0:T(8,128)(2,1)S(1)}, u32[]{:S(2)}, u32[]{:S(2)}) collective-permute-start(bf16[416,768]{1,0:T(8,128)(2,1)} %slice.216), channel_id=1, source_target_pairs={{0,16},{8,24},{16,0},{24,8},{1,17},{9,25},{17,1},{25,9},{2,18},{10... | collective-permute-start | bytes 1916936 | tf_op jit(solution)/shard_map/ppermute | solution.py:1250
  471.1 33.9 %collective-permute-start.13 = (bf16[416,768]{1,0:T(8,128)(2,1)}, bf16[416,768]{1,0:T(8,128)(2,1)}, u32[]{:S(2)}, u32[]{:S(2)}) collective-permute-start(bf16[416,768]{1,0:T(8,128)(2,1)} %slice.217), channel_id=1, source_target_pairs={{0,8},{8,0},{16,24},{24,16},{1,9},{9,1},{17,25},{25,17},{2,10},{10... | collective-permute-start | bytes 1916936 | tf_op jit(solution)/shard_map/ppermute | solution.py:1250
  514.7 48.0 %collective-permute-start.16 = (bf16[784,768]{1,0:T(8,128)(2,1)}, bf16[784,768]{1,0:T(8,128)(2,1)S(1)}, u32[]{:S(2)}, u32[]{:S(2)}) collective-permute-start(bf16[784,768]{1,0:T(8,128)(2,1)} %reshape.420), channel_id=1, source_target_pairs={{0,8},{8,0},{16,24},{24,16},{1,9},{9,1},{17,25},{25,17},{2,10},{10... | collective-permute-start | bytes 3612680 | tf_op jit(solution)/shard_map/ppermute | solution.py:1250
  516.4 48.5 %collective-permute-start.17 = (bf16[784,768]{1,0:T(8,128)(2,1)}, bf16[784,768]{1,0:T(8,128)(2,1)}, u32[]{:S(2)}, u32[]{:S(2)}) collective-permute-start(bf16[784,768]{1,0:T(8,128)(2,1)} %reshape.420), channel_id=1, source_target_pairs={{0,16},{8,24},{16,0},{24,8},{1,17},{9,25},{17,1},{25,9},{2,18},{10... | collective-permute-start | bytes 3612680 | tf_op jit(solution)/shard_map/ppermute | solution.py:1250
  520.2 207.1 %collective-permute-start.18 = (bf16[768,768]{1,0:T(8,128)(2,1)}, bf16[768,768]{1,0:T(8,128)(2,1)}, u32[]{:S(2)}, u32[]{:S(2)}) collective-permute-start(bf16[768,768]{1,0:T(8,128)(2,1)} %broadcast_select_fusion.1), channel_id=1, source_target_pairs={{0,1},{1,0},{2,3},{3,2},{4,5},{5,4},{6,7},{7,6},{8,9},{9,8},{10,11... | collective-permute-start | bytes 3538952 | tf_op jit(solution)/shard_map/ppermute | solution.py:1250
  727.3 18.0 %slice-start.4 = ((s8[4816896]{0:T(1024)(128)(4,1)}), s8[4194304]{0:T(1024)(128)(4,1)S(1)}, s32[]{:S(2)}) async-start(s8[4816896]{0:T(1024)(128)(4,1)} %bitcast.111), calls=%async_computation.6 | async-start | bytes 8388608
  732.7 12.6 %slice-start.5 = ((s8[4816896]{0:T(1024)(128)(4,1)}), s8[622592]{0:T(1024)(128)(4,1)S(1)}, s32[]{:S(2)}) async-start(s8[4816896]{0:T(1024)(128)(4,1)} %bitcast.111), calls=%async_computation.7 | async-start | bytes 1245184
  737.6 7.7 %copy-start.7 = (bf16[784,768]{1,0:T(8,128)(2,1)S(1)}, bf16[784,768]{1,0:T(8,128)(2,1)}, u32[]{:S(2)}) copy-start(bf16[784,768]{1,0:T(8,128)(2,1)} %copy-done.6) | copy-start | bytes 3612676
  (53 other events, 169.6 us)
